TPU v7x, 32 devices: a whole 2x2x4 slice. The times are simulated.
32 devices in a mesh: dp: 8 (over y, x, core), seq: 4 (over z).
Axes of the slice: x: 2, y: 2, z: 4, core: 2. Of those that a mesh axis runs over, the one named last changes fastest.
Arguments:
- tokens: bfloat16 [32, 512, 768], P('dp', 'seq'), may hold values from -6 to 6
- segments: int32 [32, 512], P('dp', 'seq'), may hold values from 0 to 2, as said below
- offset_buckets: int32 [1023], replicated, may hold values from 0 to 31
- norm_attn: float32 [768], replicated, may hold values from 0.5 to 1.5
- w_query: bfloat16 [768, 768], replicated, may hold values from -0.109375 to 0.109375
- w_key: bfloat16 [768, 768], replicated, may hold values from -0.078125 to 0.078125
- w_value: bfloat16 [768, 768], replicated, may hold values from -0.21875 to 0.21875
- w_output: bfloat16 [768, 768], replicated, may hold values from -1.75 to 1.75
- bias_table: float32 [32, 12], replicated, may hold values from -4 to 4
- norm_ff: float32 [768], replicated, may hold values from 0.5 to 1.5
- w_gate: bfloat16 [768, 2048], replicated, may hold values from -0.21875 to 0.21875
- w_up: bfloat16 [768, 2048], replicated, may hold values from -0.21875 to 0.21875
- w_down: bfloat16 [2048, 768], replicated, may hold values from -0.125 to 0.125
- cotangent: bfloat16 [32, 512, 768], P('dp', 'seq'), may hold values from -6 to 6
Outputs:
- mixed: bfloat16 [32, 512, 768], P('dp', 'seq')
- grad_tokens: float32 [32, 512, 768], P('dp', 'seq')
- grad_norm_attn: float32 [768], P('dp')
- grad_query: float32 [768, 768], P('dp')
- grad_key: float32 [768, 768], P('dp')
- grad_value: float32 [768, 768], P('dp')
- grad_output: float32 [768, 768], P('dp')
- grad_table: float32 [32, 12], replicated
- grad_norm_ff: float32 [768], P('dp')
- grad_gate: float32 [768, 2048], P('dp')
- grad_up: float32 [768, 2048], P('dp')
- grad_down: float32 [2048, 768], P('dp')
Inputs may be any that keep to these rules, and one draw needn't show every extreme that they name: `segments`: within each row the ids never fall, the first position has id 0 and the last id 2; each id is one document.
All inputs are finite; a program needn't handle non-finite values.
Results may differ from a plain program's by a relative error of at most 0.017.
Values may be sent and summed in bfloat16 or wider, within the bound.
A program may use at most 192 MiB of HBM per device.

v0:
```python
import jax
import jax.numpy as jnp
from jax import lax
from jax.sharding import PartitionSpec as P

EPSILON = 1e-06


def dot_rows(left, right):
    return lax.dot_general(
        left, right, (((0,), (0,)), ((), ())), preferred_element_type=jnp.float32
    )


def dot_back(left, right):
    return lax.dot_general(
        left, right, (((1,), (1,)), ((), ())), preferred_element_type=jnp.float32
    )


def normalize(values):
    scale = lax.rsqrt(jnp.mean(values * values, -1, keepdims=True) + EPSILON)
    return (values * scale, scale)


def norm_back(grad_out, normed, scale, gain):
    grad_normed = grad_out * gain
    return scale * (grad_normed - normed * jnp.mean(grad_normed * normed, -1, keepdims=True))


def bucket_map(offset_buckets, span, length):
    window_len = length + span - 1
    rolled = jnp.roll(offset_buckets, -(span - 1))
    tiled = jnp.tile(rolled, span)[: span * (window_len - 1)].reshape(span, window_len - 1)
    return tiled[:, :length]


def on_device(
    tokens,
    segments,
    offset_buckets,
    norm_attn,
    w_query,
    w_key,
    w_value,
    w_output,
    bias_table,
    norm_ff,
    w_gate,
    w_up,
    w_down,
    cotangent,
):
    tok_rows, seg_rows, cot_rows = (
        lax.all_to_all(tokens, "seq", split_axis=0, concat_axis=1, tiled=True),
        lax.all_to_all(segments, "seq", split_axis=0, concat_axis=1, tiled=True),
        lax.all_to_all(cotangent, "seq", split_axis=0, concat_axis=1, tiled=True),
    )
    nrows, span, width = tok_rows.shape
    buckets, heads = bias_table.shape
    head_dim = width // heads
    count = nrows * span
    inputs = tok_rows.astype(jnp.float32)
    normed_one, scale_one = normalize(inputs)
    hidden_one = (normed_one * norm_attn).astype(jnp.bfloat16).reshape(count, width)
    queries = (
        jnp.dot(hidden_one, w_query, preferred_element_type=jnp.float32)
        .astype(jnp.bfloat16)
        .reshape(nrows, span, heads, head_dim)
    )
    keys_local = (
        jnp.dot(hidden_one, w_key, preferred_element_type=jnp.float32)
        .astype(jnp.bfloat16)
        .reshape(nrows, span, width)
    )
    values_local = (
        jnp.dot(hidden_one, w_value, preferred_element_type=jnp.float32)
        .astype(jnp.bfloat16)
        .reshape(nrows, span, width)
    )
    keys_all, values_all, segs_all = (keys_local, values_local, seg_rows)
    pair_bucket = bucket_map(offset_buckets, span, span)
    one_hot = (
        pair_bucket[:, :, None] == lax.broadcasted_iota(jnp.int32, (1, 1, buckets), 2)
    ).astype(jnp.float32)
    bias = jnp.einsum("qkb,bh->hqk", one_hot, bias_table, precision=lax.Precision.HIGHEST)
    one_hot_low = one_hot.astype(jnp.bfloat16)
    keys_heads = keys_all.reshape(nrows, span, heads, head_dim)
    values_heads = values_all.reshape(nrows, span, heads, head_dim)
    raw = (
        jnp.einsum("rqhd,rkhd->rhqk", queries, keys_heads, preferred_element_type=jnp.float32)
        + bias[None]
    )
    allowed = seg_rows[:, None, :, None] == segs_all[:, None, None, :]
    scores = jnp.where(allowed, raw, -1e30)
    highest = jnp.max(scores, -1, keepdims=True)
    log_total = highest + jnp.log(jnp.sum(jnp.exp(scores - highest), -1, keepdims=True))
    probs = jnp.exp(scores - log_total)
    probs_low = probs.astype(jnp.bfloat16)
    attended = (
        jnp.einsum("rhqk,rkhd->rqhd", probs_low, values_heads, preferred_element_type=jnp.float32)
        .astype(jnp.bfloat16)
        .reshape(count, width)
    )
    resid = inputs + jnp.dot(attended, w_output, preferred_element_type=jnp.float32).reshape(
        nrows, span, width
    )
    normed_two, scale_two = normalize(resid)
    hidden_two = (normed_two * norm_ff).astype(jnp.bfloat16).reshape(count, width)
    gate = jnp.dot(hidden_two, w_gate, preferred_element_type=jnp.float32)
    upper = jnp.dot(hidden_two, w_up, preferred_element_type=jnp.float32)

    def gated(gate_in, up_in):
        return jax.nn.gelu(gate_in, approximate=True) * up_in

    product, pull_gated = jax.vjp(gated, gate, upper)
    activ = product.astype(jnp.bfloat16)
    mixed_rows = (
        resid
        + jnp.dot(activ, w_down, preferred_element_type=jnp.float32).reshape(nrows, span, width)
    ).astype(jnp.bfloat16)
    mixed = lax.all_to_all(mixed_rows, "seq", split_axis=1, concat_axis=0, tiled=True)
    grad_low = cot_rows.reshape(count, width)
    grad_down = dot_rows(activ, grad_low)
    grad_act = dot_back(grad_low, w_down)
    grad_gate_in, grad_up_in = pull_gated(grad_act)
    gate_low = grad_gate_in.astype(jnp.bfloat16)
    upper_low = grad_up_in.astype(jnp.bfloat16)
    grad_gate = dot_rows(hidden_two, gate_low)
    grad_up = dot_rows(hidden_two, upper_low)
    grad_hidden_two = (dot_back(gate_low, w_gate) + dot_back(upper_low, w_up)).reshape(
        nrows, span, width
    )
    grad_norm_ff = jnp.sum(grad_hidden_two * normed_two, axis=(0, 1))
    grad_resid = cot_rows.astype(jnp.float32) + norm_back(
        grad_hidden_two, normed_two, scale_two, norm_ff
    )
    grad_branch = grad_resid.astype(jnp.bfloat16).reshape(count, width)
    grad_output = dot_rows(attended, grad_branch)
    grad_attended = (
        dot_back(grad_branch, w_output).astype(jnp.bfloat16).reshape(nrows, span, heads, head_dim)
    )
    grad_probs = jnp.einsum(
        "rqhd,rkhd->rhqk", grad_attended, values_heads, preferred_element_type=jnp.float32
    )
    inner = jnp.sum(probs * grad_probs, -1, keepdims=True)
    grad_scores = (probs * (grad_probs - inner)).astype(jnp.bfloat16)
    grad_queries = (
        jnp.einsum("rhqk,rkhd->rqhd", grad_scores, keys_heads, preferred_element_type=jnp.float32)
        .astype(jnp.bfloat16)
        .reshape(count, width)
    )
    grad_keys_part = jnp.einsum(
        "rhqk,rqhd->rkhd", grad_scores, queries, preferred_element_type=jnp.float32
    ).reshape(nrows, span, width)
    grad_values_part = jnp.einsum(
        "rhqk,rqhd->rkhd", probs_low, grad_attended, preferred_element_type=jnp.float32
    ).reshape(nrows, span, width)
    grad_table_local = jnp.einsum(
        "qkb,rhqk->bh", one_hot_low, grad_scores, preferred_element_type=jnp.float32
    )
    grad_keys_sum, grad_values_sum = (grad_keys_part, grad_values_part)
    keys_grad_low = grad_keys_sum.astype(jnp.bfloat16).reshape(count, width)
    values_grad_low = grad_values_sum.astype(jnp.bfloat16).reshape(count, width)
    grad_query = dot_rows(hidden_one, grad_queries)
    grad_key = dot_rows(hidden_one, keys_grad_low)
    grad_value = dot_rows(hidden_one, values_grad_low)
    grad_hidden_one = (
        dot_back(grad_queries, w_query)
        + dot_back(keys_grad_low, w_key)
        + dot_back(values_grad_low, w_value)
    ).reshape(nrows, span, width)
    grad_norm_attn = jnp.sum(grad_hidden_one * normed_one, axis=(0, 1))
    grad_rows = grad_resid + norm_back(grad_hidden_one, normed_one, scale_one, norm_attn)
    grad_tokens = lax.all_to_all(
        grad_rows.astype(jnp.bfloat16), "seq", split_axis=1, concat_axis=0, tiled=True
    ).astype(grad_rows.dtype)
    (
        attn_norm_share,
        query_share,
        key_share,
        value_share,
        output_share,
        ff_norm_share,
        ff_gate_share,
        ff_up_share,
        ff_down_share,
    ) = (
        lax.psum_scatter(grad_norm_attn, "dp", scatter_dimension=0, tiled=True),
        lax.psum_scatter(grad_query, "dp", scatter_dimension=0, tiled=True),
        lax.psum_scatter(grad_key, "dp", scatter_dimension=0, tiled=True),
        lax.psum_scatter(grad_value, "dp", scatter_dimension=0, tiled=True),
        lax.psum_scatter(grad_output, "dp", scatter_dimension=0, tiled=True),
        lax.psum_scatter(grad_norm_ff, "dp", scatter_dimension=0, tiled=True),
        lax.psum_scatter(grad_gate, "dp", scatter_dimension=0, tiled=True),
        lax.psum_scatter(grad_up, "dp", scatter_dimension=0, tiled=True),
        lax.psum_scatter(grad_down, "dp", scatter_dimension=0, tiled=True),
    )
    totals = (
        lax.psum(attn_norm_share.astype(jnp.bfloat16), "seq").astype(jnp.float32),
        lax.psum(query_share.astype(jnp.bfloat16), "seq").astype(jnp.float32),
        lax.psum(key_share.astype(jnp.bfloat16), "seq").astype(jnp.float32),
        lax.psum(value_share.astype(jnp.bfloat16), "seq").astype(jnp.float32),
        lax.psum(output_share.astype(jnp.bfloat16), "seq").astype(jnp.float32),
        lax.psum(ff_norm_share.astype(jnp.bfloat16), "seq").astype(jnp.float32),
        lax.psum(ff_gate_share.astype(jnp.bfloat16), "seq").astype(jnp.float32),
        lax.psum(ff_up_share.astype(jnp.bfloat16), "seq").astype(jnp.float32),
        lax.psum(ff_down_share.astype(jnp.bfloat16), "seq").astype(jnp.float32),
    )
    table_total = lax.psum(grad_table_local, ("dp", "seq"))
    return (
        mixed,
        grad_tokens,
        totals[0],
        totals[1],
        totals[2],
        totals[3],
        totals[4],
        table_total,
        totals[5],
        totals[6],
        totals[7],
        totals[8],
    )


def solution(mesh):
    return jax.shard_map(
        on_device,
        mesh=mesh,
        in_specs=(
            P("dp", "seq", None),
            P("dp", "seq"),
            P(),
            P(),
            P(),
            P(),
            P(),
            P(),
            P(),
            P(),
            P(),
            P(),
            P(),
            P("dp", "seq", None),
        ),
        out_specs=(
            P("dp", "seq", None),
            P("dp", "seq", None),
            P("dp"),
            P("dp", None),
            P("dp", None),
            P("dp", None),
            P("dp", None),
            P(),
            P("dp"),
            P("dp", None),
            P("dp", None),
            P("dp", None),
        ),
        check_vma=False,
    )
```

profile of v0, /device:TPU:0, one launch (start us, length us, event | category | flops | bytes accessed | tf_op | source)
XLA Modules:
  0.0 654.7 jit_solution(15987207320429885172)
XLA Ops:
  7.2 12.1 %all_to_all.55 = s32[4,1,128]{2,1,0:T(1,128)S(1)} all-to-all(s32[4,1,128]{2,1,0:T(1,128)} %bitcast.156), channel_id=1, replica_groups=mesh['dp'=8,'seq'=4] {'seq'}, dimensions={0} | all-to-all | bytes 4096 | tf_op jit(solution)/shard_map/all_to_all | solution.py:56
  19.3 4.2 all-to-all-start
  26.5 4.2 tile.10
  33.8 4.5 reshape.371
  43.1 14.8 %fusion = f32[512,512,12]{0,2,1:T(8,128)} fusion(s32[512,512]{0,1:T(8,128)} %copy.69, f32[32,12]{0,1:T(8,128)S(1)} %copy-done.29), kind=kOutput, calls=%fused_computation.2 | convolution fusion | flops 1216348160 | bytes 13633024 | tf_op jit(solution)/shard_map/qkb,bh->hqk/dot_general | solution.py:86
  58.1 5.1 all-to-all-start.3
  80.6 14.7 %fusion.47 = (f32[12,512]{1,0:T(8,128)S(1)}, f32[12,512,512]{1,2,0:T(8,128)S(1)}) fusion(f32[512,512,12]{0,2,1:T(8,128)} %fusion, bf16[512,12,64]{0,2,1:T(8,128)(2,1)} %bitcast.138, bf16[512,12,64]{0,2,1:T(8,128)(2,1)} %bitcast.132, pred[512,512]{0,1:T(8,128)(4,1)S(1)} %broadcast_compare_fusion), kind=kOutput, calls=%fused_computation.78 | convolution fusion | flops 412084224 | bytes 27025408 | tf_op jit(solution)/shard_map/rqhd,rkhd->rhqk/dot_general | solution.py:91
  105.8 3.7 fusion.49
  113.3 8.8 %multiply_convert_fusion.1 = (bf16[512,2048]{1,0:T(8,128)(2,1)S(1)}, bf16[512,2048]{1,0:T(8,128)(2,1)S(1)}, bf16[512,2048]{1,0:T(8,128)(2,1)}) fusion(f32[512,2048]{1,0:T(8,128)} %fusion.48, f32[512,2048]{1,0:T(8,128)} %fusion.49, bf16[512,768]{1,0:T(8,128)(2,1)} %bitcast.13, bf16[2048,768]{1,0:T(8,128)(2,1)S(1)} %copy-done), kind=kOutput, calls=%fused_computation.23 | convolution fusion | flops 1637875712 | bytes 18612224 | tf_op jit(solution)/shard_map/dot_general | solution.py:16
  140.4 7.6 %fusion.35 = bf16[12,64,512]{2,1,0:T(8,128)(2,1)S(1)} fusion(bf16[512,12,64]{0,2,1:T(8,128)(2,1)S(1)} %bitcast.137, f32[12,512,512]{1,2,0:T(8,128)} %copy-done.1, f32[12,512]{1,0:T(8,128)S(1)} %log_add_fusion), kind=kOutput, calls=%fused_computation.59 | convolution fusion | flops 409337856 | bytes 14180352 | tf_op jit(solution)/shard_map/rhqk,rqhd->rkhd/dot_general | solution.py:156
  151.4 8.0 %multiply_reduce_fusion = (f32[12,512]{1,0:T(8,128)S(1)}, f32[12,512,512]{1,2,0:T(8,128)S(1)}) fusion(f32[12,512,512]{1,2,0:T(8,128)} %copy-done.1, f32[12,512]{1,0:T(8,128)S(1)} %log_add_fusion, bf16[512,12,64]{0,2,1:T(8,128)(2,1)} %bitcast.136, bf16[512,12,64]{0,2,1:T(8,128)(2,1)} %bitcast.134), kind=kOutput, calls=%fused_computation.9 | convolution fusion | flops 412084224 | bytes 26787840 | tf_op jit(solution)/shard_map/rqhd,rkhd->rhqk/dot_general | solution.py:143
  159.4 7.0 %multiply_convert_fusion = bf16[12,512,512]{1,2,0:T(8,128)(2,1)S(1)} fusion(f32[12,512,512]{1,2,0:T(8,128)S(1)} %get-tuple-element.38, f32[12,512,512]{1,2,0:T(8,128)} %copy-done.1, f32[12,512]{1,0:T(8,128)S(1)} %get-tuple-element.37, f32[12,512]{1,0:T(8,128)S(1)} %log_add_fusion), kind=kLoop, calls=%fused_computation.8 | loop fusion | flops 12582912 | bytes 31506432 | tf_op jit(solution)/shard_map/convert_element_type | solution.py:147
  172.3 4.2 convolution_convert_fusion.5
  179.7 6.3 fusion.57
  186.1 6.3 fusion.56
  192.7 6.3 fusion.58
  199.0 3.8 fusion.38
  205.7 7.3 %reduce.20 = bf16[512,768]{1,0:T(8,128)(2,1)} reduce(bf16[512,1,768]{2,1,0:T(2,128)(2,1)} %bitcast.144, bf16[]{:T(256)} %broadcast.188), dimensions={1}, to_apply=%bitcast.128.reduce_sub_computation | reduce | bytes 1572866
  215.0 5.2 all-to-all-start.2
  229.4 39.9 %reduce-scatter.10.cloned.1.call-done = f32[96,768]{1,0:T(8,128)} async-done(((f32[768,768]{1,0:T(8,128)}), f32[96,768]{1,0:T(8,128)}) %reduce-scatter.10.cloned.1.call-update) | async-done | bytes 294928 | tf_op jit(solution)/shard_map/reduce_scatter | solution.py:191
  271.0 44.5 %reduce-scatter.8.cloned.1.call-done = f32[96,768]{1,0:T(8,128)} async-done(((f32[768,768]{1,0:T(8,128)}), f32[96,768]{1,0:T(8,128)}) %reduce-scatter.8.cloned.1.call-update) | async-done | bytes 294928 | tf_op jit(solution)/shard_map/reduce_scatter | solution.py:190
  317.1 63.4 %reduce-scatter.18.cloned.1.call-done = f32[96,2048]{1,0:T(8,128)} async-done(((f32[768,2048]{1,0:T(8,128)}), f32[96,2048]{1,0:T(8,128)}) %reduce-scatter.18.cloned.1.call-update) | async-done | bytes 786448 | tf_op jit(solution)/shard_map/reduce_scatter | solution.py:196
  382.4 63.5 %reduce-scatter.16.cloned.1.call-done = f32[96,2048]{1,0:T(8,128)} async-done(((f32[768,2048]{1,0:T(8,128)}), f32[96,2048]{1,0:T(8,128)}) %reduce-scatter.16.cloned.1.call-update) | async-done | bytes 786448 | tf_op jit(solution)/shard_map/reduce_scatter | solution.py:195
  447.8 63.2 %reduce-scatter.20.cloned.1.call-done = f32[256,768]{1,0:T(8,128)} async-done(((f32[2048,768]{1,0:T(8,128)}), f32[256,768]{1,0:T(8,128)}) %reduce-scatter.20.cloned.1.call-update) | async-done | bytes 786448 | tf_op jit(solution)/shard_map/reduce_scatter | solution.py:197
  513.0 4.1 fusion.28
  521.1 7.3 %reduce.21 = bf16[512,768]{1,0:T(8,128)(2,1)} reduce(bf16[512,1,768]{2,1,0:T(2,128)(2,1)} %bitcast.145, bf16[]{:T(256)} %broadcast.188), dimensions={1}, to_apply=%bitcast.127.reduce_sub_computation | reduce | bytes 1572866
  530.3 4.6 all-to-all-start.4
  536.2 13.5 %all-reduce.2 = (bf16[768]{0:T(1024)(128)(2,1)S(1)}, bf16[768]{0:T(1024)(128)(2,1)S(1)}) all-reduce(f32[768]{0:T(1024)S(1)} %get-tuple-element.14, f32[768]{0:T(1024)S(1)} %get-tuple-element.12), channel_id=2, replica_groups=mesh['dp'=8,'seq'=4] {'dp'}, use_global_device_ids=true, to_apply=%region_8.9.clone | all-reduce | flops 1536 | bytes 9216
  549.8 17.7 %all-reduce.3 = (bf16[96]{0:T(256)(128)(2,1)S(1)}, bf16[96]{0:T(256)(128)(2,1)S(1)}) all-reduce(bf16[96]{0:T(256)(128)(2,1)S(1)} %dynamic-slice.7, bf16[96]{0:T(256)(128)(2,1)S(1)} %dynamic-slice.6), channel_id=1, replica_groups=mesh['dp'=8,'seq'=4] {'seq'}, use_global_device_ids=true, to_apply=%region_9.10 | all-reduce | flops 192 | bytes 768 | tf_op jit(solution)/shard_map/psum | solution.py:200
  568.5 11.2 %fusion.39 = f32[32,12]{0,1:T(8,128)S(1)} fusion(bf16[12,512,512]{1,2,0:T(8,128)(2,1)} %copy-done.2, s32[512,512]{0,1:T(8,128)} %copy.69), kind=kOutput, calls=%fused_computation.63 | convolution fusion | flops 226492416 | bytes 7341568 | tf_op jit(solution)/shard_map/qkb,rhqk->bh/dot_general | solution.py:159
  579.7 44.6 %psum.75 = f32[32,12]{0,1:T(8,128)} all-reduce(f32[32,12]{0,1:T(8,128)S(1)} %fusion.39), channel_id=1, replica_groups=mesh['dp'=8,'seq'=4] {'dp','seq'}, use_global_device_ids=true, to_apply=%region_18.19 | all-reduce | flops 384 | bytes 3072 | tf_op jit(solution)/shard_map/psum | solution.py:210
  630.5 3.7 reshape.384
  (166 shorter events, 123.6 us)
Async XLA Ops:
  7.2 106.1 %copy-start = (bf16[2048,768]{1,0:T(8,128)(2,1)S(1)}, bf16[2048,768]{1,0:T(8,128)(2,1)}, u32[]{:S(2)}) copy-start(bf16[2048,768]{1,0:T(8,128)(2,1)} %param.26) | copy-start | bytes 9437188
  19.3 38.9 %all-to-all-start = ((bf16[4,128,768]{2,1,0:T(8,128)(2,1)}), bf16[4,128,768]{2,1,0:T(8,128)(2,1)}, u32[]{:S(2)}, u32[]{:S(2)}) async-start(bf16[4,128,768]{2,1,0:T(8,128)(2,1)} %param.14), calls=%async_computation | async-start | bytes 1572864 | tf_op jit(solution)/shard_map/all_to_all | solution.py:55
  38.2 4.8 copy-start.29
  57.9 7.0 %copy-start.27 = (f32[768]{0:T(1024)S(1)}, f32[768]{0:T(1024)}, u32[]{:S(2)}) copy-start(f32[768]{0:T(1024)} %param.17) | copy-start | bytes 9220
  58.1 55.1 %all-to-all-start.3 = ((bf16[4,128,768]{2,1,0:T(8,128)(2,1)}), bf16[4,128,768]{2,1,0:T(8,128)(2,1)}, u32[]{:S(2)}, u32[]{:S(2)}) async-start(bf16[4,128,768]{2,1,0:T(8,128)(2,1)} %param.27), calls=%async_computation.3 | async-start | bytes 1572864 | tf_op jit(solution)/shard_map/all_to_all | solution.py:57
  63.2 163.0 %reduce-scatter.14.cloned.1.call-start = ((), (), s32[]{:S(2)}) async-start(), calls=%async_computation.15 | async-start | bytes 2654208 | tf_op jit(solution)/shard_map/reduce_scatter | solution.py:193
  63.4 3.8 copy-start.35
  95.4 4.5 copy-start.1
  95.4 4.5 copy-start.8
  102.0 3.8 copy-start.32
  105.8 3.8 copy-start.11
  105.8 3.8 copy-start.30
  113.3 8.8 %copy-start.31 = (bf16[768,2048]{1,0:T(8,128)(2,1)S(1)}, bf16[768,2048]{1,0:T(8,128)(2,1)}, u32[]{:S(2)}) copy-start(bf16[768,2048]{1,0:T(8,128)(2,1)} %param.24) | copy-start | bytes 9437188
  122.0 3.9 copy-start.33
  133.1 94.7 %reduce-scatter.12.cloned.1.call-start = ((), (), s32[]{:S(2)}) async-start(), calls=%async_computation.14 | async-start | bytes 2654208 | tf_op jit(solution)/shard_map/reduce_scatter | solution.py:192
  140.4 7.6 %copy-start.5 = (bf16[4,128,768]{2,1,0:T(8,128)(2,1)}, bf16[4,128,768]{2,1,0:T(8,128)(2,1)S(1)}, u32[]{:S(2)}) copy-start(bf16[4,128,768]{2,1,0:T(8,128)(2,1)S(1)} %fusion.31) | copy-start | bytes 2359300
  151.2 118.1 %reduce-scatter.10.cloned.1.call-start = ((), (), s32[]{:S(2)}) async-start(), calls=%async_computation.13 | async-start | bytes 2654208 | tf_op jit(solution)/shard_map/reduce_scatter | solution.py:191
  159.4 7.0 %copy-start.10 = (bf16[512,768]{0,1:T(8,128)(2,1)S(1)}, bf16[512,768]{0,1:T(8,128)(2,1)}, u32[]{:S(2)}) copy-start(bf16[512,768]{0,1:T(8,128)(2,1)} %copy.67) | copy-start | bytes 2359300
  172.3 143.2 %reduce-scatter.8.cloned.1.call-start = ((), (), s32[]{:S(2)}) async-start(), calls=%async_computation.12 | async-start | bytes 2654208 | tf_op jit(solution)/shard_map/reduce_scatter | solution.py:190
  172.3 5.1 copy-start.7
  179.7 200.8 %reduce-scatter.18.cloned.1.call-start = ((), (), s32[]{:S(2)}) async-start(), calls=%async_computation.17 | async-start | bytes 7077888 | tf_op jit(solution)/shard_map/reduce_scatter | solution.py:196
  186.0 259.9 %reduce-scatter.16.cloned.1.call-start = ((), (), s32[]{:S(2)}) async-start(), calls=%async_computation.16 | async-start | bytes 7077888 | tf_op jit(solution)/shard_map/reduce_scatter | solution.py:195
  192.4 318.6 %reduce-scatter.20.cloned.1.call-start = ((), (), s32[]{:S(2)}) async-start(), calls=%async_computation.18 | async-start | bytes 7077888 | tf_op jit(solution)/shard_map/reduce_scatter | solution.py:197
  215.0 315.3 %all-to-all-start.2 = ((bf16[4,2,49152]{2,1,0:T(2,128)(2,1)}), bf16[4,2,49152]{2,1,0:T(2,128)(2,1)}, u32[]{:S(2)}, u32[]{:S(2)}) async-start(bf16[4,2,49152]{2,1,0:T(2,128)(2,1)} %reshape.381), calls=%async_computation.2 | async-start | bytes 1572864 | tf_op jit(solution)/shard_map/all_to_all | solution.py:122
  220.2 416.7 %all-reduce.7.cloned.1.call-start = ((), (), s32[]{:S(2)}) async-start(), calls=%async_computation.19 | async-start | bytes 3538944 | tf_op jit(solution)/shard_map/psum | solution.py:201
  220.5 3.7 copy-start.14
  220.5 3.7 copy-start.36
  513.0 4.1 copy-start.4
  528.3 6.6 %copy-start.37 = (u32[32]{0:T(128)S(1)}, u32[32]{0:T(128)}, u32[]{:S(2)}) copy-start(u32[32]{0:T(128)} %constant.31) | copy-start | bytes 388
  530.3 100.2 %all-to-all-start.4 = ((bf16[4,2,49152]{2,1,0:T(2,128)(2,1)}), bf16[4,2,49152]{2,1,0:T(2,128)(2,1)}, u32[]{:S(2)}, u32[]{:S(2)}) async-start(bf16[4,2,49152]{2,1,0:T(2,128)(2,1)} %reshape.383), calls=%async_computation.4 | async-start | bytes 1572864 | tf_op jit(solution)/shard_map/all_to_all | solution.py:175
  636.9 8.6 %copy-start.26 = (bf16[96,2048]{1,0:T(8,128)(2,1)S(1)}, bf16[96,2048]{1,0:T(8,128)(2,1)}, u32[]{:S(2)}) copy-start(bf16[96,2048]{1,0:T(8,128)(2,1)} %get-tuple-element.25) | copy-start | bytes 1179652
  636.9 9.5 %copy-start.25 = (bf16[256,768]{1,0:T(8,128)(2,1)S(1)}, bf16[256,768]{1,0:T(8,128)(2,1)}, u32[]{:S(2)}) copy-start(bf16[256,768]{1,0:T(8,128)(2,1)} %get-tuple-element.26) | copy-start | bytes 1179652
  (18 other events, 37.8 us)
Sparse Core Ops, SparseCore 0:
  133.2 43.9 reduce-scatter.13
  180.9 42.4 reduce-scatter.11
  226.8 42.4 reduce-scatter.9
  272.9 42.4 reduce-scatter.7
  318.7 61.7 reduce-scatter.17
  384.1 61.7 reduce-scatter.15
  449.3 61.7 reduce-scatter.19
  514.8 94.0 all-reduce.6
where the time goes:
time: 663 us; the launch traced here: 655 us
  waiting for transfers between devices  275 us (41%)
  matrix products  139 us (21%)
  blocking collectives  87.9 us (13%)
  local copies, waits for them, and re-layouts  62.2 us (9%)
  other arithmetic  55.5 us (8%)
  starting transfers between devices  20.1 us (3%)
  between operations  15.8 us (2%)
    reduce_scatter x1, waiting for transfers between devices, on_device(): lax.psum_scatter(grad_gate, 'dp', scatter_dimension=0, tiled=True)  63.5 us
    reduce_scatter x1, waiting for transfers between devices, on_device(): lax.psum_scatter(grad_up, 'dp', scatter_dimension=0, tiled=True)  63.4 us
    reduce_scatter x1, waiting for transfers between devices, on_device(): lax.psum_scatter(grad_down, 'dp', scatter_dimension=0, tiled=True)  63.2 us
    psum x1, blocking collectives, on_device(): table_total = lax.psum(grad_table_local, ('dp', 'seq'))  44.6 us
    reduce_scatter x1, waiting for transfers between devices, on_device(): lax.psum_scatter(grad_query, 'dp', scatter_dimension=0, tiled=True)  44.5 us
    reduce_scatter x1, waiting for transfers between devices, on_device(): lax.psum_scatter(grad_key, 'dp', scatter_dimension=0, tiled=True)  39.9 us
    unnamed x86, local copies, waits for them, and re-layouts  28.7 us
    dot_general x7, matrix products, dot_rows(): lax.dot_general(left, right, (((0,), (0,)), ((), ())), preferred_element_...  27.8 us
  transfers between devices with their start and end apart: 12, of which 5 were waited for; matrix products, arithmetic and copies ran while one was open for 33% of the time, Pallas kernels for 0%

commit v1 on v0

v1 whole, which is shorter than its diff:
```python
import functools

import jax
import jax.numpy as jnp
from jax import lax
from jax.experimental import pallas as pl
from jax.experimental.pallas import tpu as pltpu
from jax.sharding import PartitionSpec as P

MESH = pl.DeviceIdType.MESH
VMEM = pltpu.VMEM
LOW = jnp.bfloat16
F32 = jnp.float32
EPSILON = 1e-06
MASKED = -1e30
GROUP = 8
VMEM_BYTES = 63 * 2**20


def dot(left, right):
    return jnp.dot(left, right, preferred_element_type=F32)


def dot_back(left, right):
    return lax.dot_general(left, right, (((1,), (1,)), ((), ())), preferred_element_type=F32)


def inverse_rms(values):
    return lax.rsqrt(jnp.mean(values * values, -1, keepdims=True) + EPSILON)


def zero_padded(block, half):
    blank = jnp.zeros_like(block)
    return jnp.concatenate([blank, block] if half else [block, blank], axis=0)


def forward_kernel(
    x_ref, seg_ref, bucket_ref, gain_one_ref, wq_ref, wk_ref, wv_ref, wo_ref, table_ref, gain_two_ref,
    wg_ref, wu_ref, wd_ref,
    probs_ref, slope_up_ref, slope_gate_ref, activ_t_ref, attended_t_ref, q_ref, k_ref, v_ref, k_t_ref,
    resid_ref, mixed_ref,
    bias_ref, mask_ref, offset_ref, hidden_ref, q_t_ref, v_t_ref, activ_ref,
):
    span, width = x_ref.shape
    buckets, heads = table_ref.shape
    head_dim = width // heads
    blocks = span // 128
    pairs = heads // 2

    one_hot = (
        lax.broadcasted_iota(jnp.int32, (buckets, bucket_ref.shape[1]), 0) == bucket_ref[...]
    ).astype(F32)
    offset_ref[:heads, :] = lax.dot_general(
        table_ref[...], one_hot, (((0,), (0,)), ((), ())),
        precision=lax.Precision.HIGHEST, preferred_element_type=F32,
    )

    @pl.loop(0, heads)
    def _(h):
        row = offset_ref[pl.ds(h, 1), :]
        for d in range(2 * blocks - 1):
            window = jnp.broadcast_to(row[:, 128 * d : 128 * d + 256], (128, 256))
            bias_ref[h, d] = pltpu.roll(window, 129, 1, stride=1, stride_axis=0)[:, :128].T

    seg_row = seg_ref[...].astype(F32)
    for kb in range(blocks):
        column = jnp.broadcast_to(seg_row[:, 128 * kb : 128 * kb + 128], (128, 128)).T
        for qb in range(blocks):
            same = column == seg_row[:, 128 * qb : 128 * qb + 128]
            mask_ref[128 * kb : 128 * kb + 128, 128 * qb : 128 * qb + 128] = jnp.where(same, 0.0, MASKED)

    @pl.loop(0, blocks)
    def _(i):
        rows = pl.ds(pl.multiple_of(i * 128, 128), 128)
        inputs = x_ref[rows, :].astype(F32)
        hidden_ref[rows, :] = (inputs * inverse_rms(inputs) * gain_one_ref[...]).astype(LOW)

    for tile in range(width // 256):
        cols = slice(256 * tile, 256 * tile + 256)
        q = dot(hidden_ref[...], wq_ref[:, cols])
        q_t_ref[cols, :] = q.T.astype(LOW)
        k = dot(hidden_ref[...], wk_ref[:, cols])
        k_t_ref[cols, :] = k.T.astype(LOW)
        v = dot(hidden_ref[...], wv_ref[:, cols])
        v_t_ref[cols, :] = v.T.astype(LOW)
        for i in range(2):
            lanes = slice(128 * i, 128 * i + 128)
            q_ref[2 * tile + i] = q[:, lanes].astype(LOW)
            k_ref[2 * tile + i] = k[:, lanes].astype(LOW)
            v_ref[2 * tile + i] = v[:, lanes].astype(LOW)

    @pl.loop(0, pairs)
    def _(pair):
        keys = k_ref[pair]
        for b in range(2):
            h = 2 * pair + b
            rows = pl.ds(pl.multiple_of(h * head_dim, head_dim), head_dim)
            q_t = zero_padded(q_t_ref[rows, :], b)
            v_t = v_t_ref[rows, :]
            for half in range(span // 256):
                cols = slice(256 * half, 256 * half + 256)
                bias = jnp.concatenate(
                    [
                        jnp.concatenate(
                            [bias_ref[h, kb - qb + blocks - 1] for qb in (2 * half, 2 * half + 1)], axis=1
                        )
                        for kb in range(blocks)
                    ],
                    axis=0,
                )
                scores = dot(keys, q_t[:, cols]) + bias + mask_ref[:, cols]
                powers = jnp.exp(scores - jnp.max(scores, axis=0, keepdims=True))
                probs = (powers * (1.0 / jnp.sum(powers, axis=0, keepdims=True))).astype(LOW)
                probs_ref[h, :, cols] = probs
                attended_t_ref[rows, cols] = dot(v_t, probs).astype(LOW)

    attended = attended_t_ref[...].T
    for tile in range(width // 256):
        cols = slice(256 * tile, 256 * tile + 256)
        resid_ref[:, cols] = x_ref[:, cols].astype(F32) + dot(attended, wo_ref[:, cols])

    @pl.loop(0, blocks)
    def _(i):
        rows = pl.ds(pl.multiple_of(i * 128, 128), 128)
        resid = resid_ref[rows, :]
        hidden_ref[rows, :] = (resid * inverse_rms(resid) * gain_two_ref[...]).astype(LOW)

    @pl.loop(0, wg_ref.shape[1] // 512)
    def _(g):
        for sub in range(2):
            cols = pl.ds(pl.multiple_of(512 * g + 256 * sub, 256), 256)
            gate = dot(hidden_ref[...], wg_ref[:, cols])
            upper = dot(hidden_ref[...], wu_ref[:, cols])
            square = gate * gate
            curve = jnp.tanh(0.7978845608028654 * gate * (1.0 + 0.044715 * square))
            gelu = 0.5 * gate * (1.0 + curve)
            slope = 0.5 * (1.0 + curve) + 0.5 * gate * (1.0 - curve * curve) * (
                0.7978845608028654 * (1.0 + 3 * 0.044715 * square)
            )
            activ = gelu * upper
            lanes = slice(256 * sub, 256 * sub + 256)
            slope_up_ref[g, :, lanes] = gelu.astype(LOW)
            slope_gate_ref[g, :, lanes] = (upper * slope).astype(LOW)
            activ_ref[:, cols] = activ.astype(LOW)
            activ_t_ref[2 * g + sub] = activ.T.astype(LOW)

    for tile in range(width // 256):
        cols = slice(256 * tile, 256 * tile + 256)
        mixed_ref[:, cols] = (resid_ref[:, cols] + dot(activ_ref[...], wd_ref[:, cols])).astype(LOW)


def forward(x, seg, buckets, gain_one, wq, wk, wv, wo, table, gain_two, wg, wu, wd):
    span, width = x.shape
    ff = wg.shape[1]
    heads = table.shape[1]
    low = lambda *shape: jax.ShapeDtypeStruct(shape, LOW)
    pairs = low(heads // 2, span, 128)
    return pl.pallas_call(
        forward_kernel,
        out_shape=[
            low(heads, span, span), low(ff // 512, span, 512), low(ff // 512, span, 512),
            low(ff // 256, 256, span), low(width, span), pairs, pairs, pairs, low(width, span),
            jax.ShapeDtypeStruct((span, width), F32), low(span, width),
        ],
        scratch_shapes=[
            VMEM((heads, 2 * (span // 128) - 1, 128, 128), F32), VMEM((span, span), F32), VMEM((16, 1024), F32),
            VMEM((span, width), LOW), VMEM((width, span), LOW), VMEM((width, span), LOW), VMEM((span, ff), LOW),
        ],
        compiler_params=pltpu.CompilerParams(vmem_limit_bytes=VMEM_BYTES),
        name="forward",
    )(x, seg, buckets, gain_one, wq, wk, wv, wo, table, gain_two, wg, wu, wd)


class Place:
    def __init__(self, n_dp, n_seq):
        stride = n_dp // GROUP
        dp = lax.axis_index("dp")
        z = lax.axis_index("seq")
        index = dp // stride
        self.n_seq = n_seq
        self.core, self.x, self.y, self.z = index % 2, (index // 2) % 2, index // 4, z
        self.dp = dp
        self.core_peer = (dp + stride * (1 - 2 * self.core), z)
        self.x_peer = (dp + 2 * stride * (1 - 2 * self.x), z)
        self.y_peer = (dp + 4 * stride * (1 - 2 * self.y), z)

    def z_peer(self, z):
        return (self.dp, z)

    def z_pair(self, bit):
        return (self.dp, self.z + bit * (1 - 2 * ((self.z // bit) % 2)))


def remote(src, dst, sems, index, peer):
    return pltpu.make_async_remote_copy(
        src_ref=src, dst_ref=dst, send_sem=sems.at[0, index], recv_sem=sems.at[1, index],
        device_id=peer, device_id_type=MESH,
    )


class Sums:
    def __init__(self, place, own, sems, got0, got1, got2, low_z, high_z):
        self.place, self.own, self.sems = place, own, sems
        self.got0, self.got1, self.got2, self.low_z, self.high_z = got0, got1, got2, low_z, high_z

    def copy0(self, p):
        at = self.place
        return remote(self.own.at[p, 1 - at.core], self.got0.at[p], self.sems.at[0], p, at.core_peer)

    def copy1(self, p, k):
        at = self.place
        mine = self.own.at[p, at.core]
        src = mine.at[1 - at.y] if k else mine.at[:, 1 - at.x]
        return remote(src, self.got1.at[p], self.sems.at[1], p, at.y_peer if k else at.x_peer)

    def copy2(self, p, k):
        at = self.place
        mine = self.own.at[p, at.core]
        src = mine.at[at.y, 1 - at.x] if k else mine.at[1 - at.y, at.x]
        return remote(src, self.got2.at[p], self.sems.at[2], p, at.x_peer if k else at.y_peer)

    def kept(self, p):
        at = self.place
        return self.own.at[p, at.core, at.y, at.x]

    def up(self, p, first):
        src = self.kept(p) if first else self.got2.at[p]
        return remote(src, self.low_z.at[p], self.sems.at[3], p, self.place.z_peer(self.place.z + 1))

    def down(self, p, first):
        src = self.kept(p) if first else self.got1.at[p, 0]
        return remote(src, self.high_z.at[p], self.sems.at[4], p, self.place.z_peer(self.place.z - 1))

    def stage0(self, j):
        for k in range(2):
            self.copy0(2 * j + k).start()

    def stage1(self, j):
        at = self.place
        for k in range(2):
            p = 2 * j + k
            self.copy0(p).wait_recv()
            for a in range(2):
                for b in range(2):
                    self.own[p, at.core, a, b] = self.own[p, at.core, a, b] + self.got0[p, a, b]
            self.copy1(p, k).start()

    def stage2(self, j):
        at = self.place
        for k in range(2):
            p = 2 * j + k
            self.copy1(p, k).wait_recv()
            for a in range(2):
                if k:
                    self.own[p, at.core, at.y, a] = self.own[p, at.core, at.y, a] + self.got1[p, a]
                else:
                    self.own[p, at.core, a, at.x] = self.own[p, at.core, a, at.x] + self.got1[p, a]
            self.copy2(p, k).start()

    def stage3(self, j):
        at = self.place
        for k in range(2):
            p = 2 * j + k
            self.copy2(p, k).wait_recv()
            self.own[p, at.core, at.y, at.x] = self.own[p, at.core, at.y, at.x] + self.got2[p]
        self.hop(j, 0)

    def hop(self, j, step):
        at = self.place
        last = at.n_seq - 1

        @pl.when(at.z == step)
        def _():
            for k in range(2):
                p = 2 * j + k
                if step:
                    self.up(p, False).wait_recv()
                    self.got2[p] = self.low_z[p] + self.own[p, at.core, at.y, at.x]
                self.up(p, step == 0).start()

        @pl.when(at.z == last - step)
        def _():
            for k in range(2):
                p = 2 * j + k
                if step:
                    self.down(p, False).wait_recv()
                    self.got1[p, 0] = self.high_z[p] + self.own[p, at.core, at.y, at.x]
                self.down(p, step == 0).start()

    def finish(self, j, out, out_sems):
        at = self.place
        last = at.n_seq - 1
        for k in range(2):
            p = 2 * j + k

            @pl.when(at.z == last)
            def _():
                self.up(p, False).wait_recv()
                self.low_z[p] = self.low_z[p] + self.own[p, at.core, at.y, at.x]

            @pl.when(at.z == 0)
            def _():
                self.down(p, False).wait_recv()
                self.low_z[p] = self.high_z[p] + self.own[p, at.core, at.y, at.x]

            @pl.when((at.z > 0) & (at.z < last))
            def _():
                total = self.low_z[p].astype(F32) + self.high_z[p].astype(F32)
                self.low_z[p] = (total + self.own[p, at.core, at.y, at.x].astype(F32)).astype(LOW)

            pltpu.make_async_copy(self.low_z.at[p], out.at[p], out_sems.at[p]).start()

    def drain(self, j, out, out_sems):
        at = self.place
        last = at.n_seq - 1
        for k in range(2):
            p = 2 * j + k
            self.copy0(p).wait_send()
            self.copy1(p, k).wait_send()
            self.copy2(p, k).wait_send()

            @pl.when(at.z == 0)
            def _():
                self.up(p, True).wait_send()

            @pl.when((at.z > 0) & (at.z < last))
            def _():
                self.up(p, False).wait_send()
                self.down(p, False).wait_send()

            @pl.when(at.z == last)
            def _():
                self.down(p, True).wait_send()

            pltpu.make_async_copy(self.low_z.at[p], out.at[p], out_sems.at[p]).wait()


FF_JOBS, ATT_JOBS = 6, 4
FF_ROWS, ATT_ROWS = 384, 288


def backward_kernel(
    n_dp, n_seq,
    x_hbm, cot_hbm, mixed_ref, bucket_ref, gain_one_ref, gain_two_ref,
    wq_hbm, wk_hbm, wv_hbm, wo_hbm, wg_hbm, wu_hbm, wd_hbm,
    probs_hbm, slope_up_hbm, slope_gate_hbm, activ_t_hbm, attended_t_hbm, q_hbm, k_hbm, v_hbm, k_t_hbm, resid_hbm,
    mixed_out, tokens_out, ff_out, att_out, small_out,
    ff_own, ff_got0, ff_got1, ff_got2, ff_low, ff_high, ff_sems, ff_out_sems,
    att_own, att_got0, att_got1, att_got2, att_low, att_high, att_sems, att_out_sems,
    small_own, small_got, small_sems,
    wq_ref, wk_ref, wv_ref, wo_ref, wgu_ref, wd_ref, probs_ref, slope_up_ref, slope_gate_ref,
    activ_t_ref, attended_t_ref, q_ref, k_ref, v_ref, k_t_ref, resid_ref,
    hidden_t_ref, acc_ref, branch_ref, d_att_ref, d_att_t_ref, d_q_t_ref, d_k_ref, d_v_ref, offset_ref,
    x_ref, load_sems, ff_load_sems, probs_sems, row_sems, own_sems,
):
    span, width = x_hbm.shape
    cot_ref = x_ref
    buckets_wide = bucket_ref.shape[1]
    heads = probs_hbm.shape[0]
    head_dim = width // heads
    blocks = span // 128
    pairs = heads // 2
    at = Place(n_dp, n_seq)

    loads = [
        pltpu.make_async_copy(src, dst, load_sems.at[i])
        for i, (src, dst) in enumerate(
            [
                (activ_t_hbm, activ_t_ref), (resid_hbm, resid_ref), (attended_t_hbm, attended_t_ref), (wo_hbm, wo_ref),
                (q_hbm, q_ref), (k_hbm, k_ref), (v_hbm, v_ref), (k_t_hbm, k_t_ref),
                (wq_hbm, wq_ref), (wk_hbm, wk_ref), (wv_hbm, wv_ref), (cot_hbm, x_ref),
            ]
        )
    ]
    for load in loads:
        load.start()

    def ff_loads(g, sub):
        cols = pl.ds(pl.multiple_of(g * 512 + sub * 256, 256), 256)
        lanes = pl.ds(sub * 256, 256)
        pairs_ = [
            (wd_hbm.at[cols, :], wd_ref.at[sub]),
            (wg_hbm.at[:, cols], wgu_ref.at[sub, :, pl.ds(0, 256)]),
            (wu_hbm.at[:, cols], wgu_ref.at[sub, :, pl.ds(256, 256)]),
            (slope_up_hbm.at[g, :, lanes], slope_up_ref.at[sub]),
            (slope_gate_hbm.at[g, :, lanes], slope_gate_ref.at[sub]),
        ]
        return [
            pltpu.make_async_copy(src, dst, ff_load_sems.at[i, sub]) for i, (src, dst) in enumerate(pairs_)
        ]

    def probs_load(pair, slot):
        return pltpu.make_async_copy(probs_hbm.at[pl.ds(2 * pair, 2)], probs_ref.at[slot], probs_sems.at[slot])

    for sub in range(2):
        for load in ff_loads(0, sub):
            load.start()
    probs_load(0, 0).start()

    barrier = pltpu.get_barrier_semaphore()
    peers = [at.core_peer, at.x_peer, at.y_peer] + [
        at.z_peer(lax.rem(at.z + i, n_seq)) for i in range(1, n_seq)
    ]
    for peer in peers:
        pl.semaphore_signal(barrier, inc=1, device_id=peer, device_id_type=MESH)
    pl.semaphore_wait(barrier, len(peers))

    ff = Sums(at, ff_own, ff_sems, ff_got0, ff_got1, ff_got2, ff_low, ff_high)
    att = Sums(at, att_own, att_sems, att_got0, att_got1, att_got2, att_low, att_high)

    def rows_back(src, out, kind):
        copies = []
        for i in range(1, n_seq):
            to = lax.rem(at.z + i, n_seq)
            copies.append(
                pltpu.make_async_remote_copy(
                    src_ref=src.at[pl.ds(pl.multiple_of(to * 128, 128), 128), :], dst_ref=out.at[at.z],
                    send_sem=row_sems.at[kind, 0, i], recv_sem=row_sems.at[kind, 1, i],
                    device_id=at.z_peer(to), device_id_type=MESH,
                )
            )
        copies.append(
            pltpu.make_async_copy(
                src.at[pl.ds(pl.multiple_of(at.z * 128, 128), 128), :], out.at[at.z], own_sems.at[kind]
            )
        )
        return copies

    for copy in rows_back(mixed_ref, mixed_out, 0):
        copy.start()

    loads[0].wait()
    loads[11].wait()
    for j in range(2):

        @pl.loop(0, GROUP)
        def _(s):
            product = dot(activ_t_ref[s, 128 * j : 128 * j + 128, :], cot_ref[...]).astype(LOW)
            for k in range(2):
                for i in range(width // 128):
                    ff_own[2 * j + k, s % 2, s // 4, (s // 2) % 2, 64 * i : 64 * i + 64, :] = product[
                        64 * k : 64 * k + 64, 128 * i : 128 * i + 128
                    ]

        ff.stage0(j)
    loads[1].wait()

    @pl.loop(0, blocks)
    def _(i):
        rows = pl.ds(pl.multiple_of(i * 128, 128), 128)
        resid = resid_ref[rows, :]
        hidden_t_ref[:, rows] = (resid * inverse_rms(resid) * gain_two_ref[...]).T.astype(LOW)

    ff.stage1(0)
    shard = width // GROUP
    tiles = wg_hbm.shape[1] // 512
    acc_ref[...] = jnp.zeros_like(acc_ref)

    @pl.loop(0, tiles)
    def _(g):
        job = 2 + g
        for sub in range(2):
            for load in ff_loads(g, sub):
                load.wait()
            d_act = dot_back(cot_ref[...], wd_ref[sub])
            d_gate = (d_act * slope_gate_ref[sub].astype(F32)).astype(LOW)
            d_upper = (d_act * slope_up_ref[sub].astype(F32)).astype(LOW)
            for k, d_half in enumerate((d_gate, d_upper)):
                product = dot(hidden_t_ref[...], d_half).astype(LOW)
                for s in range(GROUP):
                    for i in range(2):
                        place = shard * (2 * sub + i)
                        ff_own[2 * job + k, s % 2, s // 4, (s // 2) % 2, place : place + shard, :] = product[
                            shard * s : shard * s + shard, 128 * i : 128 * i + 128
                        ]
            if sub:
                ff.stage0(job)
            d_both = jnp.concatenate([d_gate, d_upper], axis=1)
            for tile in range(width // 256):
                cols = slice(256 * tile, 256 * tile + 256)
                acc_ref[:, cols] += dot_back(d_both, wgu_ref[sub, cols, :])

            @pl.when(g < tiles - 1)
            def _():
                for load in ff_loads(g + 1, sub):
                    load.start()

        ff.stage1(job - 1)

    def norm_back(vector_ref, gain_ref, extra_ref, low_ref, row):
        total = jnp.zeros((1, width), F32)
        for i in range(blocks):
            rows = slice(128 * i, 128 * i + 128)
            vector = vector_ref[rows, :].astype(F32)
            scale = inverse_rms(vector)
            normed = vector * scale
            grad = acc_ref[rows, :]
            total = total + jnp.sum(grad * normed, axis=0, keepdims=True)
            inner = grad * gain_ref[...]
            result = extra_ref[rows, :].astype(F32) + scale * (
                inner - normed * jnp.mean(inner * normed, -1, keepdims=True)
            )
            acc_ref[rows, :] = result
            low_ref[rows, :] = result.astype(LOW)
        small_own[0, row : row + 1, :] = total

    norm_back(resid_ref, gain_two_ref, cot_ref, branch_ref, 12)
    x_load = pltpu.make_async_copy(x_hbm, x_ref, load_sems.at[12])
    x_load.start()
    ff.stage1(FF_JOBS - 1)

    def share(sums, j, left_t, right):
        for k in range(2):
            half = slice(width // 2 * k, width // 2 * k + width // 2)
            product = dot(left_t, right[:, half]).astype(LOW)
            for s in range(GROUP):
                for i in range(width // 256):
                    sums.own[2 * j + k, s % 2, s // 4, (s // 2) % 2, shard * i : shard * i + shard, :] = product[
                        shard * s : shard * s + shard, 128 * i : 128 * i + 128
                    ]
        sums.stage0(j)

    loads[2].wait()
    share(att, 0, attended_t_ref[...], branch_ref[...])
    loads[3].wait()
    for tile in range(width // 256):
        rows = slice(256 * tile, 256 * tile + 256)
        d_att = dot_back(branch_ref[...], wo_ref[rows, :])
        d_att_t_ref[rows, :] = d_att.T.astype(LOW)
        for i in range(2):
            d_att_ref[2 * tile + i] = d_att[:, 128 * i : 128 * i + 128].astype(LOW)
    att.stage1(0)
    for i in range(4, 8):
        loads[i].wait()
    left_half = lax.broadcasted_iota(jnp.int32, (span, 128), 1) < head_dim
    flip = (
        lax.broadcasted_iota(jnp.int32, (128, 128), 0) + lax.broadcasted_iota(jnp.int32, (128, 128), 1) == 127
    ).astype(F32)

    @pl.loop(0, pairs)
    def _(pair):
        slot = lax.rem(pair, 2)
        probs_load(pair, slot).wait()

        @pl.when(pair < pairs - 1)
        def _():
            probs_load(pair + 1, 1 - slot).start()

        values = v_ref[pair]
        d_att = d_att_ref[pair]
        queries = q_ref[pair]
        lanes = pl.ds(pl.multiple_of(pair * 128, 128), 128)
        d_values = jnp.zeros((span, 128), F32)
        d_keys = jnp.zeros((span, 128), F32)
        for b in range(2):
            h = 2 * pair + b
            rows = pl.ds(pl.multiple_of(h * head_dim, head_dim), head_dim)
            d_att_t = zero_padded(d_att_t_ref[rows, :], b)
            k_t = k_t_ref[rows, :]
            sides = []
            sums = [None] * (2 * blocks - 1)
            for half in range(span // 256):
                cols = slice(256 * half, 256 * half + 256)
                d_probs = dot(values, d_att_t[:, cols])
                probs = probs_ref[slot, b, :, cols].astype(F32)
                inner = jnp.sum(probs * d_probs, axis=0, keepdims=True)
                d_scores = probs * (d_probs - inner)
                for kb in range(blocks):
                    for i in range(2):
                        d = kb - (2 * half + i) + blocks - 1
                        block = d_scores[128 * kb : 128 * kb + 128, 128 * i : 128 * i + 128]
                        sums[d] = block if sums[d] is None else sums[d] + block
                d_scores = d_scores.astype(LOW)
                d_q_t_ref[rows, cols] = dot(k_t, d_scores).astype(LOW)
                sides.append(d_scores)
            mine = left_half if b == 0 else jnp.logical_not(left_half)
            d_values = d_values + dot(probs_ref[slot, b], jnp.where(mine, d_att, jnp.zeros_like(d_att)))
            d_keys = d_keys + dot(
                jnp.concatenate(sides, axis=1), jnp.where(mine, queries, jnp.zeros_like(queries))
            )
            totals = []
            for d in range(2 * blocks - 1):
                flipped = jnp.dot(sums[d], flip, precision=lax.Precision.HIGHEST, preferred_element_type=F32)
                wide = jnp.concatenate([flipped, jnp.zeros((128, 128), F32)], axis=1)
                totals.append(jnp.sum(pltpu.roll(wide, 0, 1, stride=1, stride_axis=0), axis=0, keepdims=True))
            pieces = [totals[0][:, :128]]
            for d in range(1, 2 * blocks - 1):
                pieces.append(totals[d - 1][:, 128:] + totals[d][:, :128])
            pieces.append(totals[-1][:, 128:])
            offset_ref[pl.ds(h, 1), :] = jnp.concatenate(pieces, axis=1)
        d_v_ref[:, lanes] = d_values.astype(LOW)
        d_k_ref[:, lanes] = d_keys.astype(LOW)

    x_load.wait()

    @pl.loop(0, blocks)
    def _(i):
        rows = pl.ds(pl.multiple_of(i * 128, 128), 128)
        inputs = x_ref[rows, :].astype(F32)
        hidden_t_ref[:, rows] = (inputs * inverse_rms(inputs) * gain_one_ref[...]).T.astype(LOW)

    share(att, 1, hidden_t_ref[...], d_v_ref[...])
    share(att, 2, hidden_t_ref[...], d_k_ref[...])
    att.stage1(1)
    branch_ref[...] = d_q_t_ref[...].T
    share(att, 3, hidden_t_ref[...], branch_ref[...])
    att.stage1(2)
    for i in range(8, 11):
        loads[i].wait()
    for tile in range(width // 256):
        rows = slice(256 * tile, 256 * tile + 256)
        resid_ref[:, rows] = acc_ref[:, rows]
        acc_ref[:, rows] = (
            dot_back(branch_ref[...], wq_ref[rows, :])
            + dot_back(d_k_ref[...], wk_ref[rows, :])
            + dot_back(d_v_ref[...], wv_ref[rows, :])
        )
    att.stage1(3)
    norm_back(x_ref, gain_one_ref, resid_ref, branch_ref, 13)
    for copy in rows_back(branch_ref, tokens_out, 1):
        copy.start()

    one_hot = (
        lax.broadcasted_iota(jnp.int32, (128, buckets_wide), 0) == bucket_ref[...]
    ).astype(F32)
    small_own[0, :12, :128] = lax.dot_general(
        offset_ref[:12, :], one_hot, (((1,), (1,)), ((), ())),
        precision=lax.Precision.HIGHEST, preferred_element_type=F32,
    )
    small_peers = [at.core_peer, at.x_peer, at.y_peer]
    bit = 1
    while bit < n_seq:
        small_peers.append(at.z_pair(bit))
        bit *= 2

    def small_copy(i):
        return remote(small_own.at[i], small_got.at[i], small_sems, i, small_peers[i])

    small_copy(0).start()

    def small_step(i):
        small_copy(i).wait_recv()
        small_own[i + 1] = small_own[i] + small_got[i]
        if i + 1 < len(small_peers):
            small_copy(i + 1).start()

    for sums, jobs in ((ff, FF_JOBS), (att, ATT_JOBS)):

        @pl.loop(0, jobs)
        def _(j):
            sums.stage2(j)

    for sums, jobs in ((ff, FF_JOBS), (att, ATT_JOBS)):

        @pl.loop(0, jobs)
        def _(j):
            sums.stage3(j)

    for step in range(1, n_seq - 1):
        for sums, jobs in ((ff, FF_JOBS), (att, ATT_JOBS)):

            @pl.loop(0, jobs)
            def _(j):
                sums.hop(j, step)

    for i in range(len(small_peers)):
        small_step(i)
    for sums, jobs, out, sems in ((ff, FF_JOBS, ff_out, ff_out_sems), (att, ATT_JOBS, att_out, att_out_sems)):

        @pl.loop(0, jobs)
        def _(j):
            sums.finish(j, out, sems)

    small_out[...] = small_own[len(small_peers)]
    for sums, jobs, out, sems in ((ff, FF_JOBS, ff_out, ff_out_sems), (att, ATT_JOBS, att_out, att_out_sems)):

        @pl.loop(0, jobs)
        def _(j):
            sums.drain(j, out, sems)

    for i in range(len(small_peers)):
        small_copy(i).wait_send()
    for copy in rows_back(mixed_ref, mixed_out, 0) + rows_back(branch_ref, tokens_out, 1):
        copy.wait()


def backward(n_dp, n_seq, x, cot, mixed, buckets, gain_one, gain_two, weights, saved):
    span, width = x.shape
    wq, wk, wv, wo, wg, wu, wd = weights
    probs = saved[0]
    heads = probs.shape[0]
    ff_pieces, att_pieces = 2 * FF_JOBS, 2 * ATT_JOBS
    low = lambda *shape: VMEM(shape, LOW)
    dma = pltpu.SemaphoreType.DMA
    steps = 3 + (n_seq - 1).bit_length()

    def sums(pieces, rows):
        return [
            low(pieces, 2, 2, 2, rows, 128), low(pieces, 2, 2, rows, 128), low(pieces, 2, rows, 128),
            low(pieces, rows, 128), low(pieces, rows, 128), low(pieces, rows, 128),
            dma((5, 2, pieces)), dma((pieces,)),
        ]

    pairs = low(heads // 2, span, 128)
    whole = low(width, width)
    any_, vmem = pl.BlockSpec(memory_space=pl.ANY), pl.BlockSpec(memory_space=VMEM)
    return pl.pallas_call(
        functools.partial(backward_kernel, n_dp, n_seq),
        out_shape=[
            jax.ShapeDtypeStruct((n_seq, span // n_seq, width), LOW),
            jax.ShapeDtypeStruct((n_seq, span // n_seq, width), LOW),
            jax.ShapeDtypeStruct((ff_pieces, FF_ROWS, 128), LOW),
            jax.ShapeDtypeStruct((att_pieces, ATT_ROWS, 128), LOW),
            jax.ShapeDtypeStruct((16, width), F32),
        ],
        in_specs=[any_] * 3 + [vmem] * 3 + [any_] * (7 + len(saved)),
        out_specs=[any_] * 4 + [vmem],
        scratch_shapes=sums(ff_pieces, FF_ROWS)
        + sums(att_pieces, ATT_ROWS)
        + [VMEM((steps + 1, 16, width), F32), VMEM((steps, 16, width), F32), dma((2, steps))]
        + [
            whole, whole, whole, whole, low(2, width, 512), low(2, 256, width),
            low(2, 2, span, span), low(2, span, 256), low(2, span, 256),
            low(*saved[3].shape), low(width, span), pairs, pairs, pairs, low(width, span), VMEM((span, width), F32),
            low(width, span), VMEM((span, width), F32), low(span, width), pairs, low(width, span),
            low(width, span), low(span, width), low(span, width), VMEM((16, 1024), F32),
            low(span, width), dma((13,)), dma((5, 2)), dma((2,)), dma((2, 2, n_seq)), dma((2,)),
        ],
        compiler_params=pltpu.CompilerParams(
            collective_id=0, has_side_effects=True, vmem_limit_bytes=VMEM_BYTES
        ),
        name="backward",
    )(x, cot, mixed, buckets, gain_one, gain_two, wq, wk, wv, wo, wg, wu, wd, *saved)


def outputs_kernel(
    n_dp, mixed_ref, tokens_ref, ff_ref, att_ref, small_ref,
    mixed_out, tokens_out, gn_one_out, gq_out, gk_out, gv_out, go_out, table_out, gn_two_out, gg_out, gu_out, gd_out,
):
    mixed_out[...] = mixed_ref[...]
    tokens_out[...] = tokens_ref[...].astype(F32)
    width = mixed_ref.shape[-1]
    shard = width // GROUP
    for j, out in enumerate((go_out, gv_out, gk_out, gq_out)):
        for k in range(2):
            for i in range(width // 256):
                col = width // 2 * k + 128 * i
                out[:, col : col + 128] = att_ref[2 * j + k, shard * i : shard * i + shard, :].astype(F32)
    for p in range(4):
        for i in range(width // 128):
            gd_out[64 * p : 64 * p + 64, 128 * i : 128 * i + 128] = ff_ref[p, 64 * i : 64 * i + 64, :].astype(F32)
    for g in range(4):
        for k, out in enumerate((gg_out, gu_out)):
            for i in range(4):
                col = 512 * g + 128 * i
                out[:, col : col + 128] = ff_ref[4 + 2 * g + k, shard * i : shard * i + shard, :].astype(F32)
    table_out[...] = small_ref[: table_out.shape[1], :128].T[: table_out.shape[0], :]
    mine = lax.axis_index("dp") // (n_dp // GROUP)
    for row, out in ((12, gn_two_out), (13, gn_one_out)):
        total = jnp.zeros((1, shard), F32)
        for s in range(GROUP):
            total = total + jnp.where(mine == s, small_ref[row : row + 1, shard * s : shard * s + shard], 0.0)
        out[...] = total


def outputs(n_dp, buckets, heads, mixed, tokens, ff, att, small):
    width = mixed.shape[-1]
    shard = width // GROUP
    full = lambda *shape: jax.ShapeDtypeStruct(shape, F32)
    return pl.pallas_call(
        functools.partial(outputs_kernel, n_dp),
        out_shape=[
            jax.ShapeDtypeStruct(mixed.shape, LOW), full(*tokens.shape), full(1, shard),
            full(shard, width), full(shard, width), full(shard, width), full(shard, width), full(buckets, heads),
            full(1, shard), full(shard, 2048), full(shard, 2048), full(256, width),
        ],
        compiler_params=pltpu.CompilerParams(vmem_limit_bytes=VMEM_BYTES),
        name="outputs",
    )(mixed, tokens, ff, att, small)


def solution(mesh):
    n_dp, n_seq = mesh.shape["dp"], mesh.shape["seq"]

    def on_device(
        tokens, segments, offset_buckets, norm_attn, w_query, w_key, w_value, w_output, bias_table,
        norm_ff, w_gate, w_up, w_down, cotangent,
    ):
        width = tokens.shape[-1]
        x, seg, cot = [
            lax.all_to_all(v, "seq", split_axis=0, concat_axis=1, tiled=True) for v in (tokens, segments, cotangent)
        ]
        x, cot = x.reshape(-1, width), cot.reshape(-1, width)
        buckets = jnp.pad(offset_buckets, (0, 1)).reshape(1, -1)
        gain_one, gain_two = norm_attn.reshape(1, -1), norm_ff.reshape(1, -1)
        *saved, mixed = forward(
            x, seg, buckets, gain_one, w_query, w_key, w_value, w_output, bias_table, gain_two, w_gate, w_up, w_down
        )
        weights = (w_query, w_key, w_value, w_output, w_gate, w_up, w_down)
        sums = backward(n_dp, n_seq, x, cot, mixed, buckets, gain_one, gain_two, weights, saved)
        results = list(outputs(n_dp, bias_table.shape[0], bias_table.shape[1], *sums))
        results[2], results[8] = results[2].reshape(-1), results[8].reshape(-1)
        rest = n_dp // GROUP
        if rest > 1:
            groups = [[i * rest + j for j in range(rest)] for i in range(GROUP)]
            for i in (2, 3, 4, 5, 6, 8, 9, 10, 11):
                results[i] = lax.psum_scatter(
                    results[i], "dp", scatter_dimension=0, axis_index_groups=groups, tiled=True
                )
            results[7] = lax.psum(results[7], "dp", axis_index_groups=groups)
        return tuple(results)

    rows, shares = P("dp", "seq", None), P("dp", None)
    return jax.shard_map(
        on_device,
        mesh=mesh,
        in_specs=(rows, P("dp", "seq")) + (P(),) * 11 + (rows,),
        out_specs=(rows, rows, P("dp"), shares, shares, shares, shares, P(), P("dp"), shares, shares, shares),
        check_vma=False,
    )
```

time: 663 us -> 248 us (0.37)
  waiting for transfers between devices: 275 us -> 0.01 us
  Pallas kernels: 0 us -> 200 us
  matrix products: 139 us -> 0 us
  local copies, waits for them, and re-layouts: 62.2 us -> 4.73 us
  other arithmetic: 55.5 us -> 0 us
  blocking collectives: 87.9 us -> 35.2 us
  starting transfers between devices: 20.1 us -> 3.5 us
  between operations: 15.8 us -> 0.72 us
    reduce_scatter x7 -> x0, waiting for transfers between devices: 274 us -> none  [the longest x1 63.5 us: on_device(): lax.psum_scatter(grad_gate, 'dp', scatter_dimension=0, tiled=True)]
    pallas_call x0 -> x3, Pallas kernels: none -> 200 us  [the longest x1 157 us: backward(): pl.pallas_call(functools.partial(backward_kernel, n_dp, n_seq), out_shape...]
    dot_general x29 -> x0, matrix products: 139 us -> none  [the longest x7 27.8 us: dot_rows(): lax.dot_general(left, right, (((0,), (0,)), ((), ())), preferred_element_...]
    psum x2 -> x0, blocking collectives: 62.3 us -> none  [the longest x1 44.6 us: on_device(): table_total = lax.psum(grad_table_local, ('dp', 'seq'))]
    convert_element_type x21 -> x0, other arithmetic: 35.5 us -> none  [the longest x1 7.02 us: on_device(): grad_scores = (probs * (grad_probs - inner)).astype(jnp.bfloat16)]
    unnamed x86 -> x12, local copies, waits for them, and re-layouts: 28.7 us -> 2.97 us
    all_to_all x1 -> x2, blocking collectives: 12.1 us -> 35.2 us  [on_device(): lax.all_to_all(v, 'seq', split_axis=0, concat_axis=1, tiled=True)]
    all_to_all x4 -> x1, starting transfers between devices: 19.1 us -> 3.5 us  [on_device(): lax.all_to_all(v, 'seq', split_axis=0, concat_axis=1, tiled=True)]
  transfers between devices with their start and end apart: 12 -> 1, of which waited for: 5 -> 0; matrix products, arithmetic and copies ran while one was open for 33% -> 1% of each run, Pallas kernels for 0% -> 16%
where the time goes in v1:
time: 248 us; the launch traced here: 245 us
  Pallas kernels  200 us (81%)
  blocking collectives  35.2 us (14%)
  local copies, waits for them, and re-layouts  4.73 us (2%)
  starting transfers between devices  3.5 us (1%)
    pallas_call x1, Pallas kernels, backward(): pl.pallas_call(functools.partial(backward_kernel, n_dp, n_seq), out_shape...  157 us
    pallas_call x1, Pallas kernels, forward(): pl.pallas_call(forward_kernel, out_shape=[low(heads, span, span), low(ff...  39.2 us
    all_to_all x2, blocking collectives, on_device(): lax.all_to_all(v, 'seq', split_axis=0, concat_axis=1, tiled=True)  35.2 us
  transfers between devices with their start and end apart: 1, of which 0 were waited for; matrix products, arithmetic and copies ran while one was open for 1% of the time, Pallas kernels for 16%

profile of v1, /device:TPU:0, one launch (start us, length us, event | category | flops | bytes accessed | tf_op | source)
XLA Modules:
  0.0 244.6 jit_solution(4434841365656299985)
XLA Ops:
  0.6 0.0 copy-start.2
  0.7 0.0 copy-start.3
  0.7 0.0 copy-start.1
  0.7 0.0 copy-start.4
  0.7 11.9 %all_to_all.34 = s32[4,1,128]{2,1,0:T(1,128)} all-to-all(s32[4,1,128]{2,1,0:T(1,128)} %bitcast.13), channel_id=1, replica_groups=mesh['dp'=8,'seq'=4] {'seq'}, dimensions={0} | all-to-all | bytes 4096 | tf_op jit(solution)/shard_map/all_to_all | solution.py:791
  12.6 23.3 %all_to_all.35 = bf16[4,128,768]{2,1,0:T(8,128)(2,1)} all-to-all(bf16[4,128,768]{2,1,0:T(8,128)(2,1)} %param.14), channel_id=1, replica_groups=mesh['dp'=8,'seq'=4] {'seq'}, dimensions={0} | all-to-all | bytes 1572864 | tf_op jit(solution)/shard_map/all_to_all | solution.py:791
  35.9 3.5 %all-to-all-start.1 = ((bf16[4,128,768]{2,1,0:T(8,128)(2,1)}), bf16[4,128,768]{2,1,0:T(8,128)(2,1)S(1)}, u32[]{:S(2)}, u32[]{:S(2)}) async-start(bf16[4,128,768]{2,1,0:T(8,128)(2,1)} %param.27), calls=%async_computation.1 | async-start | bytes 1572864 | tf_op jit(solution)/shard_map/all_to_all | solution.py:791
  39.4 0.0 copy-done.2
  39.4 0.6 reshape.62.gain_one_ref
  40.0 0.0 copy-done.3
  40.0 0.6 reshape.63.gain_two_ref
  40.6 0.0 copy-done.1
  40.6 0.7 copy.28.table_ref
  41.3 0.0 copy-done.4
  41.3 0.6 pad.4
  41.9 39.2 %forward.1 = (bf16[12,512,512]{2,1,0:T(8,128)(2,1)}, bf16[4,512,512]{2,1,0:T(8,128)(2,1)}, bf16[4,512,512]{2,1,0:T(8,128)(2,1)}, bf16[8,256,512]{2,1,0:T(8,128)(...) custom-call(bf16[512,768]{1,0:T(8,128)(2,1)} %bitcast.7, ...), custom_call_target="tpu_custom_call" | custom-call | tf_op jit(solution)/shard_map/forward/pallas_call | solution.py:158
  81.1 0.0 all-to-all-done.1
  81.1 0.0 copy-start
  81.1 0.9 copy-done
  82.0 156.6 %backward.1 = (bf16[4,128,768]{2,1,0:T(8,128)(2,1)}, bf16[4,128,768]{2,1,0:T(8,128)(2,1)}, bf16[12,384,128]{2,1,0:T(8,128)(2,1)}, bf16[8,288,128]{2,1,0:T(8,128)(2,1)}, f32[16,768]{1,0:T(8,128)}) custom-call(bf16[512,768]{1,0:T(8,128)(2,1)} %bitcast.8, bf16[512,768]{1,0:T(8,128)(2,1)} %bitcast.9, bf16[512,768]{1,0:T(8,128)(2,1)} %get-tuple-element.40.mixed_ref, ...), custom_call_target="tpu_custom_call" | custom-call | tf_op jit(solution)/shard_map/backward/pallas_call | solution.py:707
  238.6 4.6 %outputs.1 = (bf16[4,128,768]{2,1,0:T(8,128)(2,1)}, f32[4,128,768]{2,1,0:T(8,128)}, f32[1,96]{1,0:T(1,128)}, f32[96,768]{1,0:T(8,128)}, f32[96,768]{1,0:T(8,128)...) custom-call(bf16[4,128,768]{2,1,0:T(8,128)(2,1)} %get-tuple-element., ...), custom_call_target="tpu_custom_call" | custom-call | tf_op jit(solution)/shard_map/outputs/pallas_call | solution.py:770
  243.2 1.4 copy.29
Async XLA Ops:
  0.6 38.8 %copy-start.2 = (f32[768]{0:T(1024)S(1)}, f32[768]{0:T(1024)}, u32[]{:S(2)}) copy-start(f32[768]{0:T(1024)} %param.17) | copy-start | bytes 9220
  0.7 39.4 %copy-start.3 = (f32[768]{0:T(1024)S(1)}, f32[768]{0:T(1024)}, u32[]{:S(2)}) copy-start(f32[768]{0:T(1024)} %param.23) | copy-start | bytes 9220
  0.7 39.9 %copy-start.1 = (f32[32,12]{0,1:T(8,128)S(1)}, f32[32,12]{0,1:T(8,128)}, u32[]{:S(2)}) copy-start(f32[32,12]{0,1:T(8,128)} %param.22) | copy-start | bytes 4612
  0.7 40.6 %copy-start.4 = (s32[1023]{0:T(1024)S(1)}, s32[1023]{0:T(1024)}, u32[]{:S(2)}) copy-start(s32[1023]{0:T(1024)} %param.16) | copy-start | bytes 12280
  35.9 45.2 %all-to-all-start.1 = ((bf16[4,128,768]{2,1,0:T(8,128)(2,1)}), bf16[4,128,768]{2,1,0:T(8,128)(2,1)S(1)}, u32[]{:S(2)}, u32[]{:S(2)}) async-start(bf16[4,128,768]{2,1,0:T(8,128)(2,1)} %param.27), calls=%async_computation.1 | async-start | bytes 1572864 | tf_op jit(solution)/shard_map/all_to_all | solution.py:791
  81.1 0.9 copy-start

commit v2 on v1

v2 whole, which is shorter than its diff:
```python
import functools

import jax
import jax.numpy as jnp
from jax import lax
from jax.experimental import pallas as pl
from jax.experimental.pallas import tpu as pltpu
from jax.sharding import PartitionSpec as P

MESH = pl.DeviceIdType.MESH
VMEM = pltpu.VMEM
LOW = jnp.bfloat16
F32 = jnp.float32
EPSILON = 1e-06
MASKED = -1e30
GROUP = 8
VMEM_BYTES = 63 * 2**20


def dot(left, right):
    return jnp.dot(left, right, preferred_element_type=F32)


def dot_back(left, right):
    return lax.dot_general(left, right, (((1,), (1,)), ((), ())), preferred_element_type=F32)


def inverse_rms(values):
    return lax.rsqrt(jnp.mean(values * values, -1, keepdims=True) + EPSILON)


def zero_padded(block, half):
    blank = jnp.zeros_like(block)
    return jnp.concatenate([blank, block] if half else [block, blank], axis=0)


class Place:
    def __init__(self, n_dp, n_seq):
        stride = n_dp // GROUP
        dp = lax.axis_index("dp")
        z = lax.axis_index("seq")
        index = dp // stride
        self.n_seq = n_seq
        self.core, self.x, self.y, self.z = index % 2, (index // 2) % 2, index // 4, z
        self.dp = dp
        self.core_peer = (dp + stride * (1 - 2 * self.core), z)
        self.x_peer = (dp + 2 * stride * (1 - 2 * self.x), z)
        self.y_peer = (dp + 4 * stride * (1 - 2 * self.y), z)

    def z_peer(self, z):
        return (self.dp, z)

    def z_pair(self, bit):
        return (self.dp, self.z + bit * (1 - 2 * ((self.z // bit) % 2)))


def remote(src, dst, sems, index, peer):
    return pltpu.make_async_remote_copy(
        src_ref=src, dst_ref=dst, send_sem=sems.at[0, index], recv_sem=sems.at[1, index],
        device_id=peer, device_id_type=MESH,
    )


class Sums:
    def __init__(self, place, own, sems, got0, got1, got2, low_z, high_z):
        self.place, self.own, self.sems = place, own, sems
        self.got0, self.got1, self.got2, self.low_z, self.high_z = got0, got1, got2, low_z, high_z

    def copy0(self, p):
        at = self.place
        return remote(self.own.at[p, 1 - at.core], self.got0.at[p], self.sems.at[0], p, at.core_peer)

    def copy1(self, p, k):
        at = self.place
        mine = self.own.at[p, at.core]
        src = mine.at[1 - at.y] if k else mine.at[:, 1 - at.x]
        return remote(src, self.got1.at[p], self.sems.at[1], p, at.y_peer if k else at.x_peer)

    def copy2(self, p, k):
        at = self.place
        mine = self.own.at[p, at.core]
        src = mine.at[at.y, 1 - at.x] if k else mine.at[1 - at.y, at.x]
        return remote(src, self.got2.at[p], self.sems.at[2], p, at.x_peer if k else at.y_peer)

    def kept(self, p):
        at = self.place
        return self.own.at[p, at.core, at.y, at.x]

    def up(self, p, first):
        src = self.kept(p) if first else self.got2.at[p]
        return remote(src, self.low_z.at[p], self.sems.at[3], p, self.place.z_peer(self.place.z + 1))

    def down(self, p, first):
        src = self.kept(p) if first else self.got1.at[p, 0]
        return remote(src, self.high_z.at[p], self.sems.at[4], p, self.place.z_peer(self.place.z - 1))

    def stage0(self, j):
        for k in range(2):
            self.copy0(2 * j + k).start()

    def stage1(self, j):
        at = self.place
        for k in range(2):
            p = 2 * j + k
            self.copy0(p).wait_recv()
            for a in range(2):
                for b in range(2):
                    self.own[p, at.core, a, b] = self.own[p, at.core, a, b] + self.got0[p, a, b]
            self.copy1(p, k).start()

    def stage2(self, j):
        at = self.place
        for k in range(2):
            p = 2 * j + k
            self.copy1(p, k).wait_recv()
            for a in range(2):
                if k:
                    self.own[p, at.core, at.y, a] = self.own[p, at.core, at.y, a] + self.got1[p, a]
                else:
                    self.own[p, at.core, a, at.x] = self.own[p, at.core, a, at.x] + self.got1[p, a]
            self.copy2(p, k).start()

    def stage3(self, j):
        at = self.place
        for k in range(2):
            p = 2 * j + k
            self.copy2(p, k).wait_recv()
            self.own[p, at.core, at.y, at.x] = self.own[p, at.core, at.y, at.x] + self.got2[p]
        self.hop(j, 0)

    def hop(self, j, step):
        at = self.place
        last = at.n_seq - 1

        @pl.when(at.z == step)
        def _():
            for k in range(2):
                p = 2 * j + k
                if step:
                    self.up(p, False).wait_recv()
                    self.got2[p] = self.low_z[p] + self.own[p, at.core, at.y, at.x]
                self.up(p, step == 0).start()

        @pl.when(at.z == last - step)
        def _():
            for k in range(2):
                p = 2 * j + k
                if step:
                    self.down(p, False).wait_recv()
                    self.got1[p, 0] = self.high_z[p] + self.own[p, at.core, at.y, at.x]
                self.down(p, step == 0).start()

    def finish(self, j, out, out_sems):
        at = self.place
        last = at.n_seq - 1
        for k in range(2):
            p = 2 * j + k

            @pl.when(at.z == last)
            def _():
                self.up(p, False).wait_recv()
                self.low_z[p] = self.low_z[p] + self.own[p, at.core, at.y, at.x]

            @pl.when(at.z == 0)
            def _():
                self.down(p, False).wait_recv()
                self.low_z[p] = self.high_z[p] + self.own[p, at.core, at.y, at.x]

            @pl.when((at.z > 0) & (at.z < last))
            def _():
                total = self.low_z[p].astype(F32) + self.high_z[p].astype(F32)
                self.low_z[p] = (total + self.own[p, at.core, at.y, at.x].astype(F32)).astype(LOW)

            pltpu.make_async_copy(self.low_z.at[p], out.at[p], out_sems.at[p]).start()

    def drain(self, j, out, out_sems):
        at = self.place
        last = at.n_seq - 1
        for k in range(2):
            p = 2 * j + k
            self.copy0(p).wait_send()
            self.copy1(p, k).wait_send()
            self.copy2(p, k).wait_send()

            @pl.when(at.z == 0)
            def _():
                self.up(p, True).wait_send()

            @pl.when((at.z > 0) & (at.z < last))
            def _():
                self.up(p, False).wait_send()
                self.down(p, False).wait_send()

            @pl.when(at.z == last)
            def _():
                self.down(p, True).wait_send()

            pltpu.make_async_copy(self.low_z.at[p], out.at[p], out_sems.at[p]).wait()


FF_JOBS, ATT_JOBS = 6, 4
FF_ROWS, ATT_ROWS = 384, 288


def layer_kernel(
    n_dp, n_seq,
    tokens_hbm, cot_hbm, seg_ref, bucket_ref, gain_one_ref, gain_two_ref, table_ref,
    wq_hbm, wk_hbm, wv_hbm, wo_hbm, wg_hbm, wu_hbm, wd_hbm,
    mixed_out, tokens_out, ff_out, att_out, small_out, probs_hbm, slope_up_hbm, slope_gate_hbm,
    ff_own, ff_got0, ff_got1, ff_got2, ff_low, ff_high, ff_sems, ff_out_sems,
    att_own, att_got0, att_got1, att_got2, att_low, att_high, att_sems, att_out_sems,
    small_own, small_got, small_sems,
    x_ref, cot_ref, seg_send_ref, seg_rows_ref, mixed_ref,
    wq_ref, wk_ref, wv_ref, wo_ref, wgu_ref, wd_ref, probs_ref, slope_up_ref, slope_gate_ref,
    activ_t_ref, attended_t_ref, q_ref, k_ref, v_ref, k_t_ref, resid_ref, acc_ref, branch_ref,
    d_att_t_ref, d_q_t_ref, offset_ref,
    load_sems, ff_load_sems, slope_sems, probs_sems, row_sems, own_sems,
):
    span, width = x_ref.shape
    buckets, heads = table_ref.shape
    buckets_wide = bucket_ref.shape[1]
    head_dim = width // heads
    blocks = span // 128
    pairs = heads // 2
    tiles = wg_hbm.shape[1] // 512
    shard = width // GROUP
    at = Place(n_dp, n_seq)

    loads = [
        pltpu.make_async_copy(src, dst, load_sems.at[i])
        for i, (src, dst) in enumerate([(wq_hbm, wq_ref), (wk_hbm, wk_ref), (wv_hbm, wv_ref), (wo_hbm, wo_ref)])
    ]

    def weight_loads(g, sub):
        cols = pl.ds(pl.multiple_of(g * 512 + sub * 256, 256), 256)
        sides = [
            (wd_hbm.at[cols, :], wd_ref.at[sub]),
            (wg_hbm.at[:, cols], wgu_ref.at[sub, :, pl.ds(0, 256)]),
            (wu_hbm.at[:, cols], wgu_ref.at[sub, :, pl.ds(256, 256)]),
        ]
        return [pltpu.make_async_copy(src, dst, ff_load_sems.at[i, sub]) for i, (src, dst) in enumerate(sides)]

    def slope_copies(g, sub, store):
        sides = [
            (slope_up_hbm.at[2 * g + sub], slope_up_ref.at[sub]),
            (slope_gate_hbm.at[2 * g + sub], slope_gate_ref.at[sub]),
        ]
        return [
            pltpu.make_async_copy(*((dst, src) if store else (src, dst)), slope_sems.at[i, sub])
            for i, (src, dst) in enumerate(sides)
        ]

    def probs_copy(pair, slot, store):
        sides = (probs_hbm.at[pl.ds(2 * pair, 2)], probs_ref.at[slot])
        return pltpu.make_async_copy(*(sides[::-1] if store else sides), probs_sems.at[slot])

    def start(copies):
        for copy in copies:
            copy.start()

    def wait(copies):
        for copy in copies:
            copy.wait()

    start(loads)
    for i in range(n_seq):
        seg_send_ref[i] = jnp.broadcast_to(seg_ref[i : i + 1, :], (8, 128))

    barrier = pltpu.get_barrier_semaphore()
    peers = [at.core_peer, at.x_peer, at.y_peer] + [
        at.z_peer(lax.rem(at.z + i, n_seq)) for i in range(1, n_seq)
    ]
    for peer in peers:
        pl.semaphore_signal(barrier, inc=1, device_id=peer, device_id_type=MESH)
    pl.semaphore_wait(barrier, len(peers))

    ff = Sums(at, ff_own, ff_sems, ff_got0, ff_got1, ff_got2, ff_low, ff_high)
    att = Sums(at, att_own, att_sems, att_got0, att_got1, att_got2, att_low, att_high)

    def block(z):
        return pl.ds(pl.multiple_of(z * 128, 128), 128)

    def exchange(kind, src, dst):
        copies = []
        for i in range(1, n_seq):
            to = lax.rem(at.z + i, n_seq)
            copies.append(
                pltpu.make_async_remote_copy(
                    src_ref=src(to), dst_ref=dst(at.z),
                    send_sem=row_sems.at[kind, 0, i], recv_sem=row_sems.at[kind, 1, i],
                    device_id=at.z_peer(to), device_id_type=MESH,
                )
            )
        copies.append(pltpu.make_async_copy(src(at.z), dst(at.z), own_sems.at[kind]))
        return copies

    segs = exchange(0, lambda z: seg_send_ref.at[z], lambda z: seg_rows_ref.at[z])
    tokens_in = exchange(1, lambda z: tokens_hbm.at[z], lambda z: x_ref.at[block(z), :])
    cot_in = exchange(2, lambda z: cot_hbm.at[z], lambda z: cot_ref.at[block(z), :])
    mixed_back = exchange(3, lambda z: mixed_ref.at[block(z), :], lambda z: mixed_out.at[z])
    tokens_back = exchange(4, lambda z: branch_ref.at[block(z), :], lambda z: tokens_out.at[z])
    start(segs)
    start(tokens_in)
    for sub in range(2):
        start(weight_loads(0, sub))

    def forward(bias_ref, mask_ref):
        one_hot = (lax.broadcasted_iota(jnp.int32, (buckets, buckets_wide), 0) == bucket_ref[...]).astype(F32)
        offset_ref[:heads, :] = lax.dot_general(
            table_ref[...], one_hot, (((0,), (0,)), ((), ())),
            precision=lax.Precision.HIGHEST, preferred_element_type=F32,
        )

        @pl.loop(0, heads)
        def _(h):
            row = offset_ref[pl.ds(h, 1), :]
            for d in range(2 * blocks - 1):
                window = jnp.broadcast_to(row[:, 128 * d : 128 * d + 256], (128, 256))
                bias_ref[h, d] = pltpu.roll(window, 129, 1, stride=1, stride_axis=0)[:, :128].T

        wait(segs)
        seg_rows = [seg_rows_ref[i, 0:1, :].astype(F32) for i in range(blocks)]
        for kb in range(blocks):
            column = jnp.broadcast_to(seg_rows[kb], (128, 128)).T
            for qb in range(blocks):
                mask_ref[128 * kb : 128 * kb + 128, 128 * qb : 128 * qb + 128] = jnp.where(
                    column == seg_rows[qb], 0.0, MASKED
                )
        wait(loads)
        wait(tokens_in)
        start(cot_in)

        @pl.loop(0, blocks)
        def _(i):
            inputs = x_ref[block(i), :].astype(F32)
            branch_ref[block(i), :] = (inputs * inverse_rms(inputs) * gain_one_ref[...]).astype(LOW)

        q_t_ref, v_t_ref = d_att_t_ref, d_q_t_ref
        for tile in range(width // 256):
            cols = slice(256 * tile, 256 * tile + 256)
            q = dot(branch_ref[...], wq_ref[:, cols])
            q_t_ref[cols, :] = q.T.astype(LOW)
            k = dot(branch_ref[...], wk_ref[:, cols])
            k_t_ref[cols, :] = k.T.astype(LOW)
            v = dot(branch_ref[...], wv_ref[:, cols])
            v_t_ref[cols, :] = v.T.astype(LOW)
            for i in range(2):
                lanes = slice(128 * i, 128 * i + 128)
                q_ref[2 * tile + i] = q[:, lanes].astype(LOW)
                k_ref[2 * tile + i] = k[:, lanes].astype(LOW)
                v_ref[2 * tile + i] = v[:, lanes].astype(LOW)

        @pl.loop(0, pairs)
        def _(pair):
            slot = lax.rem(pair, 2)

            @pl.when(pair >= 2)
            def _():
                probs_copy(pair - 2, slot, True).wait()

            keys = k_ref[pair]
            for b in range(2):
                h = 2 * pair + b
                rows = pl.ds(pl.multiple_of(h * head_dim, head_dim), head_dim)
                q_t = zero_padded(q_t_ref[rows, :], b)
                v_t = v_t_ref[rows, :]
                for half in range(span // 256):
                    cols = slice(256 * half, 256 * half + 256)
                    bias = jnp.concatenate(
                        [
                            jnp.concatenate(
                                [bias_ref[h, kb - qb + blocks - 1] for qb in (2 * half, 2 * half + 1)], axis=1
                            )
                            for kb in range(blocks)
                        ],
                        axis=0,
                    )
                    scores = dot(keys, q_t[:, cols]) + bias + mask_ref[:, cols]
                    powers = jnp.exp(scores - jnp.max(scores, axis=0, keepdims=True))
                    probs = (powers * (1.0 / jnp.sum(powers, axis=0, keepdims=True))).astype(LOW)
                    probs_ref[slot, b, :, cols] = probs
                    attended_t_ref[rows, cols] = dot(v_t, probs).astype(LOW)
            probs_copy(pair, slot, True).start()

        attended = attended_t_ref[...].T
        for tile in range(width // 256):
            cols = slice(256 * tile, 256 * tile + 256)
            resid_ref[:, cols] = x_ref[:, cols].astype(F32) + dot(attended, wo_ref[:, cols])

        @pl.loop(0, blocks)
        def _(i):
            resid = resid_ref[block(i), :]
            branch_ref[block(i), :] = (resid * inverse_rms(resid) * gain_two_ref[...]).astype(LOW)
            acc_ref[block(i), :] = resid

        for pair in (pairs - 2, pairs - 1):
            probs_copy(pair, pair % 2, True).wait()

        @pl.loop(0, tiles)
        def _(g):
            for sub in range(2):
                wait(weight_loads(g, sub))
                gate = dot(branch_ref[...], wgu_ref[sub, :, :256])
                upper = dot(branch_ref[...], wgu_ref[sub, :, 256:])
                square = gate * gate
                curve = jnp.tanh(0.7978845608028654 * gate * (1.0 + 0.044715 * square))
                gelu = 0.5 * gate * (1.0 + curve)
                slope = 0.5 * (1.0 + curve) + 0.5 * gate * (1.0 - curve * curve) * (
                    0.7978845608028654 * (1.0 + 3 * 0.044715 * square)
                )
                activ = gelu * upper

                @pl.when(g > 0)
                def _():
                    wait(slope_copies(g - 1, sub, True))

                slope_up_ref[sub] = gelu.astype(LOW)
                slope_gate_ref[sub] = (upper * slope).astype(LOW)
                start(slope_copies(g, sub, True))
                activ_t_ref[2 * g + sub] = activ.T.astype(LOW)
                acc_ref[...] += dot(activ.astype(LOW), wd_ref[sub])
                start(weight_loads(lax.rem(g + 1, tiles), sub))

        mixed_ref[...] = acc_ref[...].astype(LOW)

    pl.run_scoped(
        forward,
        bias_ref=VMEM((heads, 2 * blocks - 1, 128, 128), F32),
        mask_ref=VMEM((span, span), F32),
    )
    start(mixed_back)
    for sub in range(2):
        wait(slope_copies(tiles - 1, sub, True))
        start(slope_copies(0, sub, False))
    wait(cot_in)
    probs_copy(0, 0, False).start()

    def backward(hidden_t_ref, d_att_ref, d_k_ref, d_v_ref):
        for s in range(GROUP):
            product = dot(activ_t_ref[s], cot_ref[...]).astype(LOW)
            for p in range(4):
                for i in range(width // 128):
                    ff_own[p, s % 2, s // 4, (s // 2) % 2, 64 * i : 64 * i + 64, :] = product[
                        64 * p : 64 * p + 64, 128 * i : 128 * i + 128
                    ]
        ff.stage0(0)
        ff.stage0(1)

        @pl.loop(0, blocks)
        def _(i):
            resid = resid_ref[block(i), :]
            hidden_t_ref[:, block(i)] = (resid * inverse_rms(resid) * gain_two_ref[...]).T.astype(LOW)

        ff.stage1(0)
        acc_ref[...] = jnp.zeros_like(acc_ref)

        @pl.loop(0, tiles)
        def _(g):
            job = 2 + g
            for sub in range(2):
                wait(weight_loads(g, sub))
                wait(slope_copies(g, sub, False))
                d_act = dot_back(cot_ref[...], wd_ref[sub])
                d_gate = (d_act * slope_gate_ref[sub].astype(F32)).astype(LOW)
                d_upper = (d_act * slope_up_ref[sub].astype(F32)).astype(LOW)
                for k, d_half in enumerate((d_gate, d_upper)):
                    product = dot(hidden_t_ref[...], d_half).astype(LOW)
                    for s in range(GROUP):
                        for i in range(2):
                            place = shard * (2 * sub + i)
                            ff_own[2 * job + k, s % 2, s // 4, (s // 2) % 2, place : place + shard, :] = product[
                                shard * s : shard * s + shard, 128 * i : 128 * i + 128
                            ]
                if sub:
                    ff.stage0(job)
                d_both = jnp.concatenate([d_gate, d_upper], axis=1)
                for tile in range(width // 256):
                    cols = slice(256 * tile, 256 * tile + 256)
                    acc_ref[:, cols] += dot_back(d_both, wgu_ref[sub, cols, :])

                @pl.when(g < tiles - 1)
                def _():
                    start(weight_loads(g + 1, sub))
                    start(slope_copies(g + 1, sub, False))

            ff.stage1(job - 1)

            @pl.when(g >= 1)
            def _():
                ff.stage2(g - 1)

        def norm_back(vector_ref, gain_ref, extra_ref, low_ref, row):
            total = jnp.zeros((1, width), F32)
            for i in range(blocks):
                rows = slice(128 * i, 128 * i + 128)
                vector = vector_ref[rows, :].astype(F32)
                scale = inverse_rms(vector)
                normed = vector * scale
                grad = acc_ref[rows, :]
                total = total + jnp.sum(grad * normed, axis=0, keepdims=True)
                inner = grad * gain_ref[...]
                result = extra_ref[rows, :].astype(F32) + scale * (
                    inner - normed * jnp.mean(inner * normed, -1, keepdims=True)
                )
                acc_ref[rows, :] = result
                low_ref[rows, :] = result.astype(LOW)
            small_own[0, row : row + 1, :] = total

        norm_back(resid_ref, gain_two_ref, cot_ref, branch_ref, 12)
        ff.stage1(FF_JOBS - 1)

        def share(sums, j, left_t, right):
            for k in range(2):
                half = slice(width // 2 * k, width // 2 * k + width // 2)
                product = dot(left_t, right[:, half]).astype(LOW)
                for s in range(GROUP):
                    for i in range(width // 256):
                        sums.own[2 * j + k, s % 2, s // 4, (s // 2) % 2, shard * i : shard * i + shard, :] = product[
                            shard * s : shard * s + shard, 128 * i : 128 * i + 128
                        ]
            sums.stage0(j)

        share(att, 0, attended_t_ref[...], branch_ref[...])
        for tile in range(width // 256):
            rows = slice(256 * tile, 256 * tile + 256)
            d_att = dot_back(branch_ref[...], wo_ref[rows, :])
            d_att_t_ref[rows, :] = d_att.T.astype(LOW)
            for i in range(2):
                d_att_ref[2 * tile + i] = d_att[:, 128 * i : 128 * i + 128].astype(LOW)
        att.stage1(0)
        left_half = lax.broadcasted_iota(jnp.int32, (span, 128), 1) < head_dim
        flip = (
            lax.broadcasted_iota(jnp.int32, (128, 128), 0) + lax.broadcasted_iota(jnp.int32, (128, 128), 1) == 127
        ).astype(F32)

        @pl.loop(0, pairs)
        def _(pair):
            slot = lax.rem(pair, 2)
            probs_copy(pair, slot, False).wait()

            @pl.when(pair < pairs - 1)
            def _():
                probs_copy(pair + 1, 1 - slot, False).start()

            values = v_ref[pair]
            d_att = d_att_ref[pair]
            queries = q_ref[pair]
            lanes = pl.ds(pl.multiple_of(pair * 128, 128), 128)
            d_values = jnp.zeros((span, 128), F32)
            d_keys = jnp.zeros((span, 128), F32)
            for b in range(2):
                h = 2 * pair + b
                rows = pl.ds(pl.multiple_of(h * head_dim, head_dim), head_dim)
                d_att_t = zero_padded(d_att_t_ref[rows, :], b)
                k_t = k_t_ref[rows, :]
                sides = []
                sums = [None] * (2 * blocks - 1)
                for half in range(span // 256):
                    cols = slice(256 * half, 256 * half + 256)
                    d_probs = dot(values, d_att_t[:, cols])
                    probs = probs_ref[slot, b, :, cols].astype(F32)
                    inner = jnp.sum(probs * d_probs, axis=0, keepdims=True)
                    d_scores = probs * (d_probs - inner)
                    for kb in range(blocks):
                        for i in range(2):
                            d = kb - (2 * half + i) + blocks - 1
                            part = d_scores[128 * kb : 128 * kb + 128, 128 * i : 128 * i + 128]
                            sums[d] = part if sums[d] is None else sums[d] + part
                    d_scores = d_scores.astype(LOW)
                    d_q_t_ref[rows, cols] = dot(k_t, d_scores).astype(LOW)
                    sides.append(d_scores)
                mine = left_half if b == 0 else jnp.logical_not(left_half)
                d_values = d_values + dot(probs_ref[slot, b], jnp.where(mine, d_att, jnp.zeros_like(d_att)))
                d_keys = d_keys + dot(
                    jnp.concatenate(sides, axis=1), jnp.where(mine, queries, jnp.zeros_like(queries))
                )
                totals = []
                for d in range(2 * blocks - 1):
                    flipped = jnp.dot(sums[d], flip, precision=lax.Precision.HIGHEST, preferred_element_type=F32)
                    wide = jnp.concatenate([flipped, jnp.zeros((128, 128), F32)], axis=1)
                    totals.append(jnp.sum(pltpu.roll(wide, 0, 1, stride=1, stride_axis=0), axis=0, keepdims=True))
                pieces = [totals[0][:, :128]]
                for d in range(1, 2 * blocks - 1):
                    pieces.append(totals[d - 1][:, 128:] + totals[d][:, :128])
                pieces.append(totals[-1][:, 128:])
                offset_ref[pl.ds(h, 1), :] = jnp.concatenate(pieces, axis=1)
            d_v_ref[:, lanes] = d_values.astype(LOW)
            d_k_ref[:, lanes] = d_keys.astype(LOW)

            @pl.when(pair < FF_JOBS - 3)
            def _():
                ff.stage2(pair + 3)

            ff.stage3(pair)

            @pl.when(pair >= 1)
            def _():
                ff.hop(pair - 1, 1)

            @pl.when(pair >= 2)
            def _():
                ff.hop(pair - 2, 2)

        @pl.loop(0, blocks)
        def _(i):
            inputs = x_ref[block(i), :].astype(F32)
            hidden_t_ref[:, block(i)] = (inputs * inverse_rms(inputs) * gain_one_ref[...]).T.astype(LOW)

        share(att, 1, hidden_t_ref[...], d_v_ref[...])
        share(att, 2, hidden_t_ref[...], d_k_ref[...])
        att.stage1(1)
        branch_ref[...] = d_q_t_ref[...].T
        share(att, 3, hidden_t_ref[...], branch_ref[...])
        att.stage1(2)
        att.stage2(0)
        for tile in range(width // 256):
            rows = slice(256 * tile, 256 * tile + 256)
            resid_ref[:, rows] = acc_ref[:, rows]
            acc_ref[:, rows] = (
                dot_back(branch_ref[...], wq_ref[rows, :])
                + dot_back(d_k_ref[...], wk_ref[rows, :])
                + dot_back(d_v_ref[...], wv_ref[rows, :])
            )
        att.stage1(3)
        norm_back(x_ref, gain_one_ref, resid_ref, branch_ref, 13)
        start(tokens_back)

    pl.run_scoped(
        backward,
        hidden_t_ref=VMEM((width, span), LOW),
        d_att_ref=VMEM((pairs, span, 128), LOW),
        d_k_ref=VMEM((span, width), LOW),
        d_v_ref=VMEM((span, width), LOW),
    )

    one_hot = (lax.broadcasted_iota(jnp.int32, (128, buckets_wide), 0) == bucket_ref[...]).astype(F32)
    small_own[0, :12, :128] = lax.dot_general(
        offset_ref[:12, :], one_hot, (((1,), (1,)), ((), ())),
        precision=lax.Precision.HIGHEST, preferred_element_type=F32,
    )
    small_peers = [at.core_peer, at.x_peer, at.y_peer]
    bit = 1
    while bit < n_seq:
        small_peers.append(at.z_pair(bit))
        bit *= 2

    def small_copy(i):
        return remote(small_own.at[i], small_got.at[i], small_sems, i, small_peers[i])

    small_copy(0).start()

    def small_step(i):
        small_copy(i).wait_recv()
        small_own[i + 1] = small_own[i] + small_got[i]
        if i + 1 < len(small_peers):
            small_copy(i + 1).start()

    att.stage3(0)
    att.stage2(1)
    ff.hop(FF_JOBS - 1, 1)
    ff.hop(FF_JOBS - 2, 2)
    small_step(0)
    att.stage2(2)
    att.stage3(1)
    att.hop(0, 1)
    ff.hop(FF_JOBS - 1, 2)
    small_step(1)
    att.stage2(3)
    att.stage3(2)
    att.hop(1, 1)
    att.hop(0, 2)
    small_step(2)
    att.stage3(3)
    att.hop(2, 1)
    att.hop(1, 2)
    small_step(3)

    @pl.loop(0, FF_JOBS)
    def _(j):
        ff.finish(j, ff_out, ff_out_sems)

    att.hop(3, 1)
    att.hop(2, 2)
    small_step(4)
    att.hop(3, 2)

    @pl.loop(0, ATT_JOBS)
    def _(j):
        att.finish(j, att_out, att_out_sems)

    small_out[...] = small_own[len(small_peers)]
    for sums, jobs, out, sems in ((ff, FF_JOBS, ff_out, ff_out_sems), (att, ATT_JOBS, att_out, att_out_sems)):

        @pl.loop(0, jobs)
        def _(j):
            sums.drain(j, out, sems)

    for i in range(len(small_peers)):
        small_copy(i).wait_send()
    wait(mixed_back)
    wait(tokens_back)


def layer(n_dp, n_seq, tokens, cot, seg, buckets, gain_one, gain_two, table, weights):
    width = tokens.shape[-1]
    span = tokens.shape[0] * tokens.shape[1]
    heads = table.shape[1]
    ff_width = weights[4].shape[1]
    ff_pieces, att_pieces = 2 * FF_JOBS, 2 * ATT_JOBS
    low = lambda *shape: VMEM(shape, LOW)
    dma = pltpu.SemaphoreType.DMA
    steps = 3 + (n_seq - 1).bit_length()

    def sums(pieces, rows):
        return [
            low(pieces, 2, 2, 2, rows, 128), low(pieces, 2, 2, rows, 128), low(pieces, 2, rows, 128),
            low(pieces, rows, 128), low(pieces, rows, 128), low(pieces, rows, 128),
            dma((5, 2, pieces)), dma((pieces,)),
        ]

    pairs = low(heads // 2, span, 128)
    whole = low(width, width)
    rows, turned = low(span, width), low(width, span)
    any_, vmem = pl.BlockSpec(memory_space=pl.ANY), pl.BlockSpec(memory_space=VMEM)
    result = lambda *shape: jax.ShapeDtypeStruct(shape, LOW)
    return pl.pallas_call(
        functools.partial(layer_kernel, n_dp, n_seq),
        out_shape=[
            result(n_seq, span // n_seq, width), result(n_seq, span // n_seq, width),
            result(ff_pieces, FF_ROWS, 128), result(att_pieces, ATT_ROWS, 128),
            jax.ShapeDtypeStruct((16, width), F32),
            result(heads, span, span), result(ff_width // 256, span, 256), result(ff_width // 256, span, 256),
        ],
        in_specs=[any_] * 2 + [vmem] * 5 + [any_] * 7,
        out_specs=[any_] * 4 + [vmem] + [any_] * 3,
        scratch_shapes=sums(ff_pieces, FF_ROWS)
        + sums(att_pieces, ATT_ROWS)
        + [VMEM((steps + 1, 16, width), F32), VMEM((steps, 16, width), F32), dma((2, steps))]
        + [
            rows, rows, VMEM((n_seq, 8, 128), jnp.int32), VMEM((n_seq, 8, 128), jnp.int32), rows,
            whole, whole, whole, whole, low(2, width, 512), low(2, 256, width),
            low(2, 2, span, span), low(2, span, 256), low(2, span, 256),
            low(ff_width // 256, 256, span), turned, pairs, pairs, pairs, turned, VMEM((span, width), F32),
            VMEM((span, width), F32), rows, turned, turned, VMEM((16, 1024), F32),
            dma((4,)), dma((3, 2)), dma((2, 2)), dma((2,)), dma((5, 2, n_seq)), dma((5,)),
        ],
        compiler_params=pltpu.CompilerParams(
            collective_id=0, has_side_effects=True, vmem_limit_bytes=VMEM_BYTES
        ),
        name="layer",
    )(tokens, cot, seg, buckets, gain_one, gain_two, table, *weights)


def outputs_kernel(
    n_dp, mixed_ref, tokens_ref, ff_ref, att_ref, small_ref,
    mixed_out, tokens_out, gn_one_out, gq_out, gk_out, gv_out, go_out, table_out, gn_two_out, gg_out, gu_out, gd_out,
):
    mixed_out[...] = mixed_ref[...]
    tokens_out[...] = tokens_ref[...].astype(F32)
    width = mixed_ref.shape[-1]
    shard = width // GROUP
    for j, out in enumerate((go_out, gv_out, gk_out, gq_out)):
        for k in range(2):
            for i in range(width // 256):
                col = width // 2 * k + 128 * i
                out[:, col : col + 128] = att_ref[2 * j + k, shard * i : shard * i + shard, :].astype(F32)
    for p in range(4):
        for i in range(width // 128):
            gd_out[64 * p : 64 * p + 64, 128 * i : 128 * i + 128] = ff_ref[p, 64 * i : 64 * i + 64, :].astype(F32)
    for g in range(4):
        for k, out in enumerate((gg_out, gu_out)):
            for i in range(4):
                col = 512 * g + 128 * i
                out[:, col : col + 128] = ff_ref[4 + 2 * g + k, shard * i : shard * i + shard, :].astype(F32)
    table_out[...] = small_ref[: table_out.shape[1], :128].T[: table_out.shape[0], :]
    mine = lax.axis_index("dp") // (n_dp // GROUP)
    for row, out in ((12, gn_two_out), (13, gn_one_out)):
        total = jnp.zeros((1, shard), F32)
        for s in range(GROUP):
            total = total + jnp.where(mine == s, small_ref[row : row + 1, shard * s : shard * s + shard], 0.0)
        out[...] = total


def outputs(n_dp, buckets, heads, mixed, tokens, ff, att, small):
    width = mixed.shape[-1]
    shard = width // GROUP
    full = lambda *shape: jax.ShapeDtypeStruct(shape, F32)
    return pl.pallas_call(
        functools.partial(outputs_kernel, n_dp),
        out_shape=[
            jax.ShapeDtypeStruct(mixed.shape, LOW), full(*tokens.shape), full(1, shard),
            full(shard, width), full(shard, width), full(shard, width), full(shard, width), full(buckets, heads),
            full(1, shard), full(shard, 2048), full(shard, 2048), full(256, width),
        ],
        compiler_params=pltpu.CompilerParams(vmem_limit_bytes=VMEM_BYTES),
        name="outputs",
    )(mixed, tokens, ff, att, small)


def solution(mesh):
    n_dp, n_seq = mesh.shape["dp"], mesh.shape["seq"]

    def on_device(
        tokens, segments, offset_buckets, norm_attn, w_query, w_key, w_value, w_output, bias_table,
        norm_ff, w_gate, w_up, w_down, cotangent,
    ):
        buckets = jnp.pad(offset_buckets, (0, 1)).reshape(1, -1)
        gain_one, gain_two = norm_attn.reshape(1, -1), norm_ff.reshape(1, -1)
        weights = (w_query, w_key, w_value, w_output, w_gate, w_up, w_down)
        sums = layer(
            n_dp, n_seq, tokens, cotangent, segments, buckets, gain_one, gain_two, bias_table, weights
        )[:5]
        results = list(outputs(n_dp, bias_table.shape[0], bias_table.shape[1], *sums))
        results[2], results[8] = results[2].reshape(-1), results[8].reshape(-1)
        rest = n_dp // GROUP
        if rest > 1:
            groups = [[i * rest + j for j in range(rest)] for i in range(GROUP)]
            for i in (2, 3, 4, 5, 6, 8, 9, 10, 11):
                results[i] = lax.psum_scatter(
                    results[i], "dp", scatter_dimension=0, axis_index_groups=groups, tiled=True
                )
            results[7] = lax.psum(results[7], "dp", axis_index_groups=groups)
        return tuple(results)

    rows, shares = P("dp", "seq", None), P("dp", None)
    return jax.shard_map(
        on_device,
        mesh=mesh,
        in_specs=(rows, P("dp", "seq")) + (P(),) * 11 + (rows,),
        out_specs=(rows, rows, P("dp"), shares, shares, shares, shares, P(), P("dp"), shares, shares, shares),
        check_vma=False,
    )
```

time: 248 us -> 168 us (0.68); the launches traced: 245 us -> 168 us
  Pallas kernels: 200 us -> 160 us
  blocking collectives: 35.2 us -> 0 us
  starting transfers between devices: 3.5 us -> 0 us
    pallas_call x2 -> x1, Pallas kernels: 196 us -> 156 us  [layer(): pl.pallas_call(functools.partial(layer_kernel, n_dp, n_seq), out_shape=[r...]
    all_to_all x2 -> x0, blocking collectives: 35.2 us -> none  [on_device(): lax.all_to_all(v, 'seq', split_axis=0, concat_axis=1, tiled=True)]
    all_to_all x1 -> x0, starting transfers between devices: 3.5 us -> none  [on_device(): lax.all_to_all(v, 'seq', split_axis=0, concat_axis=1, tiled=True)]
  transfers between devices with their start and end apart: 1 -> 0, of which waited for: 0 -> 0; matrix products, arithmetic and copies ran while one was open for 1% -> 0% of each run, Pallas kernels for 16% -> 0%
where the time goes in v2:
time: 168 us
  Pallas kernels  160 us (95%)
  local copies, waits for them, and re-layouts  6.58 us (4%)
    pallas_call x1, Pallas kernels, layer(): pl.pallas_call(functools.partial(layer_kernel, n_dp, n_seq), out_shape=[r...  156 us
    pallas_call x1, Pallas kernels, outputs(): pl.pallas_call(functools.partial(outputs_kernel, n_dp), out_shape=[jax.Sh...  4.6 us

profile of v2, /device:TPU:0, one launch (start us, length us, event | category | flops | bytes accessed | tf_op | source)
XLA Modules:
  0.0 167.5 jit_solution(5114656063683051508)
XLA Ops:
  0.6 1.3 reshape.40.gain_one_ref
  1.9 1.3 reshape.41.gain_two_ref
  3.2 1.3 pad.4
  4.5 1.4 copy.26.table_ref
  5.8 155.7 %layer.1 = (bf16[4,128,768]{2,1,0:T(8,128)(2,1)}, bf16[4,128,768]{2,1,0:T(8,128)(2,1)}, bf16[12,384,128]{2,1,0:T(8,128)(2,1)}, bf16[8,288,128]{2,1,0:T(8,128)(2,...) custom-call(bf16[4,128,768]{2,1,0:T(8,128)(2,1)} %tokens_hbm.1, ...), custom_call_target="tpu_custom_call" | custom-call | tf_op jit(solution)/shard_map/layer/pallas_call | solution.py:726
  161.5 4.6 %outputs.1 = (bf16[4,128,768]{2,1,0:T(8,128)(2,1)}, f32[4,128,768]{2,1,0:T(8,128)}, f32[1,96]{1,0:T(1,128)}, f32[96,768]{1,0:T(8,128)}, f32[96,768]{1,0:T(8,128)...) custom-call(bf16[4,128,768]{2,1,0:T(8,128)(2,1)} %get-tuple-element., ...), custom_call_target="tpu_custom_call" | custom-call | tf_op jit(solution)/shard_map/outputs/pallas_call | solution.py:788
  166.1 1.4 copy.27

commit v3 on v2

--- a/solution.py
+++ b/solution.py
@@ -206,18 +206,18 @@
     n_dp, n_seq,
     tokens_hbm, cot_hbm, seg_ref, bucket_ref, gain_one_ref, gain_two_ref, table_ref,
     wq_hbm, wk_hbm, wv_hbm, wo_hbm, wg_hbm, wu_hbm, wd_hbm,
-    mixed_out, tokens_out, ff_out, att_out, small_out, probs_hbm, slope_up_hbm, slope_gate_hbm,
+    mixed_out, tokens_out, ff_out, att_out, small_out, probs_hbm, slope_hbm,
     ff_own, ff_got0, ff_got1, ff_got2, ff_low, ff_high, ff_sems, ff_out_sems,
     att_own, att_got0, att_got1, att_got2, att_low, att_high, att_sems, att_out_sems,
-    small_own, small_got, small_sems,
+    small_own, small_got, small_rows, small_sems, small_row_sems,
     x_ref, cot_ref, seg_send_ref, seg_rows_ref, mixed_ref,
-    wq_ref, wk_ref, wv_ref, wo_ref, wgu_ref, wd_ref, probs_ref, slope_up_ref, slope_gate_ref,
-    activ_t_ref, attended_t_ref, q_ref, k_ref, v_ref, k_t_ref, resid_ref, acc_ref, branch_ref,
-    d_att_t_ref, d_q_t_ref, offset_ref,
-    load_sems, ff_load_sems, slope_sems, probs_sems, row_sems, own_sems,
+    wo_ref, wgu_ref, wd_ref, probs_ref, inverse_ref,
+    activ_t_ref, attended_t_ref, q_ref, k_ref, v_ref, k_t_ref, resid_ref, acc_ref, branch_ref, d_branch_ref,
+    d_att_t_ref, d_q_t_ref, offset_ref, diag_ref,
+    load_sems, ff_load_sems, probs_sems, row_sems, own_sems,
 ):
     span, width = x_ref.shape
-    buckets, heads = table_ref.shape
+    heads, buckets = table_ref.shape
     buckets_wide = bucket_ref.shape[1]
     head_dim = width // heads
     blocks = span // 128
@@ -225,30 +225,27 @@
     tiles = wg_hbm.shape[1] // 512
     shard = width // GROUP
     at = Place(n_dp, n_seq)
-
+    d_back_ref = cot_ref
+
+    wq_ref, wk_ref, wv_ref = wgu_ref.at[0, :, pl.ds(0, width)], wgu_ref.at[1, :, pl.ds(0, width)], wd_ref.at[pl.ds(0, width)]
     loads = [
         pltpu.make_async_copy(src, dst, load_sems.at[i])
-        for i, (src, dst) in enumerate([(wq_hbm, wq_ref), (wk_hbm, wk_ref), (wv_hbm, wv_ref), (wo_hbm, wo_ref)])
+        for i, (src, dst) in enumerate([(wq_hbm, wq_ref), (wk_hbm, wk_ref), (wv_hbm, wv_ref)])
     ]
-
-    def weight_loads(g, sub):
-        cols = pl.ds(pl.multiple_of(g * 512 + sub * 256, 256), 256)
+    output_load = pltpu.make_async_copy(wo_hbm, wo_ref, load_sems.at[3])
+
+    def weight_loads(g, slot):
+        cols = pl.ds(pl.multiple_of(g * 512, 512), 512)
         sides = [
-            (wd_hbm.at[cols, :], wd_ref.at[sub]),
-            (wg_hbm.at[:, cols], wgu_ref.at[sub, :, pl.ds(0, 256)]),
-            (wu_hbm.at[:, cols], wgu_ref.at[sub, :, pl.ds(256, 256)]),
+            (wd_hbm.at[cols, :], wd_ref.at[pl.ds(pl.multiple_of(slot * 512, 512), 512)]),
+            (wg_hbm.at[:, cols], wgu_ref.at[slot, :, pl.ds(0, 512)]),
+            (wu_hbm.at[:, cols], wgu_ref.at[slot, :, pl.ds(512, 512)]),
         ]
-        return [pltpu.make_async_copy(src, dst, ff_load_sems.at[i, sub]) for i, (src, dst) in enumerate(sides)]
-
-    def slope_copies(g, sub, store):
-        sides = [
-            (slope_up_hbm.at[2 * g + sub], slope_up_ref.at[sub]),
-            (slope_gate_hbm.at[2 * g + sub], slope_gate_ref.at[sub]),
-        ]
-        return [
-            pltpu.make_async_copy(*((dst, src) if store else (src, dst)), slope_sems.at[i, sub])
-            for i, (src, dst) in enumerate(sides)
-        ]
+        return [pltpu.make_async_copy(src, dst, ff_load_sems.at[i, slot]) for i, (src, dst) in enumerate(sides)]
+
+    def slope_copy(g, slot, store):
+        sides = (slope_hbm.at[g], probs_ref.at[slot])
+        return pltpu.make_async_copy(*(sides[::-1] if store else sides), probs_sems.at[slot])
 
     def probs_copy(pair, slot, store):
         sides = (probs_hbm.at[pl.ds(2 * pair, 2)], probs_ref.at[slot])
@@ -263,6 +260,7 @@
             copy.wait()
 
     start(loads)
+    output_load.start()
     for i in range(n_seq):
         seg_send_ref[i] = jnp.broadcast_to(seg_ref[i : i + 1, :], (8, 128))
 
@@ -298,16 +296,13 @@
     tokens_in = exchange(1, lambda z: tokens_hbm.at[z], lambda z: x_ref.at[block(z), :])
     cot_in = exchange(2, lambda z: cot_hbm.at[z], lambda z: cot_ref.at[block(z), :])
     mixed_back = exchange(3, lambda z: mixed_ref.at[block(z), :], lambda z: mixed_out.at[z])
-    tokens_back = exchange(4, lambda z: branch_ref.at[block(z), :], lambda z: tokens_out.at[z])
+    tokens_back = exchange(4, lambda z: d_back_ref.at[block(z), :], lambda z: tokens_out.at[z])
     start(segs)
     start(tokens_in)
-    for sub in range(2):
-        start(weight_loads(0, sub))
-
-    def forward(bias_ref, mask_ref):
+    def forward(bias_ref, key_seg_ref, query_seg_ref):
         one_hot = (lax.broadcasted_iota(jnp.int32, (buckets, buckets_wide), 0) == bucket_ref[...]).astype(F32)
         offset_ref[:heads, :] = lax.dot_general(
-            table_ref[...], one_hot, (((0,), (0,)), ((), ())),
+            table_ref[...], one_hot, (((1,), (0,)), ((), ())),
             precision=lax.Precision.HIGHEST, preferred_element_type=F32,
         )
 
@@ -320,12 +315,12 @@
 
         wait(segs)
         seg_rows = [seg_rows_ref[i, 0:1, :].astype(F32) for i in range(blocks)]
-        for kb in range(blocks):
-            column = jnp.broadcast_to(seg_rows[kb], (128, 128)).T
-            for qb in range(blocks):
-                mask_ref[128 * kb : 128 * kb + 128, 128 * qb : 128 * qb + 128] = jnp.where(
-                    column == seg_rows[qb], 0.0, MASKED
-                )
+        for i in range(blocks):
+            column = jnp.broadcast_to(seg_rows[i], (128, 128)).T
+            across = lax.broadcasted_iota(jnp.int32, (128, 128), 1).astype(F32)
+            along = lax.broadcasted_iota(jnp.int32, (128, 128), 0).astype(F32)
+            key_seg_ref[128 * i : 128 * i + 128, :] = jnp.where(column == across, 1.0, 0.0).astype(LOW)
+            query_seg_ref[:, 128 * i : 128 * i + 128] = jnp.where(seg_rows[i] == along, 0.0, MASKED).astype(LOW)
         wait(loads)
         wait(tokens_in)
         start(cot_in)
@@ -350,6 +345,50 @@
                 k_ref[2 * tile + i] = k[:, lanes].astype(LOW)
                 v_ref[2 * tile + i] = v[:, lanes].astype(LOW)
 
+        start(weight_loads(0, 0))
+        score_refs = (acc_ref, resid_ref)
+
+        def put_scores(pair, b):
+            rows = pl.ds(pl.multiple_of((2 * pair + b) * head_dim, head_dim), head_dim)
+            keys = jnp.concatenate([k_ref[pair], key_seg_ref[...]], axis=1)
+            q_t = jnp.concatenate([zero_padded(q_t_ref[rows, :], b), query_seg_ref[...]], axis=0)
+
+            def half_of(half):
+                cols = slice(256 * half, 256 * half + 256)
+                score_refs[b][:, cols] = dot(keys, q_t[:, cols])
+
+            return half_of
+
+        def put_attended(pair, b, slot):
+            h = 2 * pair + b
+            rows = pl.ds(pl.multiple_of(h * head_dim, head_dim), head_dim)
+            v_t = v_t_ref[rows, :]
+
+            def half_of(half):
+                cols = slice(256 * half, 256 * half + 256)
+                bias = jnp.concatenate(
+                    [
+                        jnp.concatenate(
+                            [bias_ref[h, kb - qb + blocks - 1] for qb in (2 * half, 2 * half + 1)], axis=1
+                        )
+                        for kb in range(blocks)
+                    ],
+                    axis=0,
+                )
+                scores = score_refs[b][:, cols] + bias
+                powers = jnp.exp(scores - jnp.max(scores, axis=0, keepdims=True))
+                inverse = 1.0 / jnp.sum(powers, axis=0, keepdims=True)
+                probs = powers.astype(LOW)
+                probs_ref[slot, b, :, cols] = probs
+                attended_t_ref[rows, cols] = (dot(v_t, probs) * inverse).astype(LOW)
+                inverse_ref[pl.ds(h, 1), cols] = inverse
+
+            return half_of
+
+        first = put_scores(0, 0)
+        for half in range(2):
+            first(half)
+
         @pl.loop(0, pairs)
         def _(pair):
             slot = lax.rem(pair, 2)
@@ -358,30 +397,15 @@
             def _():
                 probs_copy(pair - 2, slot, True).wait()
 
-            keys = k_ref[pair]
             for b in range(2):
-                h = 2 * pair + b
-                rows = pl.ds(pl.multiple_of(h * head_dim, head_dim), head_dim)
-                q_t = zero_padded(q_t_ref[rows, :], b)
-                v_t = v_t_ref[rows, :]
-                for half in range(span // 256):
-                    cols = slice(256 * half, 256 * half + 256)
-                    bias = jnp.concatenate(
-                        [
-                            jnp.concatenate(
-                                [bias_ref[h, kb - qb + blocks - 1] for qb in (2 * half, 2 * half + 1)], axis=1
-                            )
-                            for kb in range(blocks)
-                        ],
-                        axis=0,
-                    )
-                    scores = dot(keys, q_t[:, cols]) + bias + mask_ref[:, cols]
-                    powers = jnp.exp(scores - jnp.max(scores, axis=0, keepdims=True))
-                    probs = (powers * (1.0 / jnp.sum(powers, axis=0, keepdims=True))).astype(LOW)
-                    probs_ref[slot, b, :, cols] = probs
-                    attended_t_ref[rows, cols] = dot(v_t, probs).astype(LOW)
+                ahead = put_scores(pair, 1) if b == 0 else put_scores(jnp.minimum(pair + 1, pairs - 1), 0)
+                now = put_attended(pair, b, slot)
+                for half in range(2):
+                    ahead(half)
+                    now(half)
             probs_copy(pair, slot, True).start()
 
+        output_load.wait()
         attended = attended_t_ref[...].T
         for tile in range(width // 256):
             cols = slice(256 * tile, 256 * tile + 256)
@@ -398,10 +422,19 @@
 
         @pl.loop(0, tiles)
         def _(g):
+            slot = lax.rem(g, 2)
+
+            @pl.when(g >= 2)
+            def _():
+                slope_copy(g - 2, slot, True).wait()
+
+            wait(weight_loads(g, slot))
+            start(weight_loads(lax.rem(g + 1, tiles), 1 - slot))
+            gates = [dot(branch_ref[...], wgu_ref[slot, :, 256 * i : 256 * i + 256]) for i in range(4)]
+            activs = []
             for sub in range(2):
-                wait(weight_loads(g, sub))
-                gate = dot(branch_ref[...], wgu_ref[sub, :, :256])
-                upper = dot(branch_ref[...], wgu_ref[sub, :, 256:])
+                gate, upper = gates[sub], gates[2 + sub]
+                lanes = slice(256 * sub, 256 * sub + 256)
                 square = gate * gate
                 curve = jnp.tanh(0.7978845608028654 * gate * (1.0 + 0.044715 * square))
                 gelu = 0.5 * gate * (1.0 + curve)
@@ -409,33 +442,29 @@
                     0.7978845608028654 * (1.0 + 3 * 0.044715 * square)
                 )
                 activ = gelu * upper
-
-                @pl.when(g > 0)
-                def _():
-                    wait(slope_copies(g - 1, sub, True))
-
-                slope_up_ref[sub] = gelu.astype(LOW)
-                slope_gate_ref[sub] = (upper * slope).astype(LOW)
-                start(slope_copies(g, sub, True))
+                probs_ref[slot, 0, :, lanes] = gelu.astype(LOW)
+                probs_ref[slot, 1, :, lanes] = (upper * slope).astype(LOW)
                 activ_t_ref[2 * g + sub] = activ.T.astype(LOW)
-                acc_ref[...] += dot(activ.astype(LOW), wd_ref[sub])
-                start(weight_loads(lax.rem(g + 1, tiles), sub))
+                activs.append(activ.astype(LOW))
+            down = wd_ref[pl.ds(pl.multiple_of(slot * 512, 512), 512)]
+            acc_ref[...] += dot(jnp.concatenate(activs, axis=1), down)
+            slope_copy(g, slot, True).start()
 
         mixed_ref[...] = acc_ref[...].astype(LOW)
 
     pl.run_scoped(
         forward,
         bias_ref=VMEM((heads, 2 * blocks - 1, 128, 128), F32),
-        mask_ref=VMEM((span, span), F32),
+        key_seg_ref=VMEM((span, 128), LOW),
+        query_seg_ref=VMEM((128, span), LOW),
     )
     start(mixed_back)
-    for sub in range(2):
-        wait(slope_copies(tiles - 1, sub, True))
-        start(slope_copies(0, sub, False))
+    for g in (tiles - 2, tiles - 1):
+        slope_copy(g, g % 2, True).wait()
+    slope_copy(0, 0, False).start()
     wait(cot_in)
-    probs_copy(0, 0, False).start()
-
-    def backward(hidden_t_ref, d_att_ref, d_k_ref, d_v_ref):
+
+    def backward(hidden_t_ref, d_att_ref, d_k_ref, d_v_ref, d_probs_ref):
         for s in range(GROUP):
             product = dot(activ_t_ref[s], cot_ref[...]).astype(LOW)
             for p in range(4):
@@ -446,48 +475,73 @@
         ff.stage0(0)
         ff.stage0(1)
 
+        acc_ref[...] = jnp.zeros_like(acc_ref)
+
+        def d_slot(g, k, lanes, half):
+            n = 2 * lanes + half
+            return att_own.at[2 * g + k, n // 4, (n // 2) % 2, n % 2, pl.ds(0, 256), :]
+
+        @pl.loop(0, tiles)
+        def _(g):
+            slot = lax.rem(g, 2)
+            wait(weight_loads(g, slot))
+            slope_copy(g, slot, False).wait()
+
+            @pl.when(g < tiles - 1)
+            def _():
+                start(weight_loads(g + 1, 1 - slot))
+                slope_copy(g + 1, 1 - slot, False).start()
+
+            d_sides = [[], []]
+            for sub in range(2):
+                lanes = slice(256 * sub, 256 * sub + 256)
+                down = wd_ref[pl.ds(pl.multiple_of(slot * 512 + 256 * sub, 256), 256)]
+                d_act = dot_back(cot_ref[...], down)
+                for k in range(2):
+                    d_side = (d_act * probs_ref[slot, 1 - k, :, lanes].astype(F32)).astype(LOW)
+                    d_sides[k].append(d_side)
+                    for i in range(2):
+                        for half in range(2):
+                            d_slot(g, k, 2 * sub + i, half)[...] = d_side[
+                                256 * half : 256 * half + 256, 128 * i : 128 * i + 128
+                            ]
+            d_both = jnp.concatenate(d_sides[0] + d_sides[1], axis=1)
+            for tile in range(width // 256):
+                cols = slice(256 * tile, 256 * tile + 256)
+                acc_ref[:, cols] += dot_back(d_both, wgu_ref[slot, cols, :])
+
+            @pl.when(g <= 1)
+            def _():
+                ff.stage1(g)
+
+        start(loads)
+        probs_copy(0, 0, False).start()
+
         @pl.loop(0, blocks)
         def _(i):
             resid = resid_ref[block(i), :]
             hidden_t_ref[:, block(i)] = (resid * inverse_rms(resid) * gain_two_ref[...]).T.astype(LOW)
 
-        ff.stage1(0)
-        acc_ref[...] = jnp.zeros_like(acc_ref)
-
-        @pl.loop(0, tiles)
-        def _(g):
-            job = 2 + g
-            for sub in range(2):
-                wait(weight_loads(g, sub))
-                wait(slope_copies(g, sub, False))
-                d_act = dot_back(cot_ref[...], wd_ref[sub])
-                d_gate = (d_act * slope_gate_ref[sub].astype(F32)).astype(LOW)
-                d_upper = (d_act * slope_up_ref[sub].astype(F32)).astype(LOW)
-                for k, d_half in enumerate((d_gate, d_upper)):
-                    product = dot(hidden_t_ref[...], d_half).astype(LOW)
+        ff.stage2(0)
+
+        def products(g):
+            for k in range(2):
+                for sub in range(2):
+                    right = jnp.concatenate(
+                        [
+                            jnp.concatenate([d_slot(g, k, 2 * sub + i, half)[...] for half in range(2)], axis=0)
+                            for i in range(2)
+                        ],
+                        axis=1,
+                    )
+                    product = dot(hidden_t_ref[...], right).astype(LOW)
                     for s in range(GROUP):
                         for i in range(2):
                             place = shard * (2 * sub + i)
-                            ff_own[2 * job + k, s % 2, s // 4, (s // 2) % 2, place : place + shard, :] = product[
+                            ff_own[4 + 2 * g + k, s % 2, s // 4, (s // 2) % 2, place : place + shard, :] = product[
                                 shard * s : shard * s + shard, 128 * i : 128 * i + 128
                             ]
-                if sub:
-                    ff.stage0(job)
-                d_both = jnp.concatenate([d_gate, d_upper], axis=1)
-                for tile in range(width // 256):
-                    cols = slice(256 * tile, 256 * tile + 256)
-                    acc_ref[:, cols] += dot_back(d_both, wgu_ref[sub, cols, :])
-
-                @pl.when(g < tiles - 1)
-                def _():
-                    start(weight_loads(g + 1, sub))
-                    start(slope_copies(g + 1, sub, False))
-
-            ff.stage1(job - 1)
-
-            @pl.when(g >= 1)
-            def _():
-                ff.stage2(g - 1)
+            ff.stage0(2 + g)
 
         def norm_back(vector_ref, gain_ref, extra_ref, low_ref, row):
             total = jnp.zeros((1, width), F32)
@@ -504,10 +558,11 @@
                 )
                 acc_ref[rows, :] = result
                 low_ref[rows, :] = result.astype(LOW)
-            small_own[0, row : row + 1, :] = total
-
-        norm_back(resid_ref, gain_two_ref, cot_ref, branch_ref, 12)
-        ff.stage1(FF_JOBS - 1)
+            for i in range(width // 128):
+                small_own[0, row + i : row + i + 1, :] = total[:, 128 * i : 128 * i + 128]
+
+        norm_back(resid_ref, gain_two_ref, cot_ref, d_branch_ref, 12)
+        products(0)
 
         def share(sums, j, left_t, right):
             for k in range(2):
@@ -520,18 +575,67 @@
                         ]
             sums.stage0(j)
 
-        share(att, 0, attended_t_ref[...], branch_ref[...])
         for tile in range(width // 256):
             rows = slice(256 * tile, 256 * tile + 256)
-            d_att = dot_back(branch_ref[...], wo_ref[rows, :])
-            d_att_t_ref[rows, :] = d_att.T.astype(LOW)
+            d_att_t = dot_back(d_branch_ref[...], wo_ref[rows, :]).T
+            for i in range(256 // head_dim):
+                h = 256 // head_dim * tile + i
+                d_att_t_ref[head_dim * h : head_dim * (h + 1), :] = (
+                    d_att_t[head_dim * i : head_dim * (i + 1), :] * inverse_ref[h : h + 1, :]
+                ).astype(LOW)
             for i in range(2):
-                d_att_ref[2 * tile + i] = d_att[:, 128 * i : 128 * i + 128].astype(LOW)
-        att.stage1(0)
+                d_att_ref[2 * tile + i] = d_att_t_ref[256 * tile + 128 * i : 256 * tile + 128 * i + 128, :].T
         left_half = lax.broadcasted_iota(jnp.int32, (span, 128), 1) < head_dim
-        flip = (
-            lax.broadcasted_iota(jnp.int32, (128, 128), 0) + lax.broadcasted_iota(jnp.int32, (128, 128), 1) == 127
-        ).astype(F32)
+        d_probs_refs = (resid_ref, d_probs_ref)
+
+        def put_d_probs(pair, b):
+            rows = pl.ds(pl.multiple_of((2 * pair + b) * head_dim, head_dim), head_dim)
+            values = v_ref[pair]
+            d_att_t = zero_padded(d_att_t_ref[rows, :], b)
+
+            def half_of(half):
+                cols = slice(256 * half, 256 * half + 256)
+                d_probs_refs[b][:, cols] = dot(values, d_att_t[:, cols])
+
+            return half_of
+
+        across = lax.broadcasted_iota(jnp.int32, (8, 128), 1)
+
+        def put_d_scores(pair, b, slot):
+            h = 2 * pair + b
+            rows = pl.ds(pl.multiple_of(h * head_dim, head_dim), head_dim)
+            k_t = k_t_ref[rows, :]
+            sums = [None] * (2 * blocks - 1)
+
+            def half_of(half):
+                cols = slice(256 * half, 256 * half + 256)
+                d_probs = d_probs_refs[b][:, cols]
+                probs = probs_ref[slot, b, :, cols].astype(F32)
+                inner = jnp.sum(probs * d_probs, axis=0, keepdims=True) * inverse_ref[pl.ds(h, 1), cols]
+                d_scores = probs * (d_probs - inner)
+                for kb in range(blocks):
+                    for i in range(2):
+                        d = kb - (2 * half + i) + blocks - 1
+                        part = d_scores[128 * kb : 128 * kb + 128, 128 * i : 128 * i + 128]
+                        sums[d] = part if sums[d] is None else sums[d] + part
+                d_scores = d_scores.astype(LOW)
+                for i in range(2):
+                    activ_t_ref[2 * b + i, :, cols] = d_scores[256 * i : 256 * i + 256, :]
+                d_q_t_ref[rows, cols] = dot(k_t, d_scores).astype(LOW)
+                if half == 1:
+                    for d in range(2 * blocks - 1):
+                        every, low_lanes = sums[d][:8, :], sums[d][:8, :]
+                        for a in range(1, 16):
+                            rolled = pltpu.roll(sums[d][8 * a : 8 * a + 8, :], 128 - 8 * a, 1)
+                            every = every + rolled
+                            low_lanes = low_lanes + jnp.where(across < 128 - 8 * a, rolled, 0.0)
+                        diag_ref[h, d] = jnp.concatenate([low_lanes, every - low_lanes], axis=1)
+
+            return half_of
+
+        first = put_d_probs(0, 0)
+        for half in range(2):
+            first(half)
 
         @pl.loop(0, pairs)
         def _(pair):
@@ -542,88 +646,84 @@
             def _():
                 probs_copy(pair + 1, 1 - slot, False).start()
 
-            values = v_ref[pair]
-            d_att = d_att_ref[pair]
-            queries = q_ref[pair]
+            for b in range(2):
+                ahead = put_d_probs(pair, 1) if b == 0 else put_d_probs(jnp.minimum(pair + 1, pairs - 1), 0)
+                now = put_d_scores(pair, b, slot)
+                for half in range(2):
+                    ahead(half)
+                    now(half)
             lanes = pl.ds(pl.multiple_of(pair * 128, 128), 128)
-            d_values = jnp.zeros((span, 128), F32)
-            d_keys = jnp.zeros((span, 128), F32)
-            for b in range(2):
-                h = 2 * pair + b
-                rows = pl.ds(pl.multiple_of(h * head_dim, head_dim), head_dim)
-                d_att_t = zero_padded(d_att_t_ref[rows, :], b)
-                k_t = k_t_ref[rows, :]
-                sides = []
-                sums = [None] * (2 * blocks - 1)
-                for half in range(span // 256):
-                    cols = slice(256 * half, 256 * half + 256)
-                    d_probs = dot(values, d_att_t[:, cols])
-                    probs = probs_ref[slot, b, :, cols].astype(F32)
-                    inner = jnp.sum(probs * d_probs, axis=0, keepdims=True)
-                    d_scores = probs * (d_probs - inner)
-                    for kb in range(blocks):
-                        for i in range(2):
-                            d = kb - (2 * half + i) + blocks - 1
-                            part = d_scores[128 * kb : 128 * kb + 128, 128 * i : 128 * i + 128]
-                            sums[d] = part if sums[d] is None else sums[d] + part
-                    d_scores = d_scores.astype(LOW)
-                    d_q_t_ref[rows, cols] = dot(k_t, d_scores).astype(LOW)
-                    sides.append(d_scores)
-                mine = left_half if b == 0 else jnp.logical_not(left_half)
-                d_values = d_values + dot(probs_ref[slot, b], jnp.where(mine, d_att, jnp.zeros_like(d_att)))
-                d_keys = d_keys + dot(
-                    jnp.concatenate(sides, axis=1), jnp.where(mine, queries, jnp.zeros_like(queries))
-                )
-                totals = []
-                for d in range(2 * blocks - 1):
-                    flipped = jnp.dot(sums[d], flip, precision=lax.Precision.HIGHEST, preferred_element_type=F32)
-                    wide = jnp.concatenate([flipped, jnp.zeros((128, 128), F32)], axis=1)
-                    totals.append(jnp.sum(pltpu.roll(wide, 0, 1, stride=1, stride_axis=0), axis=0, keepdims=True))
-                pieces = [totals[0][:, :128]]
-                for d in range(1, 2 * blocks - 1):
-                    pieces.append(totals[d - 1][:, 128:] + totals[d][:, :128])
-                pieces.append(totals[-1][:, 128:])
-                offset_ref[pl.ds(h, 1), :] = jnp.concatenate(pieces, axis=1)
-            d_v_ref[:, lanes] = d_values.astype(LOW)
-            d_k_ref[:, lanes] = d_keys.astype(LOW)
-
-            @pl.when(pair < FF_JOBS - 3)
-            def _():
-                ff.stage2(pair + 3)
-
-            ff.stage3(pair)
-
-            @pl.when(pair >= 1)
-            def _():
-                ff.hop(pair - 1, 1)
-
-            @pl.when(pair >= 2)
-            def _():
-                ff.hop(pair - 2, 2)
+            d_att, queries = d_att_ref[pair], q_ref[pair]
+            blank = jnp.zeros_like(d_att)
+            d_scores = [activ_t_ref[2 * b : 2 * b + 2].reshape(span, span) for b in range(2)]
+            d_v_ref[:, lanes] = (
+                dot(probs_ref[slot, 0], jnp.where(left_half, d_att, blank))
+                + dot(probs_ref[slot, 1], jnp.where(left_half, blank, d_att))
+            ).astype(LOW)
+            d_k_ref[:, lanes] = (
+                dot(d_scores[0], jnp.where(left_half, queries, blank))
+                + dot(d_scores[1], jnp.where(left_half, blank, queries))
+            ).astype(LOW)
+            @pl.when(lax.rem(pair, 2) == 1)
+            def _():
+                products((pair + 1) // 2)
+
+            @pl.when(pair == 0)
+            def _():
+                ff.stage1(2)
+                ff.stage2(1)
+
+            @pl.when(pair == 1)
+            def _():
+                ff.stage3(0)
+
+            @pl.when(pair == 2)
+            def _():
+                ff.stage1(3)
+
+            @pl.when(pair == 3)
+            def _():
+                ff.stage2(2)
+                ff.stage3(1)
+
+            @pl.when(pair == 4)
+            def _():
+                ff.stage1(4)
+                ff.hop(0, 1)
+
+            @pl.when(pair == 5)
+            def _():
+                ff.stage2(3)
+
+        branch_ref[...] = d_q_t_ref[...].T
+        wait(loads)
+        for tile in range(width // 256):
+            rows = slice(256 * tile, 256 * tile + 256)
+            resid_ref[:, rows] = acc_ref[:, rows]
+            acc_ref[:, rows] = (
+                dot_back(branch_ref[...], wgu_ref[0, rows, :width])
+                + dot_back(d_k_ref[...], wgu_ref[1, rows, :width])
+                + dot_back(d_v_ref[...], wd_ref[rows, :])
+            )
+        ff.stage1(5)
+        ff.stage3(2)
+        norm_back(x_ref, gain_one_ref, resid_ref, d_back_ref, 18)
+        ff.hop(1, 1)
+        ff.hop(0, 2)
+        start(tokens_back)
+        share(att, 0, attended_t_ref[...], d_branch_ref[...])
 
         @pl.loop(0, blocks)
         def _(i):
             inputs = x_ref[block(i), :].astype(F32)
             hidden_t_ref[:, block(i)] = (inputs * inverse_rms(inputs) * gain_one_ref[...]).T.astype(LOW)
 
+        ff.stage2(4)
+        att.stage1(0)
         share(att, 1, hidden_t_ref[...], d_v_ref[...])
+        ff.stage3(3)
         share(att, 2, hidden_t_ref[...], d_k_ref[...])
-        att.stage1(1)
-        branch_ref[...] = d_q_t_ref[...].T
         share(att, 3, hidden_t_ref[...], branch_ref[...])
-        att.stage1(2)
-        att.stage2(0)
-        for tile in range(width // 256):
-            rows = slice(256 * tile, 256 * tile + 256)
-            resid_ref[:, rows] = acc_ref[:, rows]
-            acc_ref[:, rows] = (
-                dot_back(branch_ref[...], wq_ref[rows, :])
-                + dot_back(d_k_ref[...], wk_ref[rows, :])
-                + dot_back(d_v_ref[...], wv_ref[rows, :])
-            )
-        att.stage1(3)
-        norm_back(x_ref, gain_one_ref, resid_ref, branch_ref, 13)
-        start(tokens_back)
 
     pl.run_scoped(
         backward,
@@ -631,72 +731,115 @@
         d_att_ref=VMEM((pairs, span, 128), LOW),
         d_k_ref=VMEM((span, width), LOW),
         d_v_ref=VMEM((span, width), LOW),
+        d_probs_ref=VMEM((span, span), F32),
     )
 
+    ff.hop(2, 1)
+    ff.hop(1, 2)
+    ff.stage2(5)
+    att.stage1(1)
+
+    flip = (
+        lax.broadcasted_iota(jnp.int32, (256, 256), 0) + lax.broadcasted_iota(jnp.int32, (256, 256), 1) == 255
+    ).astype(F32)
+
+    @pl.loop(0, heads)
+    def _(h):
+        tiles_ = diag_ref[h].reshape(8 * (2 * blocks - 1), 256)
+        flipped = jnp.dot(tiles_, flip, precision=lax.Precision.HIGHEST, preferred_element_type=F32)
+        totals = [
+            jnp.sum(pltpu.roll(flipped[8 * d : 8 * d + 8, :], 0, 1, stride=1, stride_axis=0), axis=0, keepdims=True)
+            for d in range(2 * blocks - 1)
+        ]
+        pieces = [totals[0][:, 128:]]
+        for d in range(1, 2 * blocks - 1):
+            pieces.append(totals[d - 1][:, :128] + totals[d][:, 128:])
+        pieces.append(totals[-1][:, :128])
+        offset_ref[pl.ds(h, 1), :] = jnp.concatenate(pieces, axis=1)
+
     one_hot = (lax.broadcasted_iota(jnp.int32, (128, buckets_wide), 0) == bucket_ref[...]).astype(F32)
-    small_own[0, :12, :128] = lax.dot_general(
+    small_own[0, :12, :] = lax.dot_general(
         offset_ref[:12, :], one_hot, (((1,), (1,)), ((), ())),
         precision=lax.Precision.HIGHEST, preferred_element_type=F32,
     )
     small_peers = [at.core_peer, at.x_peer, at.y_peer]
-    bit = 1
-    while bit < n_seq:
-        small_peers.append(at.z_pair(bit))
-        bit *= 2
+    steps = len(small_peers)
 
     def small_copy(i):
         return remote(small_own.at[i], small_got.at[i], small_sems, i, small_peers[i])
 
-    small_copy(0).start()
+    def small_row(i):
+        return pltpu.make_async_remote_copy(
+            src_ref=small_own.at[steps], dst_ref=small_rows.at[at.z],
+            send_sem=small_row_sems.at[0, i], recv_sem=small_row_sems.at[1, i],
+            device_id=at.z_peer(lax.rem(at.z + i, n_seq)), device_id_type=MESH,
+        )
 
     def small_step(i):
         small_copy(i).wait_recv()
         small_own[i + 1] = small_own[i] + small_got[i]
-        if i + 1 < len(small_peers):
+        if i + 1 < steps:
             small_copy(i + 1).start()
 
+    small_copy(0).start()
+    ff.stage3(4)
+    att.stage2(0)
+    att.stage1(2)
+    small_step(0)
+    ff.stage3(5)
+    att.stage2(1)
+    att.stage1(3)
     att.stage3(0)
-    att.stage2(1)
-    ff.hop(FF_JOBS - 1, 1)
-    ff.hop(FF_JOBS - 2, 2)
-    small_step(0)
+    ff.hop(3, 1)
     att.stage2(2)
+    small_step(1)
     att.stage3(1)
+    ff.hop(2, 2)
+    ff.hop(4, 1)
+    att.stage2(3)
+    small_step(2)
+    small_rows[at.z] = small_own[steps]
+    att.stage3(2)
+    ff.hop(3, 2)
+    ff.hop(5, 1)
+    att.stage3(3)
+    for i in range(1, n_seq):
+        small_row(i).start()
+    ff.hop(4, 2)
     att.hop(0, 1)
-    ff.hop(FF_JOBS - 1, 2)
-    small_step(1)
-    att.stage2(3)
-    att.stage3(2)
+    ff.hop(5, 2)
     att.hop(1, 1)
     att.hop(0, 2)
-    small_step(2)
-    att.stage3(3)
     att.hop(2, 1)
     att.hop(1, 2)
-    small_step(3)
+    att.hop(3, 1)
+    att.hop(2, 2)
+    att.hop(3, 2)
 
     @pl.loop(0, FF_JOBS)
     def _(j):
         ff.finish(j, ff_out, ff_out_sems)
 
-    att.hop(3, 1)
-    att.hop(2, 2)
-    small_step(4)
-    att.hop(3, 2)
-
     @pl.loop(0, ATT_JOBS)
     def _(j):
         att.finish(j, att_out, att_out_sems)
 
-    small_out[...] = small_own[len(small_peers)]
+    for i in range(1, n_seq):
+        small_row(i).wait_recv()
+    total = small_rows[0]
+    for i in range(1, n_seq):
+        total = total + small_rows[i]
+    small_out[...] = total
     for sums, jobs, out, sems in ((ff, FF_JOBS, ff_out, ff_out_sems), (att, ATT_JOBS, att_out, att_out_sems)):
 
         @pl.loop(0, jobs)
         def _(j):
             sums.drain(j, out, sems)
 
-    for i in range(len(small_peers)):
+    for i in range(steps):
         small_copy(i).wait_send()
+    for i in range(1, n_seq):
+        small_row(i).wait_send()
     wait(mixed_back)
     wait(tokens_back)
 
@@ -704,12 +847,12 @@
 def layer(n_dp, n_seq, tokens, cot, seg, buckets, gain_one, gain_two, table, weights):
     width = tokens.shape[-1]
     span = tokens.shape[0] * tokens.shape[1]
-    heads = table.shape[1]
+    heads = table.shape[0]
     ff_width = weights[4].shape[1]
     ff_pieces, att_pieces = 2 * FF_JOBS, 2 * ATT_JOBS
     low = lambda *shape: VMEM(shape, LOW)
     dma = pltpu.SemaphoreType.DMA
-    steps = 3 + (n_seq - 1).bit_length()
+    steps = 3
 
     def sums(pieces, rows):
         return [
@@ -719,7 +862,6 @@
         ]
 
     pairs = low(heads // 2, span, 128)
-    whole = low(width, width)
     rows, turned = low(span, width), low(width, span)
     any_, vmem = pl.BlockSpec(memory_space=pl.ANY), pl.BlockSpec(memory_space=VMEM)
     result = lambda *shape: jax.ShapeDtypeStruct(shape, LOW)
@@ -728,21 +870,24 @@
         out_shape=[
             result(n_seq, span // n_seq, width), result(n_seq, span // n_seq, width),
             result(ff_pieces, FF_ROWS, 128), result(att_pieces, ATT_ROWS, 128),
-            jax.ShapeDtypeStruct((16, width), F32),
-            result(heads, span, span), result(ff_width // 256, span, 256), result(ff_width // 256, span, 256),
+            jax.ShapeDtypeStruct((24, 128), F32),
+            result(heads, span, span), result(ff_width // 512, 2, span, 512),
         ],
         in_specs=[any_] * 2 + [vmem] * 5 + [any_] * 7,
-        out_specs=[any_] * 4 + [vmem] + [any_] * 3,
+        out_specs=[any_] * 4 + [vmem] + [any_] * 2,
         scratch_shapes=sums(ff_pieces, FF_ROWS)
         + sums(att_pieces, ATT_ROWS)
-        + [VMEM((steps + 1, 16, width), F32), VMEM((steps, 16, width), F32), dma((2, steps))]
+        + [
+            VMEM((steps + 1, 24, 128), F32), VMEM((steps, 24, 128), F32), VMEM((n_seq, 24, 128), F32),
+            dma((2, steps)), dma((2, n_seq)),
+        ]
         + [
             rows, rows, VMEM((n_seq, 8, 128), jnp.int32), VMEM((n_seq, 8, 128), jnp.int32), rows,
-            whole, whole, whole, whole, low(2, width, 512), low(2, 256, width),
-            low(2, 2, span, span), low(2, span, 256), low(2, span, 256),
+            low(width, width), low(2, width, 1024), low(1024, width), low(2, 2, span, span), VMEM((16, span), F32),
             low(ff_width // 256, 256, span), turned, pairs, pairs, pairs, turned, VMEM((span, width), F32),
-            VMEM((span, width), F32), rows, turned, turned, VMEM((16, 1024), F32),
-            dma((4,)), dma((3, 2)), dma((2, 2)), dma((2,)), dma((5, 2, n_seq)), dma((5,)),
+            VMEM((span, width), F32), rows, rows, turned, turned, VMEM((16, 1024), F32),
+            VMEM((heads, 2 * (span // 128) - 1, 8, 256), F32),
+            dma((4,)), dma((3, 2)), dma((2,)), dma((5, 2, n_seq)), dma((5,)),
         ],
         compiler_params=pltpu.CompilerParams(
             collective_id=0, has_side_effects=True, vmem_limit_bytes=VMEM_BYTES
@@ -772,12 +917,13 @@
             for i in range(4):
                 col = 512 * g + 128 * i
                 out[:, col : col + 128] = ff_ref[4 + 2 * g + k, shard * i : shard * i + shard, :].astype(F32)
-    table_out[...] = small_ref[: table_out.shape[1], :128].T[: table_out.shape[0], :]
+    table_out[...] = small_ref[: table_out.shape[0], : table_out.shape[1]]
     mine = lax.axis_index("dp") // (n_dp // GROUP)
-    for row, out in ((12, gn_two_out), (13, gn_one_out)):
+    for row, out in ((12, gn_two_out), (18, gn_one_out)):
+        gains = jnp.concatenate([small_ref[row + i : row + i + 1, :] for i in range(width // 128)], axis=1)
         total = jnp.zeros((1, shard), F32)
         for s in range(GROUP):
-            total = total + jnp.where(mine == s, small_ref[row : row + 1, shard * s : shard * s + shard], 0.0)
+            total = total + jnp.where(mine == s, gains[:, shard * s : shard * s + shard], 0.0)
         out[...] = total
 
 
@@ -789,7 +935,7 @@
         functools.partial(outputs_kernel, n_dp),
         out_shape=[
             jax.ShapeDtypeStruct(mixed.shape, LOW), full(*tokens.shape), full(1, shard),
-            full(shard, width), full(shard, width), full(shard, width), full(shard, width), full(buckets, heads),
+            full(shard, width), full(shard, width), full(shard, width), full(shard, width), full(heads, buckets),
             full(1, shard), full(shard, 2048), full(shard, 2048), full(256, width),
         ],
         compiler_params=pltpu.CompilerParams(vmem_limit_bytes=VMEM_BYTES),
@@ -808,10 +954,10 @@
         gain_one, gain_two = norm_attn.reshape(1, -1), norm_ff.reshape(1, -1)
         weights = (w_query, w_key, w_value, w_output, w_gate, w_up, w_down)
         sums = layer(
-            n_dp, n_seq, tokens, cotangent, segments, buckets, gain_one, gain_two, bias_table, weights
+            n_dp, n_seq, tokens, cotangent, segments, buckets, gain_one, gain_two, bias_table.T, weights
         )[:5]
         results = list(outputs(n_dp, bias_table.shape[0], bias_table.shape[1], *sums))
-        results[2], results[8] = results[2].reshape(-1), results[8].reshape(-1)
+        results[2], results[7], results[8] = results[2].reshape(-1), results[7].T, results[8].reshape(-1)
         rest = n_dp // GROUP
         if rest > 1:
             groups = [[i * rest + j for j in range(rest)] for i in range(GROUP)]

time: 168 us -> 154 us (0.917)
  Pallas kernels: 160 us -> 149 us
  local copies, waits for them, and re-layouts: 6.58 us -> 3.82 us
    pallas_call x1, Pallas kernels: 156 us -> 144 us  [layer(): pl.pallas_call(functools.partial(layer_kernel, n_dp, n_seq), out_shape=[r...]
    unnamed x2 -> x0, local copies, waits for them, and re-layouts: 2.77 us -> none
where the time goes in v3:
time: 154 us; the launch traced here: 153 us
  Pallas kernels  149 us (97%)
  local copies, waits for them, and re-layouts  3.82 us (2%)
    pallas_call x1, Pallas kernels, layer(): pl.pallas_call(functools.partial(layer_kernel, n_dp, n_seq), out_shape=[r...  144 us
    pallas_call x1, Pallas kernels, outputs(): pl.pallas_call(functools.partial(outputs_kernel, n_dp), out_shape=[jax.Sh...  4.59 us

profile of v3, /device:TPU:0, one launch (start us, length us, event | category | flops | bytes accessed | tf_op | source)
XLA Modules:
  0.0 153.4 jit_solution(1923447973121607524)
XLA Ops:
  0.6 1.3 reshape.40.gain_one_ref
  1.9 1.3 reshape.41.gain_two_ref
  3.2 1.3 pad.4
  4.5 144.3 %layer.1 = (bf16[4,128,768]{2,1,0:T(8,128)(2,1)}, bf16[4,128,768]{2,1,0:T(8,128)(2,1)}, bf16[12,384,128]{2,1,0:T(8,128)(2,1)}, bf16[8,288,128]{2,1,0:T(8,128)(2,...) custom-call(bf16[4,128,768]{2,1,0:T(8,128)(2,1)} %tokens_hbm.1, ...), custom_call_target="tpu_custom_call" | custom-call | tf_op jit(solution)/shard_map/layer/pallas_call | solution.py:868
  148.8 4.6 %outputs.1 = (bf16[4,128,768]{2,1,0:T(8,128)(2,1)}, f32[4,128,768]{2,1,0:T(8,128)}, f32[1,96]{1,0:T(1,128)}, f32[96,768]{1,0:T(8,128)}, f32[96,768]{1,0:T(8,128)...) custom-call(bf16[4,128,768]{2,1,0:T(8,128)(2,1)} %get-tuple-element., ...), custom_call_target="tpu_custom_call" | custom-call | tf_op jit(solution)/shard_map/outputs/pallas_call | solution.py:934

commit v4 on v3

--- a/solution.py
+++ b/solution.py
@@ -54,33 +54,43 @@
         return (self.dp, self.z + bit * (1 - 2 * ((self.z // bit) % 2)))
 
 
-def remote(src, dst, sems, index, peer):
+def remote(src, dst, send_sem, recv_sem, peer):
     return pltpu.make_async_remote_copy(
-        src_ref=src, dst_ref=dst, send_sem=sems.at[0, index], recv_sem=sems.at[1, index],
-        device_id=peer, device_id_type=MESH,
+        src_ref=src, dst_ref=dst, send_sem=send_sem, recv_sem=recv_sem, device_id=peer, device_id_type=MESH
     )
 
 
 class Sums:
-    def __init__(self, place, own, sems, got0, got1, got2, low_z, high_z):
-        self.place, self.own, self.sems = place, own, sems
+    def __init__(self, place, own, got0, got1, got2, low_z, high_z, send_sems, recv_sems, z_sems, out_sem):
+        self.place, self.own = place, own
         self.got0, self.got1, self.got2, self.low_z, self.high_z = got0, got1, got2, low_z, high_z
-
-    def copy0(self, p):
-        at = self.place
-        return remote(self.own.at[p, 1 - at.core], self.got0.at[p], self.sems.at[0], p, at.core_peer)
-
-    def copy1(self, p, k):
-        at = self.place
+        self.send_sems, self.recv_sems, self.z_sems, self.out_sem = send_sems, recv_sems, z_sems, out_sem
+
+    def arrived(self, stage, j):
+        got = (self.got0, self.got1, self.got2)[stage].at[pl.ds(2 * j, 2)]
+        remote(got, got, self.send_sems.at[stage], self.recv_sems.at[stage, j], self.place.core_peer).wait_recv()
+
+    def send0(self, j, k):
+        at, p = self.place, 2 * j + k
+        remote(
+            self.own.at[p, 1 - at.core], self.got0.at[p], self.send_sems.at[0], self.recv_sems.at[0, j], at.core_peer
+        ).start()
+
+    def send1(self, j, k):
+        at, p = self.place, 2 * j + k
         mine = self.own.at[p, at.core]
         src = mine.at[1 - at.y] if k else mine.at[:, 1 - at.x]
-        return remote(src, self.got1.at[p], self.sems.at[1], p, at.y_peer if k else at.x_peer)
-
-    def copy2(self, p, k):
-        at = self.place
+        remote(
+            src, self.got1.at[p], self.send_sems.at[1], self.recv_sems.at[1, j], at.y_peer if k else at.x_peer
+        ).start()
+
+    def send2(self, j, k):
+        at, p = self.place, 2 * j + k
         mine = self.own.at[p, at.core]
         src = mine.at[at.y, 1 - at.x] if k else mine.at[1 - at.y, at.x]
-        return remote(src, self.got2.at[p], self.sems.at[2], p, at.x_peer if k else at.y_peer)
+        remote(
+            src, self.got2.at[p], self.send_sems.at[2], self.recv_sems.at[2, j], at.x_peer if k else at.y_peer
+        ).start()
 
     def kept(self, p):
         at = self.place
@@ -88,43 +98,47 @@
 
     def up(self, p, first):
         src = self.kept(p) if first else self.got2.at[p]
-        return remote(src, self.low_z.at[p], self.sems.at[3], p, self.place.z_peer(self.place.z + 1))
+        return remote(
+            src, self.low_z.at[p], self.send_sems.at[3], self.z_sems.at[0, p], self.place.z_peer(self.place.z + 1)
+        )
 
     def down(self, p, first):
         src = self.kept(p) if first else self.got1.at[p, 0]
-        return remote(src, self.high_z.at[p], self.sems.at[4], p, self.place.z_peer(self.place.z - 1))
+        return remote(
+            src, self.high_z.at[p], self.send_sems.at[4], self.z_sems.at[1, p], self.place.z_peer(self.place.z - 1)
+        )
 
     def stage0(self, j):
         for k in range(2):
-            self.copy0(2 * j + k).start()
+            self.send0(j, k)
 
     def stage1(self, j):
         at = self.place
+        self.arrived(0, j)
         for k in range(2):
             p = 2 * j + k
-            self.copy0(p).wait_recv()
             for a in range(2):
                 for b in range(2):
                     self.own[p, at.core, a, b] = self.own[p, at.core, a, b] + self.got0[p, a, b]
-            self.copy1(p, k).start()
+            self.send1(j, k)
 
     def stage2(self, j):
         at = self.place
+        self.arrived(1, j)
         for k in range(2):
             p = 2 * j + k
-            self.copy1(p, k).wait_recv()
             for a in range(2):
                 if k:
                     self.own[p, at.core, at.y, a] = self.own[p, at.core, at.y, a] + self.got1[p, a]
                 else:
                     self.own[p, at.core, a, at.x] = self.own[p, at.core, a, at.x] + self.got1[p, a]
-            self.copy2(p, k).start()
+            self.send2(j, k)
 
     def stage3(self, j):
         at = self.place
+        self.arrived(2, j)
         for k in range(2):
             p = 2 * j + k
-            self.copy2(p, k).wait_recv()
             self.own[p, at.core, at.y, at.x] = self.own[p, at.core, at.y, at.x] + self.got2[p]
         self.hop(j, 0)
 
@@ -150,7 +164,7 @@
                     self.got1[p, 0] = self.high_z[p] + self.own[p, at.core, at.y, at.x]
                 self.down(p, step == 0).start()
 
-    def finish(self, j, out, out_sems):
+    def finish(self, j, out):
         at = self.place
         last = at.n_seq - 1
         for k in range(2):
@@ -171,31 +185,29 @@
                 total = self.low_z[p].astype(F32) + self.high_z[p].astype(F32)
                 self.low_z[p] = (total + self.own[p, at.core, at.y, at.x].astype(F32)).astype(LOW)
 
-            pltpu.make_async_copy(self.low_z.at[p], out.at[p], out_sems.at[p]).start()
-
-    def drain(self, j, out, out_sems):
+            pltpu.make_async_copy(self.low_z.at[p], out.at[p], self.out_sem.at[0]).start()
+
+    def drain(self, out):
         at = self.place
         last = at.n_seq - 1
-        for k in range(2):
-            p = 2 * j + k
-            self.copy0(p).wait_send()
-            self.copy1(p, k).wait_send()
-            self.copy2(p, k).wait_send()
-
-            @pl.when(at.z == 0)
-            def _():
-                self.up(p, True).wait_send()
-
-            @pl.when((at.z > 0) & (at.z < last))
-            def _():
-                self.up(p, False).wait_send()
-                self.down(p, False).wait_send()
-
-            @pl.when(at.z == last)
-            def _():
-                self.down(p, True).wait_send()
-
-            pltpu.make_async_copy(self.low_z.at[p], out.at[p], out_sems.at[p]).wait()
+
+        def sent(stage, all_pieces):
+            remote(
+                all_pieces, all_pieces, self.send_sems.at[stage], self.recv_sems.at[0, 0], at.core_peer
+            ).wait_send()
+
+        for stage, got in enumerate((self.got0, self.got1, self.got2)):
+            sent(stage, got)
+
+        @pl.when(at.z < last)
+        def _():
+            sent(3, self.low_z)
+
+        @pl.when(at.z > 0)
+        def _():
+            sent(4, self.high_z)
+
+        pltpu.make_async_copy(self.low_z, out, self.out_sem.at[0]).wait()
 
 
 FF_JOBS, ATT_JOBS = 6, 4
@@ -204,17 +216,17 @@
 
 def layer_kernel(
     n_dp, n_seq,
-    tokens_hbm, cot_hbm, seg_ref, bucket_ref, gain_one_ref, gain_two_ref, table_ref,
+    tokens_hbm, cot_hbm, seg_ref, bucket_row, gain_one_row, gain_two_row, table_ref,
     wq_hbm, wk_hbm, wv_hbm, wo_hbm, wg_hbm, wu_hbm, wd_hbm,
     mixed_out, tokens_out, ff_out, att_out, small_out, probs_hbm, slope_hbm,
-    ff_own, ff_got0, ff_got1, ff_got2, ff_low, ff_high, ff_sems, ff_out_sems,
-    att_own, att_got0, att_got1, att_got2, att_low, att_high, att_sems, att_out_sems,
-    small_own, small_got, small_rows, small_sems, small_row_sems,
+    ff_own, ff_got0, ff_got1, ff_got2, ff_low, ff_high, ff_sends, ff_recvs, ff_z_recvs, ff_out_sem,
+    att_own, att_got0, att_got1, att_got2, att_low, att_high, att_sends, att_recvs, att_z_recvs, att_out_sem,
+    small_own, small_got, small_rows, small_sems,
     x_ref, cot_ref, seg_send_ref, seg_rows_ref, mixed_ref,
     wo_ref, wgu_ref, wd_ref, probs_ref, inverse_ref,
     activ_t_ref, attended_t_ref, q_ref, k_ref, v_ref, k_t_ref, resid_ref, acc_ref, branch_ref, d_branch_ref,
-    d_att_t_ref, d_q_t_ref, offset_ref, diag_ref,
-    load_sems, ff_load_sems, probs_sems, row_sems, own_sems,
+    d_att_t_ref, d_q_t_ref, offset_ref, diag_ref, bucket_ref, gain_one_ref, gain_two_ref,
+    load_sems, ff_load_sems, probs_sems, send_sems, recv_sems, token_sems, own_sems,
 ):
     span, width = x_ref.shape
     heads, buckets = table_ref.shape
@@ -272,33 +284,62 @@
         pl.semaphore_signal(barrier, inc=1, device_id=peer, device_id_type=MESH)
     pl.semaphore_wait(barrier, len(peers))
 
-    ff = Sums(at, ff_own, ff_sems, ff_got0, ff_got1, ff_got2, ff_low, ff_high)
-    att = Sums(at, att_own, att_sems, att_got0, att_got1, att_got2, att_low, att_high)
+    ff = Sums(
+        at, ff_own, ff_got0, ff_got1, ff_got2, ff_low, ff_high, ff_sends, ff_recvs, ff_z_recvs, ff_out_sem
+    )
+    att = Sums(
+        at, att_own, att_got0, att_got1, att_got2, att_low, att_high, att_sends, att_recvs, att_z_recvs, att_out_sem
+    )
 
     def block(z):
         return pl.ds(pl.multiple_of(z * 128, 128), 128)
 
-    def exchange(kind, src, dst):
-        copies = []
-        for i in range(1, n_seq):
-            to = lax.rem(at.z + i, n_seq)
-            copies.append(
-                pltpu.make_async_remote_copy(
-                    src_ref=src(to), dst_ref=dst(at.z),
-                    send_sem=row_sems.at[kind, 0, i], recv_sem=row_sems.at[kind, 1, i],
-                    device_id=at.z_peer(to), device_id_type=MESH,
-                )
-            )
-        copies.append(pltpu.make_async_copy(src(at.z), dst(at.z), own_sems.at[kind]))
-        return copies
-
-    segs = exchange(0, lambda z: seg_send_ref.at[z], lambda z: seg_rows_ref.at[z])
-    tokens_in = exchange(1, lambda z: tokens_hbm.at[z], lambda z: x_ref.at[block(z), :])
-    cot_in = exchange(2, lambda z: cot_hbm.at[z], lambda z: cot_ref.at[block(z), :])
-    mixed_back = exchange(3, lambda z: mixed_ref.at[block(z), :], lambda z: mixed_out.at[z])
-    tokens_back = exchange(4, lambda z: d_back_ref.at[block(z), :], lambda z: tokens_out.at[z])
-    start(segs)
-    start(tokens_in)
+    def pick(values):
+        return sum(jnp.where(at.z == z, value, 0) for z, value in enumerate(values))
+
+    nearest = [sorted(range(n_seq), key=lambda other: abs(other - z)) for z in range(n_seq)]
+
+    def exchange(kind, src, dst, recv_of=None):
+        sends = []
+        for i in range(n_seq - 1):
+            to = pick([near[i + 1] for near in nearest])
+            recv = recv_sems.at[kind] if recv_of is None else recv_of.at[at.z]
+            sends.append(remote(src(to), dst(at.z), send_sems.at[kind], recv, at.z_peer(to)))
+        return sends, pltpu.make_async_copy(src(at.z), dst(at.z), own_sems.at[kind])
+
+    def begin(exchanged):
+        sends, own = exchanged
+        start(sends)
+        own.start()
+
+    def arrive(kind, others, one):
+        remote(others, others, send_sems.at[kind], recv_sems.at[kind], at.core_peer).wait_recv()
+        pltpu.make_async_copy(one, one, own_sems.at[kind]).wait()
+
+    def sent(kind, others):
+        remote(others, others, send_sems.at[kind], recv_sems.at[kind], at.core_peer).wait_send()
+
+    SEGS, TOKENS, COT, MIXED, BACK = range(5)
+    segs = exchange(SEGS, lambda z: seg_send_ref.at[z], lambda z: seg_rows_ref.at[z])
+    tokens_in = exchange(TOKENS, lambda z: tokens_hbm.at[z], lambda z: x_ref.at[block(z), :], token_sems)
+    cot_in = exchange(COT, lambda z: cot_hbm.at[z], lambda z: cot_ref.at[block(z), :])
+    mixed_back = exchange(MIXED, lambda z: mixed_ref.at[block(z), :], lambda z: mixed_out.at[z])
+    tokens_back = [
+        exchange(
+            BACK,
+            lambda z, part=part: d_back_ref.at[pl.ds(pl.multiple_of(z * 128 + 32 * part, 32), 32), :],
+            lambda z, part=part: tokens_out.at[z, pl.ds(32 * part, 32), :],
+        )
+        for part in range(4)
+    ]
+    three_segs, one_seg = seg_rows_ref.at[pl.ds(0, n_seq - 1)], seg_rows_ref.at[0]
+    three_blocks, one_block = x_ref.at[pl.ds(0, 128 * (n_seq - 1)), :], x_ref.at[pl.ds(0, 128), :]
+    begin(segs)
+    bucket_ref[...] = jnp.zeros_like(bucket_ref)
+    bucket_ref[:, : bucket_row.shape[0]] = bucket_row[...].reshape(1, -1)
+    gain_one_ref[...] = gain_one_row[...].reshape(1, -1)
+    gain_two_ref[...] = gain_two_row[...].reshape(1, -1)
+    begin(tokens_in)
     def forward(bias_ref, key_seg_ref, query_seg_ref):
         one_hot = (lax.broadcasted_iota(jnp.int32, (buckets, buckets_wide), 0) == bucket_ref[...]).astype(F32)
         offset_ref[:heads, :] = lax.dot_general(
@@ -313,7 +354,7 @@
                 window = jnp.broadcast_to(row[:, 128 * d : 128 * d + 256], (128, 256))
                 bias_ref[h, d] = pltpu.roll(window, 129, 1, stride=1, stride_axis=0)[:, :128].T
 
-        wait(segs)
+        arrive(SEGS, three_segs, one_seg)
         seg_rows = [seg_rows_ref[i, 0:1, :].astype(F32) for i in range(blocks)]
         for i in range(blocks):
             column = jnp.broadcast_to(seg_rows[i], (128, 128)).T
@@ -322,28 +363,43 @@
             key_seg_ref[128 * i : 128 * i + 128, :] = jnp.where(column == across, 1.0, 0.0).astype(LOW)
             query_seg_ref[:, 128 * i : 128 * i + 128] = jnp.where(seg_rows[i] == along, 0.0, MASKED).astype(LOW)
         wait(loads)
-        wait(tokens_in)
-        start(cot_in)
-
-        @pl.loop(0, blocks)
+        q_t_ref, v_t_ref = d_att_t_ref, d_q_t_ref
+
+        @pl.loop(0, n_seq)
         def _(i):
-            inputs = x_ref[block(i), :].astype(F32)
-            branch_ref[block(i), :] = (inputs * inverse_rms(inputs) * gain_one_ref[...]).astype(LOW)
-
-        q_t_ref, v_t_ref = d_att_t_ref, d_q_t_ref
-        for tile in range(width // 256):
-            cols = slice(256 * tile, 256 * tile + 256)
-            q = dot(branch_ref[...], wq_ref[:, cols])
-            q_t_ref[cols, :] = q.T.astype(LOW)
-            k = dot(branch_ref[...], wk_ref[:, cols])
-            k_t_ref[cols, :] = k.T.astype(LOW)
-            v = dot(branch_ref[...], wv_ref[:, cols])
-            v_t_ref[cols, :] = v.T.astype(LOW)
-            for i in range(2):
-                lanes = slice(128 * i, 128 * i + 128)
-                q_ref[2 * tile + i] = q[:, lanes].astype(LOW)
-                k_ref[2 * tile + i] = k[:, lanes].astype(LOW)
-                v_ref[2 * tile + i] = v[:, lanes].astype(LOW)
+            source = pick([jnp.where(i == 0, z, 0) for z in range(n_seq)])
+            for j in range(1, n_seq):
+                source = source + jnp.where(i == j, pick([near[j] for near in nearest]), 0)
+
+            @pl.when(i == 0)
+            def _():
+                tokens_in[1].wait()
+
+            @pl.when(i > 0)
+            def _():
+                arrived = x_ref.at[block(source), :]
+                remote(
+                    arrived, arrived, send_sems.at[TOKENS], token_sems.at[source], at.z_peer(source)
+                ).wait_recv()
+
+            @pl.when(i == n_seq - 1)
+            def _():
+                begin(cot_in)
+
+            rows = block(source)
+            inputs = x_ref[rows, :].astype(F32)
+            hidden = (inputs * inverse_rms(inputs) * gain_one_ref[...]).astype(LOW)
+            for tile in range(width // 256):
+                cols = slice(256 * tile, 256 * tile + 256)
+                q, k, v = [dot(hidden, ref[:, cols]) for ref in (wq_ref, wk_ref, wv_ref)]
+                q_t_ref[cols, rows] = q.T.astype(LOW)
+                k_t_ref[cols, rows] = k.T.astype(LOW)
+                v_t_ref[cols, rows] = v.T.astype(LOW)
+                for b in range(2):
+                    lanes = slice(128 * b, 128 * b + 128)
+                    q_ref[2 * tile + b, rows, :] = q[:, lanes].astype(LOW)
+                    k_ref[2 * tile + b, rows, :] = k[:, lanes].astype(LOW)
+                    v_ref[2 * tile + b, rows, :] = v[:, lanes].astype(LOW)
 
         start(weight_loads(0, 0))
         score_refs = (acc_ref, resid_ref)
@@ -429,7 +485,11 @@
                 slope_copy(g - 2, slot, True).wait()
 
             wait(weight_loads(g, slot))
-            start(weight_loads(lax.rem(g + 1, tiles), 1 - slot))
+
+            @pl.when(g < tiles - 1)
+            def _():
+                start(weight_loads(g + 1, 1 - slot))
+
             gates = [dot(branch_ref[...], wgu_ref[slot, :, 256 * i : 256 * i + 256]) for i in range(4)]
             activs = []
             for sub in range(2):
@@ -448,7 +508,11 @@
                 activs.append(activ.astype(LOW))
             down = wd_ref[pl.ds(pl.multiple_of(slot * 512, 512), 512)]
             acc_ref[...] += dot(jnp.concatenate(activs, axis=1), down)
-            slope_copy(g, slot, True).start()
+
+            @pl.when(g < tiles - 2)
+            def _():
+                slope_copy(g, slot, True).start()
+
 
         mixed_ref[...] = acc_ref[...].astype(LOW)
 
@@ -458,11 +522,7 @@
         key_seg_ref=VMEM((span, 128), LOW),
         query_seg_ref=VMEM((128, span), LOW),
     )
-    start(mixed_back)
-    for g in (tiles - 2, tiles - 1):
-        slope_copy(g, g % 2, True).wait()
-    slope_copy(0, 0, False).start()
-    wait(cot_in)
+    arrive(COT, three_blocks, one_block)
 
     def backward(hidden_t_ref, d_att_ref, d_k_ref, d_v_ref, d_probs_ref):
         for s in range(GROUP):
@@ -474,6 +534,8 @@
                     ]
         ff.stage0(0)
         ff.stage0(1)
+        sent(COT, three_blocks)
+        begin(mixed_back)
 
         acc_ref[...] = jnp.zeros_like(acc_ref)
 
@@ -482,15 +544,14 @@
             return att_own.at[2 * g + k, n // 4, (n // 2) % 2, n % 2, pl.ds(0, 256), :]
 
         @pl.loop(0, tiles)
-        def _(g):
+        def _(step):
+            g = tiles - 1 - step
             slot = lax.rem(g, 2)
-            wait(weight_loads(g, slot))
-            slope_copy(g, slot, False).wait()
-
-            @pl.when(g < tiles - 1)
-            def _():
-                start(weight_loads(g + 1, 1 - slot))
-                slope_copy(g + 1, 1 - slot, False).start()
+
+            @pl.when(step >= 2)
+            def _():
+                wait(weight_loads(g, slot))
+                slope_copy(g, slot, False).wait()
 
             d_sides = [[], []]
             for sub in range(2):
@@ -505,64 +566,63 @@
                             d_slot(g, k, 2 * sub + i, half)[...] = d_side[
                                 256 * half : 256 * half + 256, 128 * i : 128 * i + 128
                             ]
+            resid = resid_ref[block(step), :]
+            hidden_t_ref[:, block(step)] = (resid * inverse_rms(resid) * gain_two_ref[...]).T.astype(LOW)
             d_both = jnp.concatenate(d_sides[0] + d_sides[1], axis=1)
             for tile in range(width // 256):
                 cols = slice(256 * tile, 256 * tile + 256)
                 acc_ref[:, cols] += dot_back(d_both, wgu_ref[slot, cols, :])
 
-            @pl.when(g <= 1)
-            def _():
-                ff.stage1(g)
+            @pl.when(step <= 1)
+            def _():
+                start(weight_loads(g - 2, slot))
+                slope_copy(g - 2, slot, False).start()
+
+
+            @pl.when(step == 0)
+            def _():
+                ff.stage1(0)
 
         start(loads)
         probs_copy(0, 0, False).start()
 
-        @pl.loop(0, blocks)
-        def _(i):
-            resid = resid_ref[block(i), :]
-            hidden_t_ref[:, block(i)] = (resid * inverse_rms(resid) * gain_two_ref[...]).T.astype(LOW)
-
-        ff.stage2(0)
-
-        def products(g):
-            for k in range(2):
-                for sub in range(2):
-                    right = jnp.concatenate(
-                        [
-                            jnp.concatenate([d_slot(g, k, 2 * sub + i, half)[...] for half in range(2)], axis=0)
-                            for i in range(2)
-                        ],
-                        axis=1,
-                    )
-                    product = dot(hidden_t_ref[...], right).astype(LOW)
-                    for s in range(GROUP):
-                        for i in range(2):
-                            place = shard * (2 * sub + i)
-                            ff_own[4 + 2 * g + k, s % 2, s // 4, (s // 2) % 2, place : place + shard, :] = product[
-                                shard * s : shard * s + shard, 128 * i : 128 * i + 128
-                            ]
-            ff.stage0(2 + g)
-
-        def norm_back(vector_ref, gain_ref, extra_ref, low_ref, row):
+
+        def product(g, k, sub):
+            right = jnp.concatenate(
+                [
+                    jnp.concatenate([d_slot(g, k, 2 * sub + i, half)[...] for half in range(2)], axis=0)
+                    for i in range(2)
+                ],
+                axis=1,
+            )
+            result = dot(hidden_t_ref[...], right).astype(LOW)
+            for s in range(GROUP):
+                for i in range(2):
+                    place = shard * (2 * sub + i)
+                    ff_own[4 + 2 * g + k, s % 2, s // 4, (s // 2) % 2, place : place + shard, :] = result[
+                        shard * s : shard * s + shard, 128 * i : 128 * i + 128
+                    ]
+
+        def norm_back(grad_ref, vector_ref, gain_ref, extra_ref, out_ref, low_ref, row):
             total = jnp.zeros((1, width), F32)
             for i in range(blocks):
                 rows = slice(128 * i, 128 * i + 128)
                 vector = vector_ref[rows, :].astype(F32)
                 scale = inverse_rms(vector)
                 normed = vector * scale
-                grad = acc_ref[rows, :]
+                grad = grad_ref[rows, :]
                 total = total + jnp.sum(grad * normed, axis=0, keepdims=True)
                 inner = grad * gain_ref[...]
                 result = extra_ref[rows, :].astype(F32) + scale * (
                     inner - normed * jnp.mean(inner * normed, -1, keepdims=True)
                 )
-                acc_ref[rows, :] = result
+                if out_ref is not None:
+                    out_ref[rows, :] = result
                 low_ref[rows, :] = result.astype(LOW)
             for i in range(width // 128):
                 small_own[0, row + i : row + i + 1, :] = total[:, 128 * i : 128 * i + 128]
 
-        norm_back(resid_ref, gain_two_ref, cot_ref, d_branch_ref, 12)
-        products(0)
+        norm_back(acc_ref, resid_ref, gain_two_ref, cot_ref, acc_ref, d_branch_ref, 12)
 
         def share(sums, j, left_t, right):
             for k in range(2):
@@ -633,12 +693,13 @@
 
             return half_of
 
+        ff.stage2(0)
+        ff.stage1(1)
         first = put_d_probs(0, 0)
         for half in range(2):
             first(half)
 
-        @pl.loop(0, pairs)
-        def _(pair):
+        def attention_back(pair, with_products):
             slot = lax.rem(pair, 2)
             probs_copy(pair, slot, False).wait()
 
@@ -651,6 +712,8 @@
                 now = put_d_scores(pair, b, slot)
                 for half in range(2):
                     ahead(half)
+                    if with_products:
+                        product(pair, b, half)
                     now(half)
             lanes = pl.ds(pl.multiple_of(pair * 128, 128), 128)
             d_att, queries = d_att_ref[pair], q_ref[pair]
@@ -664,66 +727,67 @@
                 dot(d_scores[0], jnp.where(left_half, queries, blank))
                 + dot(d_scores[1], jnp.where(left_half, blank, queries))
             ).astype(LOW)
-            @pl.when(lax.rem(pair, 2) == 1)
-            def _():
-                products((pair + 1) // 2)
+
+        @pl.loop(0, tiles)
+        def _(pair):
+            attention_back(pair, True)
+            ff.stage0(2 + pair)
 
             @pl.when(pair == 0)
             def _():
+                ff.stage3(0)
+
+            @pl.when(pair == 1)
+            def _():
                 ff.stage1(2)
+
+            @pl.when(pair == 2)
+            def _():
                 ff.stage2(1)
-
-            @pl.when(pair == 1)
-            def _():
-                ff.stage3(0)
-
-            @pl.when(pair == 2)
-            def _():
                 ff.stage1(3)
-
-            @pl.when(pair == 3)
+                ff.hop(0, 1)
+
+        @pl.loop(tiles, pairs)
+        def _(pair):
+            attention_back(pair, False)
+
+            @pl.when(pair == tiles)
             def _():
                 ff.stage2(2)
+                ff.stage1(4)
                 ff.stage3(1)
-
-            @pl.when(pair == 4)
-            def _():
-                ff.stage1(4)
-                ff.hop(0, 1)
-
-            @pl.when(pair == 5)
-            def _():
-                ff.stage2(3)
 
         branch_ref[...] = d_q_t_ref[...].T
         wait(loads)
         for tile in range(width // 256):
             rows = slice(256 * tile, 256 * tile + 256)
-            resid_ref[:, rows] = acc_ref[:, rows]
-            acc_ref[:, rows] = (
+            resid_ref[:, rows] = (
                 dot_back(branch_ref[...], wgu_ref[0, rows, :width])
                 + dot_back(d_k_ref[...], wgu_ref[1, rows, :width])
                 + dot_back(d_v_ref[...], wd_ref[rows, :])
             )
+        ff.stage2(3)
         ff.stage1(5)
+        norm_back(resid_ref, x_ref, gain_one_ref, acc_ref, None, d_back_ref, 18)
+        ff.hop(1, 1)
         ff.stage3(2)
-        norm_back(x_ref, gain_one_ref, resid_ref, d_back_ref, 18)
-        ff.hop(1, 1)
+        begin(tokens_back[0])
+        share(att, 0, attended_t_ref[...], d_branch_ref[...])
         ff.hop(0, 2)
-        start(tokens_back)
-        share(att, 0, attended_t_ref[...], d_branch_ref[...])
 
         @pl.loop(0, blocks)
         def _(i):
             inputs = x_ref[block(i), :].astype(F32)
             hidden_t_ref[:, block(i)] = (inputs * inverse_rms(inputs) * gain_one_ref[...]).T.astype(LOW)
 
+        share(att, 1, hidden_t_ref[...], d_v_ref[...])
+        share(att, 2, hidden_t_ref[...], d_k_ref[...])
         ff.stage2(4)
         att.stage1(0)
-        share(att, 1, hidden_t_ref[...], d_v_ref[...])
+        share(att, 3, hidden_t_ref[...], branch_ref[...])
+        ff.hop(2, 1)
+        begin(tokens_back[1])
         ff.stage3(3)
-        share(att, 2, hidden_t_ref[...], d_k_ref[...])
-        share(att, 3, hidden_t_ref[...], branch_ref[...])
 
     pl.run_scoped(
         backward,
@@ -733,11 +797,6 @@
         d_v_ref=VMEM((span, width), LOW),
         d_probs_ref=VMEM((span, span), F32),
     )
-
-    ff.hop(2, 1)
-    ff.hop(1, 2)
-    ff.stage2(5)
-    att.stage1(1)
 
     flip = (
         lax.broadcasted_iota(jnp.int32, (256, 256), 0) + lax.broadcasted_iota(jnp.int32, (256, 256), 1) == 255
@@ -766,13 +825,12 @@
     steps = len(small_peers)
 
     def small_copy(i):
-        return remote(small_own.at[i], small_got.at[i], small_sems, i, small_peers[i])
+        return remote(small_own.at[i], small_got.at[i], small_sems.at[3], small_sems.at[i], small_peers[i])
 
     def small_row(i):
-        return pltpu.make_async_remote_copy(
-            src_ref=small_own.at[steps], dst_ref=small_rows.at[at.z],
-            send_sem=small_row_sems.at[0, i], recv_sem=small_row_sems.at[1, i],
-            device_id=at.z_peer(lax.rem(at.z + i, n_seq)), device_id_type=MESH,
+        return remote(
+            small_own.at[steps], small_rows.at[at.z], small_sems.at[4], small_sems.at[5],
+            at.z_peer(lax.rem(at.z + i, n_seq)),
         )
 
     def small_step(i):
@@ -781,67 +839,82 @@
         if i + 1 < steps:
             small_copy(i + 1).start()
 
+    inner = (at.z > 0) & (at.z < n_seq - 1)
     small_copy(0).start()
+    ff.stage2(5)
+    att.stage1(1)
     ff.stage3(4)
+    small_step(0)
+    ff.hop(1, 2)
     att.stage2(0)
     att.stage1(2)
-    small_step(0)
+    ff.hop(3, 1)
+    begin(tokens_back[2])
     ff.stage3(5)
     att.stage2(1)
     att.stage1(3)
+    ff.hop(4, 1)
+    ff.hop(2, 2)
     att.stage3(0)
-    ff.hop(3, 1)
+    small_step(1)
     att.stage2(2)
-    small_step(1)
+    ff.hop(5, 1)
+    ff.hop(3, 2)
     att.stage3(1)
-    ff.hop(2, 2)
-    ff.hop(4, 1)
+    att.hop(0, 1)
     att.stage2(3)
+    ff.hop(4, 2)
     small_step(2)
     small_rows[at.z] = small_own[steps]
     att.stage3(2)
-    ff.hop(3, 2)
-    ff.hop(5, 1)
+    att.hop(1, 1)
     att.stage3(3)
     for i in range(1, n_seq):
         small_row(i).start()
-    ff.hop(4, 2)
-    att.hop(0, 1)
     ff.hop(5, 2)
-    att.hop(1, 1)
     att.hop(0, 2)
     att.hop(2, 1)
+    att.hop(3, 1)
+
+    @pl.when(inner)
+    def _():
+        begin(tokens_back[3])
+
     att.hop(1, 2)
-    att.hop(3, 1)
     att.hop(2, 2)
     att.hop(3, 2)
 
     @pl.loop(0, FF_JOBS)
     def _(j):
-        ff.finish(j, ff_out, ff_out_sems)
+        ff.finish(j, ff_out)
+
+    @pl.when(jnp.logical_not(inner))
+    def _():
+        begin(tokens_back[3])
 
     @pl.loop(0, ATT_JOBS)
     def _(j):
-        att.finish(j, att_out, att_out_sems)
-
-    for i in range(1, n_seq):
-        small_row(i).wait_recv()
+        att.finish(j, att_out)
+
+    three_rows = small_rows.at[pl.ds(0, n_seq - 1)]
+    remote(three_rows, three_rows, small_sems.at[4], small_sems.at[5], at.core_peer).wait_recv()
     total = small_rows[0]
     for i in range(1, n_seq):
         total = total + small_rows[i]
-    small_out[...] = total
-    for sums, jobs, out, sems in ((ff, FF_JOBS, ff_out, ff_out_sems), (att, ATT_JOBS, att_out, att_out_sems)):
-
-        @pl.loop(0, jobs)
-        def _(j):
-            sums.drain(j, out, sems)
-
-    for i in range(steps):
-        small_copy(i).wait_send()
-    for i in range(1, n_seq):
-        small_row(i).wait_send()
-    wait(mixed_back)
-    wait(tokens_back)
+    small_rows[0] = total
+    small_store = pltpu.make_async_copy(small_rows.at[0], small_out, own_sems.at[5])
+    small_store.start()
+    ff.drain(ff_out)
+    att.drain(att_out)
+    three_steps = small_own.at[pl.ds(0, steps)]
+    remote(three_steps, three_steps, small_sems.at[3], small_sems.at[0], at.core_peer).wait_send()
+    remote(three_rows, three_rows, small_sems.at[4], small_sems.at[5], at.core_peer).wait_send()
+    sent(SEGS, three_segs)
+    for kind in (TOKENS, MIXED, BACK):
+        sent(kind, three_blocks)
+    for kind in (MIXED, BACK):
+        arrive(kind, three_blocks, one_block)
+    small_store.wait()
 
 
 def layer(n_dp, n_seq, tokens, cot, seg, buckets, gain_one, gain_two, table, weights):
@@ -858,7 +931,7 @@
         return [
             low(pieces, 2, 2, 2, rows, 128), low(pieces, 2, 2, rows, 128), low(pieces, 2, rows, 128),
             low(pieces, rows, 128), low(pieces, rows, 128), low(pieces, rows, 128),
-            dma((5, 2, pieces)), dma((pieces,)),
+            dma((5,)), dma((3, pieces // 2)), dma((2, pieces)), dma((1,)),
         ]
 
     pairs = low(heads // 2, span, 128)
@@ -874,12 +947,12 @@
             result(heads, span, span), result(ff_width // 512, 2, span, 512),
         ],
         in_specs=[any_] * 2 + [vmem] * 5 + [any_] * 7,
-        out_specs=[any_] * 4 + [vmem] + [any_] * 2,
+        out_specs=[any_] * 7,
         scratch_shapes=sums(ff_pieces, FF_ROWS)
         + sums(att_pieces, ATT_ROWS)
         + [
             VMEM((steps + 1, 24, 128), F32), VMEM((steps, 24, 128), F32), VMEM((n_seq, 24, 128), F32),
-            dma((2, steps)), dma((2, n_seq)),
+            dma((6,)),
         ]
         + [
             rows, rows, VMEM((n_seq, 8, 128), jnp.int32), VMEM((n_seq, 8, 128), jnp.int32), rows,
@@ -887,7 +960,8 @@
             low(ff_width // 256, 256, span), turned, pairs, pairs, pairs, turned, VMEM((span, width), F32),
             VMEM((span, width), F32), rows, rows, turned, turned, VMEM((16, 1024), F32),
             VMEM((heads, 2 * (span // 128) - 1, 8, 256), F32),
-            dma((4,)), dma((3, 2)), dma((2,)), dma((5, 2, n_seq)), dma((5,)),
+            VMEM((1, 1024), jnp.int32), VMEM((1, width), F32), VMEM((1, width), F32),
+            dma((4,)), dma((3, 2)), dma((2,)), dma((5,)), dma((5,)), dma((n_seq,)), dma((6,)),
         ],
         compiler_params=pltpu.CompilerParams(
             collective_id=0, has_side_effects=True, vmem_limit_bytes=VMEM_BYTES
@@ -899,45 +973,79 @@
 def outputs_kernel(
     n_dp, mixed_ref, tokens_ref, ff_ref, att_ref, small_ref,
     mixed_out, tokens_out, gn_one_out, gq_out, gk_out, gv_out, go_out, table_out, gn_two_out, gg_out, gu_out, gd_out,
+    mixed_in, tokens_in, ff_in, att_in, small_in, gn_one, gq, gk, gv, go, table, gn_two, gg, gu, gd, tokens, sems,
 ):
-    mixed_out[...] = mixed_ref[...]
-    tokens_out[...] = tokens_ref[...].astype(F32)
+    copies = [
+        pltpu.make_async_copy(src, dst, sems.at[i])
+        for i, (src, dst) in enumerate(
+            [(small_ref, small_in), (tokens_ref, tokens_in), (ff_ref, ff_in), (att_ref, att_in), (mixed_ref, mixed_in)]
+        )
+    ]
+    for copy in copies:
+        copy.start()
+    stores = []
+
+    def store(src, dst):
+        stores.append(pltpu.make_async_copy(src, dst, sems.at[len(copies) + len(stores)]))
+        stores[-1].start()
+
     width = mixed_ref.shape[-1]
     shard = width // GROUP
-    for j, out in enumerate((go_out, gv_out, gk_out, gq_out)):
+    copies[0].wait()
+    table[...] = small_in[: table.shape[0], : table.shape[1]]
+    store(table, table_out)
+    mine = lax.axis_index("dp") // (n_dp // GROUP)
+    for row, part, out in ((12, gn_two, gn_two_out), (18, gn_one, gn_one_out)):
+        gains = jnp.concatenate([small_in[row + i : row + i + 1, :] for i in range(width // 128)], axis=1)
+        total = jnp.zeros((1, shard), F32)
+        for s in range(GROUP):
+            total = total + jnp.where(mine == s, gains[:, shard * s : shard * s + shard], 0.0)
+        part[...] = total
+        store(part, out)
+    copies[1].wait()
+    tokens[...] = tokens_in[...].astype(F32)
+    store(tokens, tokens_out)
+    copies[2].wait()
+    for k, (part, out) in enumerate(((gg, gg_out), (gu, gu_out))):
+        for g in range(4):
+            for i in range(4):
+                col = 512 * g + 128 * i
+                part[:, col : col + 128] = ff_in[4 + 2 * g + k, shard * i : shard * i + shard, :].astype(F32)
+        store(part, out)
+    for p in range(4):
+        for i in range(width // 128):
+            gd[64 * p : 64 * p + 64, 128 * i : 128 * i + 128] = ff_in[p, 64 * i : 64 * i + 64, :].astype(F32)
+    store(gd, gd_out)
+    copies[3].wait()
+    for j, (part, out) in enumerate(((go, go_out), (gv, gv_out), (gk, gk_out), (gq, gq_out))):
         for k in range(2):
             for i in range(width // 256):
                 col = width // 2 * k + 128 * i
-                out[:, col : col + 128] = att_ref[2 * j + k, shard * i : shard * i + shard, :].astype(F32)
-    for p in range(4):
-        for i in range(width // 128):
-            gd_out[64 * p : 64 * p + 64, 128 * i : 128 * i + 128] = ff_ref[p, 64 * i : 64 * i + 64, :].astype(F32)
-    for g in range(4):
-        for k, out in enumerate((gg_out, gu_out)):
-            for i in range(4):
-                col = 512 * g + 128 * i
-                out[:, col : col + 128] = ff_ref[4 + 2 * g + k, shard * i : shard * i + shard, :].astype(F32)
-    table_out[...] = small_ref[: table_out.shape[0], : table_out.shape[1]]
-    mine = lax.axis_index("dp") // (n_dp // GROUP)
-    for row, out in ((12, gn_two_out), (18, gn_one_out)):
-        gains = jnp.concatenate([small_ref[row + i : row + i + 1, :] for i in range(width // 128)], axis=1)
-        total = jnp.zeros((1, shard), F32)
-        for s in range(GROUP):
-            total = total + jnp.where(mine == s, gains[:, shard * s : shard * s + shard], 0.0)
-        out[...] = total
+                part[:, col : col + 128] = att_in[2 * j + k, shard * i : shard * i + shard, :].astype(F32)
+        store(part, out)
+    copies[4].wait()
+    store(mixed_in, mixed_out)
+    for copy in stores:
+        copy.wait()
 
 
 def outputs(n_dp, buckets, heads, mixed, tokens, ff, att, small):
     width = mixed.shape[-1]
     shard = width // GROUP
     full = lambda *shape: jax.ShapeDtypeStruct(shape, F32)
+    square, wide = full(shard, width), full(shard, 2048)
+    results = [
+        jax.ShapeDtypeStruct(mixed.shape, LOW), full(*tokens.shape), full(1, shard), square, square, square, square,
+        full(heads, buckets), full(1, shard), wide, wide, full(256, width),
+    ]
+    any_ = pl.BlockSpec(memory_space=pl.ANY)
     return pl.pallas_call(
         functools.partial(outputs_kernel, n_dp),
-        out_shape=[
-            jax.ShapeDtypeStruct(mixed.shape, LOW), full(*tokens.shape), full(1, shard),
-            full(shard, width), full(shard, width), full(shard, width), full(shard, width), full(heads, buckets),
-            full(1, shard), full(shard, 2048), full(shard, 2048), full(256, width),
-        ],
+        out_shape=results,
+        in_specs=[any_] * 5,
+        out_specs=[any_] * len(results),
+        scratch_shapes=[VMEM(a.shape, a.dtype) for a in [mixed, tokens, ff, att, small] + results[2:] + results[1:2]]
+        + [pltpu.SemaphoreType.DMA((5 + len(results),))],
         compiler_params=pltpu.CompilerParams(vmem_limit_bytes=VMEM_BYTES),
         name="outputs",
     )(mixed, tokens, ff, att, small)
@@ -950,11 +1058,9 @@
         tokens, segments, offset_buckets, norm_attn, w_query, w_key, w_value, w_output, bias_table,
         norm_ff, w_gate, w_up, w_down, cotangent,
     ):
-        buckets = jnp.pad(offset_buckets, (0, 1)).reshape(1, -1)
-        gain_one, gain_two = norm_attn.reshape(1, -1), norm_ff.reshape(1, -1)
         weights = (w_query, w_key, w_value, w_output, w_gate, w_up, w_down)
         sums = layer(
-            n_dp, n_seq, tokens, cotangent, segments, buckets, gain_one, gain_two, bias_table.T, weights
+            n_dp, n_seq, tokens, cotangent, segments, offset_buckets, norm_attn, norm_ff, bias_table.T, weights
         )[:5]
         results = list(outputs(n_dp, bias_table.shape[0], bias_table.shape[1], *sums))
         results[2], results[7], results[8] = results[2].reshape(-1), results[7].T, results[8].reshape(-1)

time: 154 us -> 140 us (0.909)
  Pallas kernels: 149 us -> 139 us
  local copies, waits for them, and re-layouts: 3.82 us -> 0 us
    pallas_call x1, Pallas kernels: 144 us -> 135 us  [layer(): pl.pallas_call(functools.partial(layer_kernel, n_dp, n_seq), out_shape=[r...]
    reshape x2 -> x0, local copies, waits for them, and re-layouts: 2.53 us -> none  [on_device(): gain_one, gain_two = (norm_attn.reshape(1, -1), norm_ff.reshape(1, -1))]
where the time goes in v4:
time: 140 us
  Pallas kernels  139 us (99%)
    pallas_call x1, Pallas kernels, layer(): pl.pallas_call(functools.partial(layer_kernel, n_dp, n_seq), out_shape=[r...  135 us
    pallas_call x1, Pallas kernels, outputs(): pl.pallas_call(functools.partial(outputs_kernel, n_dp), out_shape=results...  3.95 us

profile of v4, /device:TPU:0, one launch (start us, length us, event | category | flops | bytes accessed | tf_op | source)
XLA Modules:
  0.0 140.1 jit_solution(1259284511898174779)
XLA Ops:
  0.6 135.3 %layer.1 = (bf16[4,128,768]{2,1,0:T(8,128)(2,1)}, bf16[4,128,768]{2,1,0:T(8,128)(2,1)}, bf16[12,384,128]{2,1,0:T(8,128)(2,1)}, bf16[8,288,128]{2,1,0:T(8,128)(2,...) custom-call(bf16[4,128,768]{2,1,0:T(8,128)(2,1)} %tokens_hbm.1, ...), custom_call_target="tpu_custom_call" | custom-call | tf_op jit(solution)/shard_map/layer/pallas_call | solution.py:941
  136.0 3.9 %outputs.1 = (bf16[4,128,768]{2,1,0:T(8,128)(2,1)}, f32[4,128,768]{2,1,0:T(8,128)}, f32[1,96]{1,0:T(1,128)}, f32[96,768]{1,0:T(8,128)}, f32[96,768]{1,0:T(8,128)...) custom-call(bf16[4,128,768]{2,1,0:T(8,128)(2,1)} %get-tuple-element., ...), custom_call_target="tpu_custom_call" | custom-call | tf_op jit(solution)/shard_map/outputs/pallas_call | solution.py:1042

commit v5 on v4

--- a/solution.py
+++ b/solution.py
@@ -271,17 +271,17 @@
         for copy in copies:
             copy.wait()
 
-    start(loads)
-    output_load.start()
-    for i in range(n_seq):
-        seg_send_ref[i] = jnp.broadcast_to(seg_ref[i : i + 1, :], (8, 128))
-
     barrier = pltpu.get_barrier_semaphore()
     peers = [at.core_peer, at.x_peer, at.y_peer] + [
         at.z_peer(lax.rem(at.z + i, n_seq)) for i in range(1, n_seq)
     ]
     for peer in peers:
         pl.semaphore_signal(barrier, inc=1, device_id=peer, device_id_type=MESH)
+    start(loads)
+    output_load.start()
+    for i in range(n_seq):
+        seg_send_ref[i] = jnp.broadcast_to(seg_ref[i : i + 1, :], (8, 128))
+
     pl.semaphore_wait(barrier, len(peers))
 
     ff = Sums(
@@ -537,51 +537,59 @@
         sent(COT, three_blocks)
         begin(mixed_back)
 
-        acc_ref[...] = jnp.zeros_like(acc_ref)
-
         def d_slot(g, k, lanes, half):
             n = 2 * lanes + half
             return att_own.at[2 * g + k, n // 4, (n // 2) % 2, n % 2, pl.ds(0, 256), :]
 
-        @pl.loop(0, tiles)
-        def _(step):
-            g = tiles - 1 - step
-            slot = lax.rem(g, 2)
-
-            @pl.when(step >= 2)
-            def _():
-                wait(weight_loads(g, slot))
-                slope_copy(g, slot, False).wait()
-
-            d_sides = [[], []]
+        def put_d_sides(g):
+            slot = g % 2
             for sub in range(2):
                 lanes = slice(256 * sub, 256 * sub + 256)
-                down = wd_ref[pl.ds(pl.multiple_of(slot * 512 + 256 * sub, 256), 256)]
-                d_act = dot_back(cot_ref[...], down)
+                d_act = dot_back(cot_ref[...], wd_ref[512 * slot + 256 * sub : 512 * slot + 256 * sub + 256, :])
                 for k in range(2):
                     d_side = (d_act * probs_ref[slot, 1 - k, :, lanes].astype(F32)).astype(LOW)
-                    d_sides[k].append(d_side)
                     for i in range(2):
                         for half in range(2):
                             d_slot(g, k, 2 * sub + i, half)[...] = d_side[
                                 256 * half : 256 * half + 256, 128 * i : 128 * i + 128
                             ]
-            resid = resid_ref[block(step), :]
-            hidden_t_ref[:, block(step)] = (resid * inverse_rms(resid) * gain_two_ref[...]).T.astype(LOW)
-            d_both = jnp.concatenate(d_sides[0] + d_sides[1], axis=1)
+
+        def add_d_hidden(g, first):
+            slot = g % 2
+            d_both = jnp.concatenate(
+                [
+                    jnp.concatenate([d_slot(g, k, lanes, half)[...] for half in range(2)], axis=0)
+                    for k in range(2)
+                    for lanes in range(4)
+                ],
+                axis=1,
+            )
             for tile in range(width // 256):
                 cols = slice(256 * tile, 256 * tile + 256)
-                acc_ref[:, cols] += dot_back(d_both, wgu_ref[slot, cols, :])
-
-            @pl.when(step <= 1)
-            def _():
-                start(weight_loads(g - 2, slot))
-                slope_copy(g - 2, slot, False).start()
-
-
-            @pl.when(step == 0)
-            def _():
-                ff.stage1(0)
+                term = dot_back(d_both, wgu_ref[slot, cols, :])
+                acc_ref[:, cols] = term if first else acc_ref[:, cols] + term
+
+        steps_back = list(range(tiles - 1, -1, -1))
+        put_d_sides(steps_back[0])
+        for i, g in enumerate(steps_back):
+            if g >= 2:
+                weight_loads(g - 2, g % 2)[0].start()
+                slope_copy(g - 2, g % 2, False).start()
+            if i >= 2:
+                wait(weight_loads(g, g % 2)[1:])
+            if g >= 1:
+                if i >= 1:
+                    weight_loads(g - 1, (g - 1) % 2)[0].wait()
+                    slope_copy(g - 1, (g - 1) % 2, False).wait()
+                put_d_sides(g - 1)
+            rows = slice(128 * i, 128 * i + 128)
+            resid = resid_ref[rows, :]
+            hidden_t_ref[:, rows] = (resid * inverse_rms(resid) * gain_two_ref[...]).T.astype(LOW)
+            add_d_hidden(g, i == 0)
+            if g >= 2:
+                start(weight_loads(g - 2, g % 2)[1:])
+            if i <= 1:
+                ff.stage1(i)
 
         start(loads)
         probs_copy(0, 0, False).start()
@@ -694,7 +702,6 @@
             return half_of
 
         ff.stage2(0)
-        ff.stage1(1)
         first = put_d_probs(0, 0)
         for half in range(2):
             first(half)
@@ -733,19 +740,19 @@
             attention_back(pair, True)
             ff.stage0(2 + pair)
 
-            @pl.when(pair == 0)
-            def _():
+            @pl.when(pair == 1)
+            def _():
+                ff.stage2(1)
+                ff.stage1(2)
                 ff.stage3(0)
 
-            @pl.when(pair == 1)
-            def _():
-                ff.stage1(2)
-
             @pl.when(pair == 2)
             def _():
-                ff.stage2(1)
                 ff.stage1(3)
-                ff.hop(0, 1)
+
+            @pl.when(pair == 3)
+            def _():
+                ff.stage3(1)
 
         @pl.loop(tiles, pairs)
         def _(pair):
@@ -753,10 +760,10 @@
 
             @pl.when(pair == tiles)
             def _():
-                ff.stage2(2)
-                ff.stage1(4)
-                ff.stage3(1)
-
+                ff.hop(0, 1)
+
+        ff.stage2(2)
+        ff.stage1(4)
         branch_ref[...] = d_q_t_ref[...].T
         wait(loads)
         for tile in range(width // 256):
@@ -766,12 +773,13 @@
                 + dot_back(d_k_ref[...], wgu_ref[1, rows, :width])
                 + dot_back(d_v_ref[...], wd_ref[rows, :])
             )
+        norm_back(resid_ref, x_ref, gain_one_ref, acc_ref, None, d_back_ref, 18)
+        ff.hop(1, 1)
+        begin(tokens_back[0])
         ff.stage2(3)
         ff.stage1(5)
-        norm_back(resid_ref, x_ref, gain_one_ref, acc_ref, None, d_back_ref, 18)
-        ff.hop(1, 1)
         ff.stage3(2)
-        begin(tokens_back[0])
+        begin(tokens_back[1])
         share(att, 0, attended_t_ref[...], d_branch_ref[...])
         ff.hop(0, 2)
 
@@ -786,7 +794,7 @@
         att.stage1(0)
         share(att, 3, hidden_t_ref[...], branch_ref[...])
         ff.hop(2, 1)
-        begin(tokens_back[1])
+        begin(tokens_back[2])
         ff.stage3(3)
 
     pl.run_scoped(
@@ -849,38 +857,33 @@
     att.stage2(0)
     att.stage1(2)
     ff.hop(3, 1)
-    begin(tokens_back[2])
+    begin(tokens_back[3])
     ff.stage3(5)
+    ff.hop(2, 2)
     att.stage2(1)
     att.stage1(3)
     ff.hop(4, 1)
-    ff.hop(2, 2)
+    ff.hop(3, 2)
     att.stage3(0)
     small_step(1)
     att.stage2(2)
     ff.hop(5, 1)
-    ff.hop(3, 2)
+    ff.hop(4, 2)
     att.stage3(1)
+    att.stage2(3)
     att.hop(0, 1)
-    att.stage2(3)
-    ff.hop(4, 2)
+    ff.hop(5, 2)
     small_step(2)
     small_rows[at.z] = small_own[steps]
     att.stage3(2)
     att.hop(1, 1)
+    att.hop(0, 2)
     att.stage3(3)
     for i in range(1, n_seq):
         small_row(i).start()
-    ff.hop(5, 2)
-    att.hop(0, 2)
     att.hop(2, 1)
+    att.hop(1, 2)
     att.hop(3, 1)
-
-    @pl.when(inner)
-    def _():
-        begin(tokens_back[3])
-
-    att.hop(1, 2)
     att.hop(2, 2)
     att.hop(3, 2)
 
@@ -888,13 +891,10 @@
     def _(j):
         ff.finish(j, ff_out)
 
-    @pl.when(jnp.logical_not(inner))
-    def _():
-        begin(tokens_back[3])
-
     @pl.loop(0, ATT_JOBS)
     def _(j):
         att.finish(j, att_out)
+
 
     three_rows = small_rows.at[pl.ds(0, n_seq - 1)]
     remote(three_rows, three_rows, small_sems.at[4], small_sems.at[5], at.core_peer).wait_recv()

time: 140 us -> 134 us (0.957)
  Pallas kernels: 139 us -> 133 us
    pallas_call x1, Pallas kernels: 135 us -> 129 us  [layer(): pl.pallas_call(functools.partial(layer_kernel, n_dp, n_seq), out_shape=[r...]
where the time goes in v5:
time: 134 us
  Pallas kernels  133 us (99%)
    pallas_call x1, Pallas kernels, layer(): pl.pallas_call(functools.partial(layer_kernel, n_dp, n_seq), out_shape=[r...  129 us
    pallas_call x1, Pallas kernels, outputs(): pl.pallas_call(functools.partial(outputs_kernel, n_dp), out_shape=results...  3.95 us

profile of v5, /device:TPU:0, one launch (start us, length us, event | category | flops | bytes accessed | tf_op | source)
XLA Modules:
  0.0 133.7 jit_solution(14828615277698843597)
XLA Ops:
  0.6 128.9 %layer.1 = (bf16[4,128,768]{2,1,0:T(8,128)(2,1)}, bf16[4,128,768]{2,1,0:T(8,128)(2,1)}, bf16[12,384,128]{2,1,0:T(8,128)(2,1)}, bf16[8,288,128]{2,1,0:T(8,128)(2,...) custom-call(bf16[4,128,768]{2,1,0:T(8,128)(2,1)} %tokens_hbm.1, ...), custom_call_target="tpu_custom_call" | custom-call | tf_op jit(solution)/shard_map/layer/pallas_call | solution.py:941
  129.6 3.9 %outputs.1 = (bf16[4,128,768]{2,1,0:T(8,128)(2,1)}, f32[4,128,768]{2,1,0:T(8,128)}, f32[1,96]{1,0:T(1,128)}, f32[96,768]{1,0:T(8,128)}, f32[96,768]{1,0:T(8,128)...) custom-call(bf16[4,128,768]{2,1,0:T(8,128)(2,1)} %get-tuple-element., ...), custom_call_target="tpu_custom_call" | custom-call | tf_op jit(solution)/shard_map/outputs/pallas_call | solution.py:1042

commit v6 on v5

--- a/solution.py
+++ b/solution.py
@@ -534,8 +534,11 @@
                     ]
         ff.stage0(0)
         ff.stage0(1)
-        sent(COT, three_blocks)
-        begin(mixed_back)
+        @pl.when((at.z == 0) | (at.z == n_seq - 1))
+        def _():
+            sent(COT, three_blocks)
+            begin(mixed_back)
+
 
         def d_slot(g, k, lanes, half):
             n = 2 * lanes + half
@@ -590,6 +593,13 @@
                 start(weight_loads(g - 2, g % 2)[1:])
             if i <= 1:
                 ff.stage1(i)
+            if i == 0:
+
+                @pl.when((at.z > 0) & (at.z < n_seq - 1))
+                def _():
+                    sent(COT, three_blocks)
+                    begin(mixed_back)
+
 
         start(loads)
         probs_copy(0, 0, False).start()
@@ -749,9 +759,6 @@
             @pl.when(pair == 2)
             def _():
                 ff.stage1(3)
-
-            @pl.when(pair == 3)
-            def _():
                 ff.stage3(1)
 
         @pl.loop(tiles, pairs)
@@ -773,8 +780,8 @@
                 + dot_back(d_k_ref[...], wgu_ref[1, rows, :width])
                 + dot_back(d_v_ref[...], wd_ref[rows, :])
             )
+        ff.hop(1, 1)
         norm_back(resid_ref, x_ref, gain_one_ref, acc_ref, None, d_back_ref, 18)
-        ff.hop(1, 1)
         begin(tokens_back[0])
         ff.stage2(3)
         ff.stage1(5)
@@ -794,6 +801,7 @@
         att.stage1(0)
         share(att, 3, hidden_t_ref[...], branch_ref[...])
         ff.hop(2, 1)
+        ff.hop(1, 2)
         begin(tokens_back[2])
         ff.stage3(3)
 
@@ -853,7 +861,6 @@
     att.stage1(1)
     ff.stage3(4)
     small_step(0)
-    ff.hop(1, 2)
     att.stage2(0)
     att.stage1(2)
     ff.hop(3, 1)

time: 134 us -> 133 us (level)
  no operation moved by 1% of the time
where the time goes in v6:
time: 133 us
  Pallas kernels  132 us (99%)
    pallas_call x1, Pallas kernels, layer(): pl.pallas_call(functools.partial(layer_kernel, n_dp, n_seq), out_shape=[r...  128 us
    pallas_call x1, Pallas kernels, outputs(): pl.pallas_call(functools.partial(outputs_kernel, n_dp), out_shape=results...  3.95 us

profile of v6, /device:TPU:0, one launch (start us, length us, event | category | flops | bytes accessed | tf_op | source)
XLA Modules:
  0.0 132.8 jit_solution(10467214027808813341)
XLA Ops:
  0.6 128.1 %layer.1 = (bf16[4,128,768]{2,1,0:T(8,128)(2,1)}, bf16[4,128,768]{2,1,0:T(8,128)(2,1)}, bf16[12,384,128]{2,1,0:T(8,128)(2,1)}, bf16[8,288,128]{2,1,0:T(8,128)(2,...) custom-call(bf16[4,128,768]{2,1,0:T(8,128)(2,1)} %tokens_hbm.1, ...), custom_call_target="tpu_custom_call" | custom-call | tf_op jit(solution)/shard_map/layer/pallas_call | solution.py:948
  128.7 3.9 %outputs.1 = (bf16[4,128,768]{2,1,0:T(8,128)(2,1)}, f32[4,128,768]{2,1,0:T(8,128)}, f32[1,96]{1,0:T(1,128)}, f32[96,768]{1,0:T(8,128)}, f32[96,768]{1,0:T(8,128)...) custom-call(bf16[4,128,768]{2,1,0:T(8,128)(2,1)} %get-tuple-element., ...), custom_call_target="tpu_custom_call" | custom-call | tf_op jit(solution)/shard_map/outputs/pallas_call | solution.py:1049

commit v7 on v6

--- a/solution.py
+++ b/solution.py
@@ -99,13 +99,13 @@
     def up(self, p, first):
         src = self.kept(p) if first else self.got2.at[p]
         return remote(
-            src, self.low_z.at[p], self.send_sems.at[3], self.z_sems.at[0, p], self.place.z_peer(self.place.z + 1)
+            src, self.low_z.at[p], self.send_sems.at[3], self.z_sems.at[0, p], self.place.z_peer(lax.rem(self.place.z + 1, self.place.n_seq))
         )
 
     def down(self, p, first):
         src = self.kept(p) if first else self.got1.at[p, 0]
         return remote(
-            src, self.high_z.at[p], self.send_sems.at[4], self.z_sems.at[1, p], self.place.z_peer(self.place.z - 1)
+            src, self.high_z.at[p], self.send_sems.at[4], self.z_sems.at[1, p], self.place.z_peer(lax.rem(self.place.z + self.place.n_seq - 1, self.place.n_seq))
         )
 
     def stage0(self, j):

time: 133 us -> 133 us (level)
  no operation moved by 1% of the time
where the time goes in v7:
time: 133 us
  Pallas kernels  132 us (99%)
    pallas_call x1, Pallas kernels, layer(): pl.pallas_call(functools.partial(layer_kernel, n_dp, n_seq), out_shape=[r...  128 us
    pallas_call x1, Pallas kernels, outputs(): pl.pallas_call(functools.partial(outputs_kernel, n_dp), out_shape=results...  3.95 us

profile of v7, /device:TPU:0, one launch (start us, length us, event | category | flops | bytes accessed | tf_op | source)
XLA Modules:
  0.0 132.8 jit_solution(1390905153702215052)
XLA Ops:
  0.6 128.1 %layer.1 = (bf16[4,128,768]{2,1,0:T(8,128)(2,1)}, bf16[4,128,768]{2,1,0:T(8,128)(2,1)}, bf16[12,384,128]{2,1,0:T(8,128)(2,1)}, bf16[8,288,128]{2,1,0:T(8,128)(2,...) custom-call(bf16[4,128,768]{2,1,0:T(8,128)(2,1)} %tokens_hbm.1, ...), custom_call_target="tpu_custom_call" | custom-call | tf_op jit(solution)/shard_map/layer/pallas_call | solution.py:948
  128.7 3.9 %outputs.1 = (bf16[4,128,768]{2,1,0:T(8,128)(2,1)}, f32[4,128,768]{2,1,0:T(8,128)}, f32[1,96]{1,0:T(1,128)}, f32[96,768]{1,0:T(8,128)}, f32[96,768]{1,0:T(8,128)...) custom-call(bf16[4,128,768]{2,1,0:T(8,128)(2,1)} %get-tuple-element., ...), custom_call_target="tpu_custom_call" | custom-call | tf_op jit(solution)/shard_map/outputs/pallas_call | solution.py:1049

commit v8 on v7

--- a/solution.py
+++ b/solution.py
@@ -982,10 +982,12 @@
     mixed_out, tokens_out, gn_one_out, gq_out, gk_out, gv_out, go_out, table_out, gn_two_out, gg_out, gu_out, gd_out,
     mixed_in, tokens_in, ff_in, att_in, small_in, gn_one, gq, gk, gv, go, table, gn_two, gg, gu, gd, tokens, sems,
 ):
+    blocks = tokens_ref.shape[0]
     copies = [
         pltpu.make_async_copy(src, dst, sems.at[i])
         for i, (src, dst) in enumerate(
-            [(small_ref, small_in), (tokens_ref, tokens_in), (ff_ref, ff_in), (att_ref, att_in), (mixed_ref, mixed_in)]
+            [(tokens_ref.at[z], tokens_in.at[z]) for z in range(blocks)]
+            + [(small_ref, small_in), (ff_ref, ff_in), (att_ref, att_in), (mixed_ref, mixed_in)]
         )
     ]
     for copy in copies:
@@ -998,7 +1000,11 @@
 
     width = mixed_ref.shape[-1]
     shard = width // GROUP
-    copies[0].wait()
+    for z in range(blocks):
+        copies[z].wait()
+        tokens[z] = tokens_in[z].astype(F32)
+        store(tokens.at[z], tokens_out.at[z])
+    copies[blocks].wait()
     table[...] = small_in[: table.shape[0], : table.shape[1]]
     store(table, table_out)
     mine = lax.axis_index("dp") // (n_dp // GROUP)
@@ -1009,10 +1015,7 @@
             total = total + jnp.where(mine == s, gains[:, shard * s : shard * s + shard], 0.0)
         part[...] = total
         store(part, out)
-    copies[1].wait()
-    tokens[...] = tokens_in[...].astype(F32)
-    store(tokens, tokens_out)
-    copies[2].wait()
+    copies[blocks + 1].wait()
     for k, (part, out) in enumerate(((gg, gg_out), (gu, gu_out))):
         for g in range(4):
             for i in range(4):
@@ -1023,14 +1026,14 @@
         for i in range(width // 128):
             gd[64 * p : 64 * p + 64, 128 * i : 128 * i + 128] = ff_in[p, 64 * i : 64 * i + 64, :].astype(F32)
     store(gd, gd_out)
-    copies[3].wait()
+    copies[blocks + 2].wait()
     for j, (part, out) in enumerate(((go, go_out), (gv, gv_out), (gk, gk_out), (gq, gq_out))):
         for k in range(2):
             for i in range(width // 256):
                 col = width // 2 * k + 128 * i
                 part[:, col : col + 128] = att_in[2 * j + k, shard * i : shard * i + shard, :].astype(F32)
         store(part, out)
-    copies[4].wait()
+    copies[blocks + 3].wait()
     store(mixed_in, mixed_out)
     for copy in stores:
         copy.wait()
@@ -1052,7 +1055,7 @@
         in_specs=[any_] * 5,
         out_specs=[any_] * len(results),
         scratch_shapes=[VMEM(a.shape, a.dtype) for a in [mixed, tokens, ff, att, small] + results[2:] + results[1:2]]
-        + [pltpu.SemaphoreType.DMA((5 + len(results),))],
+        + [pltpu.SemaphoreType.DMA((3 + len(results) + 2 * tokens.shape[0],))],
         compiler_params=pltpu.CompilerParams(vmem_limit_bytes=VMEM_BYTES),
         name="outputs",
     )(mixed, tokens, ff, att, small)

time: 133 us -> 133 us (level)
  no operation moved by 1% of the time
where the time goes in v8:
time: 133 us
  Pallas kernels  132 us (99%)
    pallas_call x1, Pallas kernels, layer(): pl.pallas_call(functools.partial(layer_kernel, n_dp, n_seq), out_shape=[r...  128 us
    pallas_call x1, Pallas kernels, outputs(): pl.pallas_call(functools.partial(outputs_kernel, n_dp), out_shape=results...  3.95 us

profile of v8, /device:TPU:0, one launch (start us, length us, event | category | flops | bytes accessed | tf_op | source)
XLA Modules:
  0.0 132.8 jit_solution(13926651411193173109)
XLA Ops:
  0.6 128.1 %layer.1 = (bf16[4,128,768]{2,1,0:T(8,128)(2,1)}, bf16[4,128,768]{2,1,0:T(8,128)(2,1)}, bf16[12,384,128]{2,1,0:T(8,128)(2,1)}, bf16[8,288,128]{2,1,0:T(8,128)(2,...) custom-call(bf16[4,128,768]{2,1,0:T(8,128)(2,1)} %tokens_hbm.1, ...), custom_call_target="tpu_custom_call" | custom-call | tf_op jit(solution)/shard_map/layer/pallas_call | solution.py:948
  128.7 3.9 %outputs.1 = (bf16[4,128,768]{2,1,0:T(8,128)(2,1)}, f32[4,128,768]{2,1,0:T(8,128)}, f32[1,96]{1,0:T(1,128)}, f32[96,768]{1,0:T(8,128)}, f32[96,768]{1,0:T(8,128)...) custom-call(bf16[4,128,768]{2,1,0:T(8,128)(2,1)} %get-tuple-element., ...), custom_call_target="tpu_custom_call" | custom-call | tf_op jit(solution)/shard_map/outputs/pallas_call | solution.py:1052
